TPU v7x, 32 devices: a whole 2x2x4 slice. The times are simulated.
32 devices in a mesh: fsdp: 16 (over z, x, core), rep: 2 (over y).
Axes of the slice: x: 2, y: 2, z: 4, core: 2. Of those that a mesh axis runs over, the one named last changes fastest.
Arguments:
- tokens: bfloat16 [14336, 1152], P(('fsdp', 'rep')), may hold values from -6 to 6
- condition: bfloat16 [32, 1152], P(('fsdp', 'rep')), may hold values from -6 to 6
- lengths: int32 [32], P(('fsdp', 'rep')), may hold values from 336 to 448, as said below
- targets: bfloat16 [14336, 768], P(('fsdp', 'rep')), may hold values from -6 to 6
- cotangent: bfloat16 [14336, 1152], P(('fsdp', 'rep')), may hold values from -6 to 6
- wide_weight: float32 [2, 1152, 16128], P(None, 'fsdp'), may hold values from -0.5 to 0.5
- deep_weight: float32 [2, 4608, 1152], P(None, 'fsdp'), may hold values from -0.09375 to 0.09375
- head_first: float32 [1152, 2048], P('fsdp'), may hold values from -0.1875 to 0.1875
- head_second: float32 [2048, 2816], P('fsdp'), may hold values from -0.125 to 0.125
- block_bias: float32 [2, 16128], replicated, may hold values from -4 to 4
- head_bias: float32 [4864], replicated, may hold values from -4 to 4
- wide_mean: float32 [2, 1152, 16128], P(None, 'fsdp'), may hold values from -64 to 64
- deep_mean: float32 [2, 4608, 1152], P(None, 'fsdp'), may hold values from -64 to 64
- head_first_mean: float32 [1152, 2048], P('fsdp'), may hold values from -0.078125 to 0.078125
- head_second_mean: float32 [2048, 2816], P('fsdp'), may hold values from -0.078125 to 0.078125
- block_bias_mean: float32 [2, 16128], replicated, may hold values from -64 to 64
- head_bias_mean: float32 [4864], replicated, may hold values from -0.15625 to 0.15625
- wide_square: float32 [2, 1152, 16128], P(None, 'fsdp'), may hold values from 9.17504 to 36.70016
- deep_square: float32 [2, 4608, 1152], P(None, 'fsdp'), may hold values from 9.17504 to 36.70016
- head_first_square: float32 [1152, 2048], P('fsdp'), may hold values from 2.1875e-06 to 8.75e-06
- head_second_square: float32 [2048, 2816], P('fsdp'), may hold values from 2.1875e-06 to 8.75e-06
- block_bias_square: float32 [2, 16128], replicated, may hold values from 9.17504 to 36.70016
- head_bias_square: float32 [4864], replicated, may hold values from 8.75e-06 to 3.5e-05
Outputs:
- output: bfloat16 [14336, 1152], P(('fsdp', 'rep'))
- input_grad: float32 [14336, 1152], P(('fsdp', 'rep'))
- wide_grad: float32 [2, 1152, 16128], P(None, 'fsdp')
- deep_grad: float32 [2, 4608, 1152], P(None, 'fsdp')
- head_first_grad: float32 [1152, 2048], P('fsdp')
- head_second_grad: float32 [2048, 2816], P('fsdp')
- block_bias_grad: float32 [2, 16128], replicated
- head_bias_grad: float32 [4864], replicated
- wide_mean_new: float32 [2, 1152, 16128], P(None, 'fsdp')
- deep_mean_new: float32 [2, 4608, 1152], P(None, 'fsdp')
- head_first_mean_new: float32 [1152, 2048], P('fsdp')
- head_second_mean_new: float32 [2048, 2816], P('fsdp')
- block_bias_mean_new: float32 [2, 16128], replicated
- head_bias_mean_new: float32 [4864], replicated
- wide_square_new: float32 [2, 1152, 16128], P(None, 'fsdp')
- deep_square_new: float32 [2, 4608, 1152], P(None, 'fsdp')
- head_first_square_new: float32 [1152, 2048], P('fsdp')
- head_second_square_new: float32 [2048, 2816], P('fsdp')
- block_bias_square_new: float32 [2, 16128], replicated
- head_bias_square_new: float32 [4864], replicated
- wide_weight_new: float32 [2, 1152, 16128], P(None, 'fsdp')
- deep_weight_new: float32 [2, 4608, 1152], P(None, 'fsdp')
- head_first_new: float32 [1152, 2048], P('fsdp')
- head_second_new: float32 [2048, 2816], P('fsdp')
- block_bias_new: float32 [2, 16128], replicated
- head_bias_new: float32 [4864], replicated
Inputs may be any that keep to these rules, and one draw needn't show every extreme that they name: `lengths`: each sequence's valid tokens; some sequence is full in every draw.
All inputs are finite; a program needn't handle non-finite values.
Results may differ from a plain program's by a relative error of at most 0.024.
The roundings to bfloat16 on the way count: a program that leaves them out, or rounds other values in their place, can miss the bound.
Values may be sent and summed in bfloat16 or wider, within the bound.
A program may use at most 640 MiB of HBM per device.

v0:
```python
import jax
import jax.numpy as jnp
from jax import lax
from jax.sharding import PartitionSpec as P

MODEL_WIDTH = 1152
HEADS = 16
HEAD_DIM = 72
FF = 4608
PH = 2048
PZ = 768
SEQ_LEN = 448
STEP = 10


norm_epsilon = 1e-06
adam_epsilon = 1e-08
masked_score = -1e30
repa_weight = 0.5
matrix_rate = 0.05
bias_rate = 0.3
matrix_decay = 0.01


def normalize(values):
    centred = values - jnp.mean(values, axis=-1, keepdims=True)
    spread = jnp.mean(centred * centred, axis=-1, keepdims=True)
    return centred * lax.rsqrt(spread + norm_epsilon)


def modulate(values, offset, factor):
    return normalize(values) * (1.0 + factor) + offset


def gelu_tanh(values):
    return jax.nn.gelu(values, approximate=True)


def split_modulation(modulation):
    columns = modulation.shape[-1] // 6
    return [modulation[:, None, number * columns : (number + 1) * columns] for number in range(6)]


def outer_rows(left, right):
    flat_left = left.reshape(-1, left.shape[-1])
    flat_right = right.reshape(-1, right.shape[-1])
    return lax.dot_general(
        flat_left, flat_right, (((0,), (0,)), ((), ())), preferred_element_type=jnp.float32
    )


def fetch_block(wide_shard, deep_shard):
    return (
        lax.all_gather(wide_shard.astype(jnp.bfloat16), "fsdp", axis=0, tiled=True),
        lax.all_gather(deep_shard.astype(jnp.bfloat16), "fsdp", axis=0, tiled=True),
    )


def fetch_block_again(wide_shard, deep_shard):
    return (
        lax.all_gather(wide_shard.astype(jnp.bfloat16), "fsdp", axis=0, tiled=True),
        lax.all_gather(deep_shard.astype(jnp.bfloat16), "fsdp", axis=0, tiled=True),
    )


def reduce_wide(term_fn, row_count):
    return lax.psum_scatter(
        term_fn(jnp.int32(0), lax.axis_size("fsdp") * row_count),
        "fsdp",
        scatter_dimension=0,
        tiled=True,
    )


def reduce_deep(term_fn, row_count):
    return lax.psum_scatter(
        term_fn(jnp.int32(0), lax.axis_size("fsdp") * row_count),
        "fsdp",
        scatter_dimension=0,
        tiled=True,
    )


def reduce_head(term_fn, row_count):
    return lax.psum_scatter(
        term_fn(jnp.int32(0), lax.axis_size("fsdp") * row_count),
        "fsdp",
        scatter_dimension=0,
        tiled=True,
    )


def attention_forward(inputs):
    queries, keys_in, values_in, visible = inputs
    factor = queries.shape[-1] ** (-0.5)
    scores = (
        jnp.einsum("qhd,khd->hqk", queries, keys_in, preferred_element_type=jnp.float32) * factor
    )
    scores = jnp.where(visible[None, None, :], scores, masked_score)
    largest = jnp.max(scores, axis=-1, keepdims=True)
    expanded = jnp.exp(scores - largest)
    totals = jnp.sum(expanded, axis=-1, keepdims=True)
    weights = (expanded / totals).astype(jnp.bfloat16)
    attended = jnp.einsum("hqk,khd->qhd", weights, values_in, preferred_element_type=jnp.float32)
    return (attended, largest + jnp.log(totals))


def attention_backward(inputs):
    queries, keys_in, values_in, visible, log_total, upstream = inputs
    factor = queries.shape[-1] ** (-0.5)
    scores = (
        jnp.einsum("qhd,khd->hqk", queries, keys_in, preferred_element_type=jnp.float32) * factor
    )
    scores = jnp.where(visible[None, None, :], scores, masked_score)
    chances = jnp.exp(scores - log_total)
    chance_grad = jnp.einsum(
        "qhd,khd->hqk", upstream, values_in, preferred_element_type=jnp.float32
    )
    value_grad = jnp.einsum(
        "hqk,qhd->khd", chances.astype(jnp.bfloat16), upstream, preferred_element_type=jnp.float32
    )
    centre = jnp.sum(chance_grad * chances, axis=-1, keepdims=True)
    score_grad = (chances * (chance_grad - centre)).astype(jnp.bfloat16)
    query_grad = (
        jnp.einsum("hqk,khd->qhd", score_grad, keys_in, preferred_element_type=jnp.float32) * factor
    )
    key_grad = (
        jnp.einsum("hqk,qhd->khd", score_grad, queries, preferred_element_type=jnp.float32) * factor
    )
    return (query_grad, key_grad, value_grad)


def block_forward(hidden, silu_low, wide_matrix, deep_matrix, bias, visible):
    sequences = hidden.shape[0]
    modulation = (
        jnp.dot(silu_low, wide_matrix[:, : 6 * MODEL_WIDTH], preferred_element_type=jnp.float32)
        + bias[: 6 * MODEL_WIDTH]
    )
    offset_first, factor_first, gate_first, offset_second, factor_second, gate_second = (
        split_modulation(modulation)
    )
    normed_low = modulate(hidden, offset_first, factor_first).astype(jnp.bfloat16)
    triple_bias = jnp.concatenate(
        [
            bias[6 * MODEL_WIDTH : 7 * MODEL_WIDTH],
            jnp.zeros((MODEL_WIDTH,), jnp.float32),
            bias[7 * MODEL_WIDTH : 8 * MODEL_WIDTH],
        ]
    )
    triple = (
        jnp.dot(
            normed_low,
            wide_matrix[:, 6 * MODEL_WIDTH : 9 * MODEL_WIDTH],
            preferred_element_type=jnp.float32,
        )
        + triple_bias
    ).astype(jnp.bfloat16)
    pieces = triple.reshape(sequences, SEQ_LEN, 3, HEADS, HEAD_DIM)
    attended, log_total = lax.map(
        attention_forward, (pieces[:, :, 0], pieces[:, :, 1], pieces[:, :, 2], visible)
    )
    attended_low = attended.reshape(sequences, SEQ_LEN, MODEL_WIDTH).astype(jnp.bfloat16)
    branch = (
        jnp.dot(
            attended_low,
            wide_matrix[:, 9 * MODEL_WIDTH : 10 * MODEL_WIDTH],
            preferred_element_type=jnp.float32,
        )
        + bias[8 * MODEL_WIDTH : 9 * MODEL_WIDTH]
    )
    middle = hidden + gate_first * branch
    mixed_low = modulate(middle, offset_second, factor_second).astype(jnp.bfloat16)
    pre_active = (
        jnp.dot(mixed_low, wide_matrix[:, 10 * MODEL_WIDTH :], preferred_element_type=jnp.float32)
        + bias[9 * MODEL_WIDTH : 9 * MODEL_WIDTH + FF]
    )
    active_low = gelu_tanh(pre_active).astype(jnp.bfloat16)
    feed_out = (
        jnp.dot(active_low, deep_matrix, preferred_element_type=jnp.float32)
        + bias[9 * MODEL_WIDTH + FF :]
    )
    result = middle + gate_second * feed_out
    saved = (
        hidden,
        modulation,
        normed_low,
        triple,
        log_total,
        attended_low,
        branch,
        middle,
        mixed_low,
        pre_active,
        active_low,
        feed_out,
    )
    return (result, saved)


def block_backward(upstream, saved, silu_low, wide_matrix, deep_matrix, visible):
    (
        hidden,
        modulation,
        normed_low,
        triple,
        log_total,
        attended_low,
        branch,
        middle,
        mixed_low,
        pre_active,
        active_low,
        feed_out,
    ) = saved
    sequences = hidden.shape[0]
    offset_first, factor_first, gate_first, offset_second, factor_second, gate_second = (
        split_modulation(modulation)
    )
    feedforward_gradient = (upstream * gate_second).astype(jnp.bfloat16)
    gate_second_grad = jnp.sum(upstream * feed_out, axis=1)
    activation_gradient = jnp.einsum(
        "xjn,mn->xjm", feedforward_gradient, deep_matrix, preferred_element_type=jnp.float32
    )
    preactivation_gradient = jax.vjp(gelu_tanh, pre_active)[1](activation_gradient)[0].astype(
        jnp.bfloat16
    )
    mixed_grad = jnp.einsum(
        "qvm,am->qva",
        preactivation_gradient,
        wide_matrix[:, 10 * MODEL_WIDTH :],
        preferred_element_type=jnp.float32,
    )
    second_back = jax.vjp(modulate, middle, offset_second, factor_second)[1]
    middle_part, offset_second_grad, factor_second_grad = second_back(mixed_grad)
    middle_grad = upstream + middle_part
    gate_first_grad = jnp.sum(middle_grad * branch, axis=1)
    branch_gradient = (middle_grad * gate_first).astype(jnp.bfloat16)
    attended_grad = jnp.einsum(
        "tbr,ar->tba",
        branch_gradient,
        wide_matrix[:, 9 * MODEL_WIDTH : 10 * MODEL_WIDTH],
        preferred_element_type=jnp.float32,
    ).astype(jnp.bfloat16)
    pieces = triple.reshape(sequences, SEQ_LEN, 3, HEADS, HEAD_DIM)
    heads_grad = attended_grad.reshape(sequences, SEQ_LEN, HEADS, HEAD_DIM)
    query_grad, key_grad, value_grad = lax.map(
        attention_backward,
        (pieces[:, :, 0], pieces[:, :, 1], pieces[:, :, 2], visible, log_total, heads_grad),
    )
    triple_gradient = jnp.concatenate(
        [
            query_grad.reshape(sequences, SEQ_LEN, MODEL_WIDTH),
            key_grad.reshape(sequences, SEQ_LEN, MODEL_WIDTH),
            value_grad.reshape(sequences, SEQ_LEN, MODEL_WIDTH),
        ],
        axis=-1,
    ).astype(jnp.bfloat16)
    normed_grad = jnp.einsum(
        "tbr,ar->tba",
        triple_gradient,
        wide_matrix[:, 6 * MODEL_WIDTH : 9 * MODEL_WIDTH],
        preferred_element_type=jnp.float32,
    )
    first_back = jax.vjp(modulate, hidden, offset_first, factor_first)[1]
    hidden_part, offset_first_grad, factor_first_grad = first_back(normed_grad)
    hidden_grad = middle_grad + hidden_part
    modulation_grad = jnp.concatenate(
        [
            offset_first_grad[:, 0],
            factor_first_grad[:, 0],
            gate_first_grad,
            offset_second_grad[:, 0],
            factor_second_grad[:, 0],
            gate_second_grad,
        ],
        axis=-1,
    ).astype(jnp.bfloat16)
    bias_grad = jnp.concatenate(
        [
            jnp.sum(modulation_grad, axis=0, dtype=jnp.float32),
            jnp.sum(triple_gradient[..., :MODEL_WIDTH], axis=(0, 1), dtype=jnp.float32),
            jnp.sum(triple_gradient[..., 2 * MODEL_WIDTH :], axis=(0, 1), dtype=jnp.float32),
            jnp.sum(branch_gradient, axis=(0, 1), dtype=jnp.float32),
            jnp.sum(preactivation_gradient, axis=(0, 1), dtype=jnp.float32),
            jnp.sum(feedforward_gradient, axis=(0, 1), dtype=jnp.float32),
        ]
    )

    def wide_terms(first_row, row_total):
        return jnp.concatenate(
            [
                outer_rows(silu_low, modulation_grad),
                outer_rows(normed_low, triple_gradient),
                outer_rows(attended_low, branch_gradient),
                outer_rows(mixed_low, preactivation_gradient),
            ],
            axis=1,
        )

    def deep_terms(first_row, row_total):
        return outer_rows(active_low, feedforward_gradient)

    return (hidden_grad, bias_grad, wide_terms, deep_terms)


def adam_update(weight, grad, first, second, rate, decay):
    first_new = 0.9 * first + 0.1 * grad
    second_new = 0.999 * second + 0.001 * grad * grad
    first_hat = first_new / (1.0 - 0.9**STEP)
    second_hat = second_new / (1.0 - 0.999**STEP)
    updated = weight - rate * (first_hat / (jnp.sqrt(second_hat) + adam_epsilon) + decay * weight)
    return (first_new, second_new, updated)


def per_device(
    tokens,
    condition,
    lengths,
    targets,
    cotangent,
    wide_weight,
    deep_weight,
    head_first,
    head_second,
    block_bias,
    head_bias,
    wide_mean,
    deep_mean,
    head_first_mean,
    head_second_mean,
    block_bias_mean,
    head_bias_mean,
    wide_square,
    deep_square,
    head_first_square,
    head_second_square,
    block_bias_square,
    head_bias_square,
):
    sequences = condition.shape[0]
    hidden = tokens.astype(jnp.float32).reshape(sequences, SEQ_LEN, MODEL_WIDTH)
    silu_low = jax.nn.silu(condition.astype(jnp.float32)).astype(jnp.bfloat16)
    visible = jnp.arange(SEQ_LEN, dtype=jnp.int32)[None, :] < lengths[:, None]
    wide_early, deep_early = fetch_block(wide_weight[0], deep_weight[0])
    tapped, saved_early = block_forward(
        hidden, silu_low, wide_early, deep_early, block_bias[0], visible
    )
    first_matrix, second_w = (
        lax.all_gather(head_first.astype(jnp.bfloat16), "fsdp", axis=0, tiled=True),
        lax.all_gather(head_second.astype(jnp.bfloat16), "fsdp", axis=0, tiled=True),
    )
    tapped_low = tapped.astype(jnp.bfloat16)
    first_pre = (
        jnp.dot(tapped_low, first_matrix, preferred_element_type=jnp.float32) + head_bias[:PH]
    )
    first_low = jax.nn.silu(first_pre).astype(jnp.bfloat16)
    second_pre = (
        jnp.dot(first_low, second_w[:, :PH], preferred_element_type=jnp.float32)
        + head_bias[PH : 2 * PH]
    )
    second_low = jax.nn.silu(second_pre).astype(jnp.bfloat16)
    projected = (
        jnp.dot(second_low, second_w[:, PH:], preferred_element_type=jnp.float32)
        + head_bias[2 * PH :]
    )
    wide_late, deep_late = fetch_block(wide_weight[1], deep_weight[1])
    final, saved_late = block_forward(
        tapped, silu_low, wide_late, deep_late, block_bias[1], visible
    )
    raw_targets = targets.astype(jnp.float32).reshape(sequences, SEQ_LEN, PZ)
    target_unit = raw_targets * lax.rsqrt(
        jnp.sum(raw_targets * raw_targets, axis=-1, keepdims=True) + norm_epsilon
    )

    def alignment(values):
        unit = values * lax.rsqrt(jnp.sum(values * values, axis=-1, keepdims=True) + norm_epsilon)
        return jnp.sum(unit * target_unit, axis=-1)

    wide_late, deep_late = fetch_block_again(wide_weight[1], deep_weight[1])
    second_w = lax.all_gather(head_second.astype(jnp.bfloat16), "fsdp", axis=0, tiled=True)
    wide_early, deep_early = fetch_block_again(wide_weight[0], deep_weight[0])
    upstream = cotangent.astype(jnp.float32).reshape(sequences, SEQ_LEN, MODEL_WIDTH)
    late_input_grad, late_bias_grad, late_wide_fn, late_deep_fn = block_backward(
        upstream, saved_late, silu_low, wide_late, deep_late, visible
    )
    late_wide_grad = reduce_wide(late_wide_fn, wide_weight.shape[1])
    late_deep_grad = reduce_deep(late_deep_fn, deep_weight.shape[1])
    projected_grad = jax.vjp(alignment, projected)[1](-repa_weight * visible.astype(jnp.float32))[
        0
    ].astype(jnp.bfloat16)
    second_act_grad = jnp.einsum(
        "slz,hz->slh", projected_grad, second_w[:, PH:], preferred_element_type=jnp.float32
    )
    second_grad = jax.vjp(jax.nn.silu, second_pre)[1](second_act_grad)[0].astype(jnp.bfloat16)
    first_act_grad = jnp.einsum(
        "slh,gh->slg", second_grad, second_w[:, :PH], preferred_element_type=jnp.float32
    )
    first_gradient = jax.vjp(jax.nn.silu, first_pre)[1](first_act_grad)[0].astype(jnp.bfloat16)
    tapped_gradient = jnp.einsum(
        "ejk,rk->ejr", first_gradient, first_matrix, preferred_element_type=jnp.float32
    )
    head_bias_grad = jnp.concatenate(
        [
            jnp.sum(first_gradient, axis=(0, 1), dtype=jnp.float32),
            jnp.sum(second_grad, axis=(0, 1), dtype=jnp.float32),
            jnp.sum(projected_grad, axis=(0, 1), dtype=jnp.float32),
        ]
    )

    def first_terms(first_row, row_total):
        return outer_rows(tapped_low, first_gradient)

    def second_terms(first_row, row_total):
        return jnp.concatenate(
            [outer_rows(first_low, second_grad), outer_rows(second_low, projected_grad)], axis=1
        )

    first_weight_grad = reduce_head(first_terms, head_first.shape[0])
    second_weight_grad = reduce_head(second_terms, head_second.shape[0])
    input_grad, early_bias_grad, early_wide_fn, early_deep_fn = block_backward(
        late_input_grad + tapped_gradient, saved_early, silu_low, wide_early, deep_early, visible
    )
    early_wide_grad = reduce_wide(early_wide_fn, wide_weight.shape[1])
    early_deep_grad = reduce_deep(early_deep_fn, deep_weight.shape[1])
    wide_grad = jnp.stack([early_wide_grad, late_wide_grad])
    deep_grad = jnp.stack([early_deep_grad, late_deep_grad])
    wide_grad, deep_grad, first_weight_grad, second_weight_grad = (
        lax.psum(wide_grad.astype(jnp.bfloat16), "rep").astype(jnp.float32),
        lax.psum(deep_grad.astype(jnp.bfloat16), "rep").astype(jnp.float32),
        lax.psum(first_weight_grad.astype(jnp.bfloat16), "rep").astype(jnp.float32),
        lax.psum(second_weight_grad.astype(jnp.bfloat16), "rep").astype(jnp.float32),
    )
    block_bias_grad, head_bias_total = lax.psum(
        (jnp.stack([early_bias_grad, late_bias_grad]), head_bias_grad), ("fsdp", "rep")
    )
    wide_m, wide_v, wide_new = adam_update(
        wide_weight, wide_grad, wide_mean, wide_square, matrix_rate, matrix_decay
    )
    deep_m, deep_v, deep_new = adam_update(
        deep_weight, deep_grad, deep_mean, deep_square, matrix_rate, matrix_decay
    )
    first_m, first_v, first_new = adam_update(
        head_first, first_weight_grad, head_first_mean, head_first_square, matrix_rate, matrix_decay
    )
    second_m, second_v, second_new = adam_update(
        head_second,
        second_weight_grad,
        head_second_mean,
        head_second_square,
        matrix_rate,
        matrix_decay,
    )
    bias_m, bias_v, bias_new = adam_update(
        block_bias, block_bias_grad, block_bias_mean, block_bias_square, bias_rate, 0.0
    )
    hbias_m, hbias_v, hbias_new = adam_update(
        head_bias, head_bias_total, head_bias_mean, head_bias_square, bias_rate, 0.0
    )
    output = final.reshape(sequences * SEQ_LEN, MODEL_WIDTH).astype(jnp.bfloat16)
    input_flat = input_grad.reshape(sequences * SEQ_LEN, MODEL_WIDTH)
    return (
        output,
        input_flat,
        wide_grad,
        deep_grad,
        first_weight_grad,
        second_weight_grad,
        block_bias_grad,
        head_bias_total,
        wide_m,
        deep_m,
        first_m,
        second_m,
        bias_m,
        hbias_m,
        wide_v,
        deep_v,
        first_v,
        second_v,
        bias_v,
        hbias_v,
        wide_new,
        deep_new,
        first_new,
        second_new,
        bias_new,
        hbias_new,
    )


def solution(mesh):
    in_specs = (
        P(("fsdp", "rep"), None),
        P(("fsdp", "rep"), None),
        P(("fsdp", "rep")),
        P(("fsdp", "rep"), None),
        P(("fsdp", "rep"), None),
        P(None, "fsdp", None),
        P(None, "fsdp", None),
        P("fsdp", None),
        P("fsdp", None),
        P(),
        P(),
        P(None, "fsdp", None),
        P(None, "fsdp", None),
        P("fsdp", None),
        P("fsdp", None),
        P(),
        P(),
        P(None, "fsdp", None),
        P(None, "fsdp", None),
        P("fsdp", None),
        P("fsdp", None),
        P(),
        P(),
    )
    out_specs = (
        P(("fsdp", "rep"), None),
        P(("fsdp", "rep"), None),
        P(None, "fsdp", None),
        P(None, "fsdp", None),
        P("fsdp", None),
        P("fsdp", None),
        P(),
        P(),
        P(None, "fsdp", None),
        P(None, "fsdp", None),
        P("fsdp", None),
        P("fsdp", None),
        P(),
        P(),
        P(None, "fsdp", None),
        P(None, "fsdp", None),
        P("fsdp", None),
        P("fsdp", None),
        P(),
        P(),
        P(None, "fsdp", None),
        P(None, "fsdp", None),
        P("fsdp", None),
        P("fsdp", None),
        P(),
        P(),
    )
    return jax.shard_map(
        per_device, mesh=mesh, in_specs=in_specs, out_specs=out_specs, check_vma=False
    )
```

profile of v0, /device:TPU:0, one launch (start us, length us, event | category | flops | bytes accessed | tf_op | source)
XLA Modules:
  0.0 3246.4 jit_solution(11369717295377315129)
XLA Ops:
  25.8 175.9 %all-gather.15.cloned.1.call-done = bf16[1,1152,16128]{2,1,0:T(8,128)(2,1)} async-done(((bf16[1,72,16128]{2,1,0:T(8,128)(2,1)}), bf16[1,1152,16128]{2,1,0:T(8,128)(2,1)}) %all-gather.15.cloned.1.call-update) | async-done | bytes 37158928 | tf_op jit(solution)/shard_map/all_gather | solution.py:54
  268.0 25.3 all-gather.17.cloned.1.call-done
  293.3 14.4 fusion.186
  307.7 39.9 %all-gather.11.cloned.1.call-done = bf16[1152,2048]{1,0:T(8,128)(2,1)} async-done(((bf16[72,2048]{1,0:T(8,128)(2,1)}), bf16[1152,2048]{1,0:T(8,128)(2,1)}) %all-gather.11.cloned.1.call-update) | async-done | bytes 4718608 | tf_op jit(solution)/shard_map/all_gather | solution.py:349
  355.0 88.3 %all-gather.13.cloned.1.call-done = bf16[2048,2816]{1,0:T(8,128)(2,1)} async-done(((bf16[128,2816]{1,0:T(8,128)(2,1)}), bf16[2048,2816]{1,0:T(8,128)(2,1)}) %all-gather.13.cloned.1.call-update) | async-done | bytes 11534352 | tf_op jit(solution)/shard_map/all_gather | solution.py:350
  475.1 153.4 %all-gather.19.cloned.1.call-done = bf16[1,1152,16128]{2,1,0:T(8,128)(2,1)} async-done(((bf16[1,72,16128]{2,1,0:T(8,128)(2,1)}), bf16[1,1152,16128]{2,1,0:T(8,128)(2,1)}) %all-gather.19.cloned.1.call-update) | async-done | bytes 37158928 | tf_op jit(solution)/shard_map/all_gather | solution.py:54
  706.7 13.2 all-gather.21.cloned.1.call-done
  720.0 13.5 convert_reduce_fusion
  733.5 13.0 multiply_reduce_fusion.2
  749.0 13.8 convert_reduce_fusion.9
  843.7 15.2 pad_maximum_fusion.2
  860.4 15.7 convert_reduce_fusion.1
  897.6 12.6 multiply_reduce_fusion
  978.4 20.5 broadcast_multiply_fusion.1
  998.9 44.6 %pad_maximum_fusion.1 = f32[1152,16128]{1,0:T(8,128)} fusion(f32[1152,4608]{1,0:T(8,128)S(1)} %fusion.171, f32[1152,1152]{1,0:T(8,128)} %fusion.194, f32[1152,3456]{1,0:T(8,128)} %fusion.118, f32[1152,6912]{1,0:T(8,128)} %get-tuple-element.306), kind=kLoop, calls=%fused_computation.1 | loop fusion | flops 55738368 | bytes 148635648 | tf_op jit(solution)/shard_map/concatenate | solution.py:290
  1071.0 47.5 %pad_maximum_fusion = f32[1152,16128]{1,0:T(8,128)} fusion(f32[1152,4608]{1,0:T(8,128)S(1)} %fusion.170, f32[1152,1152]{1,0:T(8,128)} %fusion.193, f32[1152,3456]{1,0:T(8,128)} %fusion.117, f32[1152,6912]{1,0:T(8,128)} %get-tuple-element.305), kind=kLoop, calls=%fused_computation | loop fusion | flops 55738368 | bytes 148635648 | tf_op jit(solution)/shard_map/concatenate | solution.py:290
  1124.2 142.9 %reduce-scatter.11.cloned.1.call-done = f32[288,1152]{1,0:T(8,128)} async-done(((f32[4608,1152]{1,0:T(8,128)}), f32[288,1152]{1,0:T(8,128)}) %reduce-scatter.11.cloned.1.call-update) | async-done | bytes 1327120 | tf_op jit(solution)/shard_map/reduce_scatter | solution.py:76
  1269.7 227.9 %reduce-scatter.17.cloned.1.call-done = f32[128,2816]{0,1:T(8,128)} async-done(((f32[2048,2816]{0,1:T(8,128)}), f32[128,2816]{0,1:T(8,128)}) %reduce-scatter.17.cloned.1.call-update) | async-done | bytes 1441808 | tf_op jit(solution)/shard_map/reduce_scatter | solution.py:85
  1499.9 694.8 %reduce-scatter.21.cloned.1.call-done = f32[72,16128]{1,0:T(8,128)} async-done(((f32[1152,16128]{1,0:T(8,128)}), f32[72,16128]{1,0:T(8,128)}) %reduce-scatter.21.cloned.1.call-update) | async-done | bytes 4644880
  2197.3 693.7 %reduce-scatter.19.cloned.1.call-done = f32[72,16128]{1,0:T(8,128)} async-done(((f32[1152,16128]{1,0:T(8,128)}), f32[72,16128]{1,0:T(8,128)}) %reduce-scatter.19.cloned.1.call-update) | async-done | bytes 4644880
  2902.8 39.6 %psum.47 = f32[4864]{0:T(1024)S(1)} all-reduce(f32[4864]{0:T(1024)S(1)} %pad_maximum_fusion.14), channel_id=1, replica_groups=mesh['fsdp'=16,'rep'=2] {'fsdp','rep'}, use_global_device_ids=true, to_apply=%region_61.62 | all-reduce | flops 4864 | bytes 38912 | tf_op jit(solution)/shard_map/psum | solution.py:433
  2943.1 76.5 %all-reduce.6.cloned.1.call-done = f32[2,16128]{1,0:T(2,128)} async-done(((f32[2,16128]{1,0:T(2,128)}), f32[2,16128]{1,0:T(2,128)}) %all-reduce.6.cloned.1.call-update) | async-done | bytes 129040 | tf_op jit(solution)/shard_map/psum | solution.py:433
  3021.7 170.8 %all-reduce.8.cloned.1.call-done = (bf16[128,2816]{0,1:T(8,128)(2,1)}, bf16[2,72,16128]{2,1,0:T(8,128)(2,1)}, bf16[2,288,1152]{2,1,0:T(8,128)(2,1)}, bf16[72,2048]{1,0:T(8,128)(2,1)}) async-done(((bf16[128,2816]{0,1:T(8,128)(2,1)}, bf16[2,72,16128]{2,1,0:T(8,128)(2,1)}, bf16[2,288,1152]{2,1,0:T(8,128)(2,1)}, bf16[72,2048]{1,0:T(8,128)(2,1)}), (bf16[128,2816]{0,1:T(8,128)(2,1)}, ...) | async-done | bytes 6987792 | tf_op jit(solution)/shard_map/psum | solution.py:431
  3205.5 27.2 multiply_subtract_fusion
  (564 shorter events, 449.2 us)
Async XLA Ops:
  7.2 194.5 %all-gather.15.cloned.1.call-start = ((), (), s32[]{:S(2)}) async-start(), calls=%async_computation.13 | async-start | bytes 39481344 | tf_op jit(solution)/shard_map/all_gather | solution.py:54
  13.9 279.5 %all-gather.17.cloned.1.call-start = ((), (), s32[]{:S(2)}) async-start(), calls=%async_computation.14 | async-start | bytes 11280384 | tf_op jit(solution)/shard_map/all_gather | solution.py:55
  15.7 332.0 %all-gather.11.cloned.1.call-start = ((), (), s32[]{:S(2)}) async-start(), calls=%async_computation.6 | async-start | bytes 5013504 | tf_op jit(solution)/shard_map/all_gather | solution.py:349
  17.6 425.6 %all-gather.13.cloned.1.call-start = ((), (), s32[]{:S(2)}) async-start(), calls=%async_computation.7 | async-start | bytes 12255232 | tf_op jit(solution)/shard_map/all_gather | solution.py:350
  18.6 183.1 %copy-start.68 = (bf16[1,1152]{1,0:T(2,128)(2,1)S(1)}, bf16[1,1152]{1,0:T(2,128)(2,1)}, u32[]{:S(2)}) copy-start(bf16[1,1152]{1,0:T(2,128)(2,1)} %param.24) | copy-start | bytes 6916
  18.6 609.9 %all-gather.19.cloned.1.call-start = ((), (), s32[]{:S(2)}) async-start(), calls=%async_computation.15 | async-start | bytes 39481344 | tf_op jit(solution)/shard_map/all_gather | solution.py:54
  19.2 700.7 %all-gather.21.cloned.1.call-start = ((), (), s32[]{:S(2)}) async-start(), calls=%async_computation.16 | async-start | bytes 11280384 | tf_op jit(solution)/shard_map/all_gather | solution.py:55
  19.8 1101.1 %reduce-scatter.15.cloned.1.call-start = ((), (), s32[]{:S(2)}) async-start(), calls=%async_computation.10 | async-start | bytes 10027008 | tf_op jit(solution)/shard_map/reduce_scatter | solution.py:85
  24.2 186.1 %copy-start.85 = (f32[448]{0:T(512)}, f32[448]{0:T(512)S(1)}, u32[]{:S(2)}) copy-start(f32[448]{0:T(512)S(1)} %broadcast_multiply_fusion.5) | copy-start | bytes 5380
  24.6 185.0 %copy-start.93 = (f32[448]{0:T(512)}, f32[448]{0:T(512)S(1)}, u32[]{:S(2)}) copy-start(f32[448]{0:T(512)S(1)} %fusion.105) | copy-start | bytes 5380
  24.6 185.7 %copy-start.107 = (f32[448]{0:T(512)}, f32[448]{0:T(512)S(1)}, u32[]{:S(2)}) copy-start(f32[448]{0:T(512)S(1)} %fusion.159) | copy-start | bytes 5380
  347.6 95.6 %copy-start.141 = (f32[2048]{0:T(1024)S(1)}, f32[2048]{0:T(1024)}, u32[]{:S(2)}) copy-start(f32[2048]{0:T(1024)} %get-tuple-element.304) | copy-start | bytes 24580
  475.1 647.6 %reduce-scatter.13.cloned.1.call-start = ((), (), s32[]{:S(2)}) async-start(), calls=%async_computation.9 | async-start | bytes 22560768 | tf_op jit(solution)/shard_map/reduce_scatter | solution.py:76
  637.1 109.4 %copy-start.73 = (f32[1152]{0:T(1024)}, f32[1152]{0:T(1024)S(1)}, u32[]{:S(2)}) copy-start(f32[1152]{0:T(1024)S(1)} %get-tuple-element.237) | copy-start | bytes 13828
  706.7 560.4 %reduce-scatter.11.cloned.1.call-start = ((), (), s32[]{:S(2)}) async-start(), calls=%async_computation.8 | async-start | bytes 22560768 | tf_op jit(solution)/shard_map/reduce_scatter | solution.py:76
  831.5 666.1 %reduce-scatter.17.cloned.1.call-start = ((), (), s32[]{:S(2)}) async-start(), calls=%async_computation.11 | async-start | bytes 24510464 | tf_op jit(solution)/shard_map/reduce_scatter | solution.py:85
  858.9 1335.8 %reduce-scatter.21.cloned.1.call-start = ((), (), s32[]{:S(2)}) async-start(), calls=%async_computation.18 | async-start | bytes 78962688
  1043.5 1847.5 %reduce-scatter.19.cloned.1.call-start = ((), (), s32[]{:S(2)}) async-start(), calls=%async_computation.17 | async-start | bytes 78962688
  1118.6 1901.0 %all-reduce.6.cloned.1.call-start = ((), (), s32[]{:S(2)}) async-start(), calls=%async_computation.12 | async-start | bytes 258048 | tf_op jit(solution)/shard_map/psum | solution.py:433
  1120.7 2071.8 %all-reduce.8.cloned.1.call-start = ((), (), s32[]{:S(2)}) async-start(), calls=%async_computation.19 | async-start | bytes 13975552 | tf_op jit(solution)/shard_map/psum | solution.py:431
  2898.0 121.6 %copy-start.45 = (f32[2,16128]{1,0:T(2,128)S(1)}, f32[2,16128]{1,0:T(2,128)}, u32[]{:S(2)}) copy-start(f32[2,16128]{1,0:T(2,128)} %param.32) | copy-start | bytes 387076
  2898.0 121.6 %copy-start.56 = (f32[2,16128]{1,0:T(2,128)S(1)}, f32[2,16128]{1,0:T(2,128)}, u32[]{:S(2)}) copy-start(f32[2,16128]{1,0:T(2,128)} %param.44) | copy-start | bytes 387076
  2898.0 121.6 %copy-start.57 = (f32[2,16128]{1,0:T(2,128)S(1)}, f32[2,16128]{1,0:T(2,128)}, u32[]{:S(2)}) copy-start(f32[2,16128]{1,0:T(2,128)} %param.38) | copy-start | bytes 387076
  2942.4 256.9 %copy-start.61 = (f32[4864]{0:T(1024)}, f32[4864]{0:T(1024)S(1)}, u32[]{:S(2)}) copy-start(f32[4864]{0:T(1024)S(1)} %psum.47) | copy-start | bytes 58372
  (174 other events, 1662.7 us)
Sparse Core Ops, SparseCore 0:
  14.0 187.7 all-gather.14
  204.6 88.6 all-gather.16
  296.2 51.3 all-gather.10
  350.3 92.8 all-gather.12
  445.3 183.2 all-gather.18
  631.2 88.6 all-gather.20
  724.0 109.5 reduce-scatter.14
  838.3 212.6 reduce-scatter.12
  1055.1 211.9 reduce-scatter.10
  1271.6 225.9 reduce-scatter.16
  1502.7 692.0 reduce-scatter.20
  2199.0 691.9 reduce-scatter.18
  2898.0 121.5 all-reduce.5
  3024.0 168.4 all-reduce.7
where the time goes:
time: 3250 us
  waiting for transfers between devices  2500 us (77%)
  matrix products  385 us (12%)
  other arithmetic  238 us (7%)
  local copies, waits for them, and re-layouts  61.8 us (2%)
  blocking collectives  39.6 us (1%)
    unnamed x16, waiting for transfers between devices  1390 us
    all_gather x2, waiting for transfers between devices, fetch_block(): lax.all_gather(wide_shard.astype(jnp.bfloat16), 'fsdp', axis=0, tiled=True)  329 us
    reduce_scatter x2, waiting for transfers between devices, reduce_head(): lax.psum_scatter(term_fn(jnp.int32(0), lax.axis_size('fsdp') * row_count)...  228 us
    psum x1, waiting for transfers between devices, per_device(): lax.psum(second_weight_grad.astype(jnp.bfloat16), 'rep').astype(jnp.float32)  171 us
    reduce_scatter x2, waiting for transfers between devices, reduce_deep(): lax.psum_scatter(term_fn(jnp.int32(0), lax.axis_size('fsdp') * row_count)...  143 us
    concatenate x2, other arithmetic, wide_terms(): jnp.concatenate([outer_rows(silu_low, modulation_grad), outer_rows(normed...  92 us
    dot_general x11, matrix products, outer_rows(): lax.dot_general(flat_left, flat_right, (((0,), (0,)), ((), ())), preferre...  89.8 us
    all_gather x1, waiting for transfers between devices, per_device(): lax.all_gather(head_second.astype(jnp.bfloat16), 'fsdp', axis=0, tiled=True)  88.3 us
  transfers between devices with their start and end apart: 14, of which 12 were waited for; matrix products, arithmetic and copies ran while one was open for 19% of the time, Pallas kernels for 0%

commit v1 on v0

--- a/solution.py
+++ b/solution.py
@@ -41,53 +41,113 @@
     return [modulation[:, None, number * columns : (number + 1) * columns] for number in range(6)]
 
 
-def outer_rows(left, right):
-    flat_left = left.reshape(-1, left.shape[-1])
-    flat_right = right.reshape(-1, right.shape[-1])
+def ring_order(chips):
+    return list(range(0, chips, 2)) + list(range(1, chips, 2))[::-1]
+
+
+def swap_cores(values):
+    count = lax.axis_size("fsdp")
+    return lax.ppermute(values, "fsdp", [(place, place ^ 1) for place in range(count)])
+
+
+def paired_product(left, right):
+    core = lax.axis_index("fsdp") % 2
+    half = right.shape[-1] // 2
+    kept = lax.dynamic_slice_in_dim(right, core * half, half, axis=1)
+    sent = lax.dynamic_slice_in_dim(right, (1 - core) * half, half, axis=1)
+    left_both = jnp.concatenate([left, swap_cores(left)], axis=0)
+    right_both = jnp.concatenate([kept, swap_cores(sent)], axis=0)
     return lax.dot_general(
-        flat_left, flat_right, (((0,), (0,)), ((), ())), preferred_element_type=jnp.float32
-    )
+        left_both, right_both, (((0,), (0,)), ((), ())), preferred_element_type=jnp.float32
+    ).astype(jnp.bfloat16)
+
+
+def ring_reduce(term):
+    count = lax.axis_size("fsdp")
+    chips = count // 2
+    device = lax.axis_index("fsdp")
+    chip, core = device // 2, device % 2
+    order = ring_order(chips)
+    order_table = jnp.array(order, jnp.int32)
+    place = jnp.array([order.index(number) for number in range(chips)], jnp.int32)[chip]
+    parts = term.reshape(chips, 2, term.shape[0] // count, term.shape[1])
+    totals = []
+    for way, step in ((0, 1), (1, -1)):
+        route = [
+            (2 * order[spot] + side, 2 * order[(spot + step) % chips] + side)
+            for spot in range(chips)
+            for side in range(2)
+        ]
+
+        def own(hops):
+            return parts[order_table[(place - step * hops) % chips], way]
+
+        total = own(1)
+        for hop in range(1, chips):
+            total = lax.ppermute(total, "fsdp", route)
+            total = (total.astype(jnp.float32) + own(hop + 1).astype(jnp.float32)).astype(
+                jnp.bfloat16
+            )
+        totals.append(total)
+    stacked = jnp.stack(totals)
+    mine = stacked[core]
+    other = swap_cores(stacked[1 - core])
+    both = jnp.concatenate([mine, other, mine], axis=1)
+    return lax.dynamic_slice_in_dim(
+        both, core * term.shape[1], 2 * term.shape[1], axis=1
+    )
+
+
+def sum_copies(values):
+    copies = lax.axis_size("rep")
+    total = values.astype(jnp.float32)
+    if copies == 2:
+        return total + lax.ppermute(values, "rep", [(0, 1), (1, 0)]).astype(jnp.float32)
+    return lax.psum(total, "rep")
+
+
+def gathered_terms(row):
+    return lax.all_gather(row, ("fsdp", "rep"), axis=0, tiled=True)
 
 
 def fetch_block(wide_shard, deep_shard):
-    return (
-        lax.all_gather(wide_shard.astype(jnp.bfloat16), "fsdp", axis=0, tiled=True),
-        lax.all_gather(deep_shard.astype(jnp.bfloat16), "fsdp", axis=0, tiled=True),
-    )
-
-
-def fetch_block_again(wide_shard, deep_shard):
-    return (
-        lax.all_gather(wide_shard.astype(jnp.bfloat16), "fsdp", axis=0, tiled=True),
-        lax.all_gather(deep_shard.astype(jnp.bfloat16), "fsdp", axis=0, tiled=True),
-    )
-
-
-def reduce_wide(term_fn, row_count):
-    return lax.psum_scatter(
-        term_fn(jnp.int32(0), lax.axis_size("fsdp") * row_count),
-        "fsdp",
-        scatter_dimension=0,
-        tiled=True,
-    )
-
-
-def reduce_deep(term_fn, row_count):
-    return lax.psum_scatter(
-        term_fn(jnp.int32(0), lax.axis_size("fsdp") * row_count),
-        "fsdp",
-        scatter_dimension=0,
-        tiled=True,
-    )
-
-
-def reduce_head(term_fn, row_count):
-    return lax.psum_scatter(
-        term_fn(jnp.int32(0), lax.axis_size("fsdp") * row_count),
-        "fsdp",
-        scatter_dimension=0,
-        tiled=True,
-    )
+    rows = wide_shard.shape[0]
+    count = lax.axis_size("fsdp")
+    rest = wide_shard[:, 6 * MODEL_WIDTH :].astype(jnp.bfloat16)
+    groups = rest.shape[1] // MODEL_WIDTH
+    rest = rest.reshape(rows, groups, MODEL_WIDTH).transpose(1, 0, 2)
+    deep = deep_shard.astype(jnp.bfloat16).reshape(-1, rows, MODEL_WIDTH)
+    whole = lax.all_gather(
+        jnp.concatenate([rest, deep], axis=0), "fsdp", axis=1, tiled=True
+    )
+    deep_whole = whole[groups:].reshape(-1, count, rows, MODEL_WIDTH)
+    deep_whole = deep_whole.transpose(1, 0, 2, 3).reshape(-1, MODEL_WIDTH)
+    return (whole[:groups], deep_whole)
+
+
+def plane_modulation(silu_low, wide_weight, block_bias):
+    count = lax.axis_size("fsdp")
+    sequences = silu_low.shape[0]
+    rows = wide_weight.shape[1]
+    device = lax.axis_index("fsdp")
+    spread = jnp.broadcast_to(
+        silu_low.reshape(1, sequences, count, rows).transpose(2, 0, 1, 3)[:, 0],
+        (count, sequences, rows),
+    )
+    met = lax.all_to_all(spread, "fsdp", 0, 0, tiled=True)
+    met = met.reshape(count * sequences, rows)
+    partial = [
+        jnp.dot(
+            met,
+            wide_weight[block, :, : 6 * MODEL_WIDTH].astype(jnp.bfloat16),
+            preferred_element_type=jnp.float32,
+        )
+        for block in range(2)
+    ]
+    partial = jnp.stack(partial, axis=1).reshape(count, sequences, 2, 6 * MODEL_WIDTH)
+    back = lax.all_to_all(partial, "fsdp", 0, 0, tiled=True)
+    total = jnp.sum(back, axis=0)
+    return [total[:, block] + block_bias[block, : 6 * MODEL_WIDTH] for block in range(2)]
 
 
 def attention_forward(inputs):
@@ -130,12 +190,12 @@
     return (query_grad, key_grad, value_grad)
 
 
-def block_forward(hidden, silu_low, wide_matrix, deep_matrix, bias, visible):
+def joined(groups):
+    return groups.transpose(1, 0, 2).reshape(groups.shape[1], -1)
+
+
+def block_forward(hidden, modulation, wide_matrix, deep_matrix, bias, visible):
     sequences = hidden.shape[0]
-    modulation = (
-        jnp.dot(silu_low, wide_matrix[:, : 6 * MODEL_WIDTH], preferred_element_type=jnp.float32)
-        + bias[: 6 * MODEL_WIDTH]
-    )
     offset_first, factor_first, gate_first, offset_second, factor_second, gate_second = (
         split_modulation(modulation)
     )
@@ -150,7 +210,7 @@
     triple = (
         jnp.dot(
             normed_low,
-            wide_matrix[:, 6 * MODEL_WIDTH : 9 * MODEL_WIDTH],
+            wide_matrix[0],
             preferred_element_type=jnp.float32,
         )
         + triple_bias
@@ -163,7 +223,7 @@
     branch = (
         jnp.dot(
             attended_low,
-            wide_matrix[:, 9 * MODEL_WIDTH : 10 * MODEL_WIDTH],
+            wide_matrix[1],
             preferred_element_type=jnp.float32,
         )
         + bias[8 * MODEL_WIDTH : 9 * MODEL_WIDTH]
@@ -171,7 +231,7 @@
     middle = hidden + gate_first * branch
     mixed_low = modulate(middle, offset_second, factor_second).astype(jnp.bfloat16)
     pre_active = (
-        jnp.dot(mixed_low, wide_matrix[:, 10 * MODEL_WIDTH :], preferred_element_type=jnp.float32)
+        jnp.dot(mixed_low, wide_matrix[2], preferred_element_type=jnp.float32)
         + bias[9 * MODEL_WIDTH : 9 * MODEL_WIDTH + FF]
     )
     active_low = gelu_tanh(pre_active).astype(jnp.bfloat16)
@@ -197,7 +257,7 @@
     return (result, saved)
 
 
-def block_backward(upstream, saved, silu_low, wide_matrix, deep_matrix, visible):
+def block_backward(upstream, saved, wide_matrix, deep_matrix, visible):
     (
         hidden,
         modulation,
@@ -227,7 +287,7 @@
     mixed_grad = jnp.einsum(
         "qvm,am->qva",
         preactivation_gradient,
-        wide_matrix[:, 10 * MODEL_WIDTH :],
+        wide_matrix[2],
         preferred_element_type=jnp.float32,
     )
     second_back = jax.vjp(modulate, middle, offset_second, factor_second)[1]
@@ -238,7 +298,7 @@
     attended_grad = jnp.einsum(
         "tbr,ar->tba",
         branch_gradient,
-        wide_matrix[:, 9 * MODEL_WIDTH : 10 * MODEL_WIDTH],
+        wide_matrix[1],
         preferred_element_type=jnp.float32,
     ).astype(jnp.bfloat16)
     pieces = triple.reshape(sequences, SEQ_LEN, 3, HEADS, HEAD_DIM)
@@ -258,7 +318,7 @@
     normed_grad = jnp.einsum(
         "tbr,ar->tba",
         triple_gradient,
-        wide_matrix[:, 6 * MODEL_WIDTH : 9 * MODEL_WIDTH],
+        wide_matrix[0],
         preferred_element_type=jnp.float32,
     )
     first_back = jax.vjp(modulate, hidden, offset_first, factor_first)[1]
@@ -275,9 +335,9 @@
         ],
         axis=-1,
     ).astype(jnp.bfloat16)
-    bias_grad = jnp.concatenate(
+    bias_row = jnp.concatenate(
         [
-            jnp.sum(modulation_grad, axis=0, dtype=jnp.float32),
+            modulation_grad.astype(jnp.float32).sum(axis=0),
             jnp.sum(triple_gradient[..., :MODEL_WIDTH], axis=(0, 1), dtype=jnp.float32),
             jnp.sum(triple_gradient[..., 2 * MODEL_WIDTH :], axis=(0, 1), dtype=jnp.float32),
             jnp.sum(branch_gradient, axis=(0, 1), dtype=jnp.float32),
@@ -286,21 +346,16 @@
         ]
     )
 
-    def wide_terms(first_row, row_total):
-        return jnp.concatenate(
-            [
-                outer_rows(silu_low, modulation_grad),
-                outer_rows(normed_low, triple_gradient),
-                outer_rows(attended_low, branch_gradient),
-                outer_rows(mixed_low, preactivation_gradient),
-            ],
-            axis=1,
-        )
-
-    def deep_terms(first_row, row_total):
-        return outer_rows(active_low, feedforward_gradient)
-
-    return (hidden_grad, bias_grad, wide_terms, deep_terms)
+    def flat(values):
+        return values.reshape(-1, values.shape[-1])
+
+    deep_grad = ring_reduce(paired_product(flat(active_low), flat(feedforward_gradient)))
+    pre_grad = ring_reduce(paired_product(flat(mixed_low), flat(preactivation_gradient)))
+    branch_grad = ring_reduce(paired_product(flat(attended_low), flat(branch_gradient)))
+    triple_grad = ring_reduce(paired_product(flat(normed_low), flat(triple_gradient)))
+    rest_grad = sum_copies(jnp.concatenate([triple_grad, branch_grad, pre_grad], axis=1))
+    deep_grad = sum_copies(deep_grad)
+    return (hidden_grad, modulation_grad, bias_row, rest_grad, deep_grad)
 
 
 def adam_update(weight, grad, first, second, rate, decay):
@@ -342,8 +397,10 @@
     silu_low = jax.nn.silu(condition.astype(jnp.float32)).astype(jnp.bfloat16)
     visible = jnp.arange(SEQ_LEN, dtype=jnp.int32)[None, :] < lengths[:, None]
     wide_early, deep_early = fetch_block(wide_weight[0], deep_weight[0])
+    modulation_early, modulation_late = plane_modulation(silu_low, wide_weight, block_bias)
+    wide_early = [joined(wide_early[:3]), wide_early[3], joined(wide_early[4:])]
     tapped, saved_early = block_forward(
-        hidden, silu_low, wide_early, deep_early, block_bias[0], visible
+        hidden, modulation_early, wide_early, deep_early, block_bias[0], visible
     )
     first_matrix, second_w = (
         lax.all_gather(head_first.astype(jnp.bfloat16), "fsdp", axis=0, tiled=True),
@@ -364,8 +421,9 @@
         + head_bias[2 * PH :]
     )
     wide_late, deep_late = fetch_block(wide_weight[1], deep_weight[1])
+    wide_late = [joined(wide_late[:3]), wide_late[3], joined(wide_late[4:])]
     final, saved_late = block_forward(
-        tapped, silu_low, wide_late, deep_late, block_bias[1], visible
+        tapped, modulation_late, wide_late, deep_late, block_bias[1], visible
     )
     raw_targets = targets.astype(jnp.float32).reshape(sequences, SEQ_LEN, PZ)
     target_unit = raw_targets * lax.rsqrt(
@@ -376,15 +434,10 @@
         unit = values * lax.rsqrt(jnp.sum(values * values, axis=-1, keepdims=True) + norm_epsilon)
         return jnp.sum(unit * target_unit, axis=-1)
 
-    wide_late, deep_late = fetch_block_again(wide_weight[1], deep_weight[1])
-    second_w = lax.all_gather(head_second.astype(jnp.bfloat16), "fsdp", axis=0, tiled=True)
-    wide_early, deep_early = fetch_block_again(wide_weight[0], deep_weight[0])
     upstream = cotangent.astype(jnp.float32).reshape(sequences, SEQ_LEN, MODEL_WIDTH)
-    late_input_grad, late_bias_grad, late_wide_fn, late_deep_fn = block_backward(
-        upstream, saved_late, silu_low, wide_late, deep_late, visible
-    )
-    late_wide_grad = reduce_wide(late_wide_fn, wide_weight.shape[1])
-    late_deep_grad = reduce_deep(late_deep_fn, deep_weight.shape[1])
+    late_input_grad, late_modulation_grad, late_row, late_rest_grad, late_deep_grad = (
+        block_backward(upstream, saved_late, wide_late, deep_late, visible)
+    )
     projected_grad = jax.vjp(alignment, projected)[1](-repa_weight * visible.astype(jnp.float32))[
         0
     ].astype(jnp.bfloat16)
@@ -399,7 +452,7 @@
     tapped_gradient = jnp.einsum(
         "ejk,rk->ejr", first_gradient, first_matrix, preferred_element_type=jnp.float32
     )
-    head_bias_grad = jnp.concatenate(
+    head_row = jnp.concatenate(
         [
             jnp.sum(first_gradient, axis=(0, 1), dtype=jnp.float32),
             jnp.sum(second_grad, axis=(0, 1), dtype=jnp.float32),
@@ -407,32 +460,55 @@
         ]
     )
 
-    def first_terms(first_row, row_total):
-        return outer_rows(tapped_low, first_gradient)
-
-    def second_terms(first_row, row_total):
-        return jnp.concatenate(
-            [outer_rows(first_low, second_grad), outer_rows(second_low, projected_grad)], axis=1
+    def flat(values):
+        return values.reshape(-1, values.shape[-1])
+
+    first_weight_grad = sum_copies(
+        ring_reduce(paired_product(flat(tapped_low), flat(first_gradient)))
+    )
+    second_weight_grad = sum_copies(
+        jnp.concatenate(
+            [
+                ring_reduce(paired_product(flat(first_low), flat(second_grad))),
+                ring_reduce(paired_product(flat(second_low), flat(projected_grad))),
+            ],
+            axis=1,
         )
-
-    first_weight_grad = reduce_head(first_terms, head_first.shape[0])
-    second_weight_grad = reduce_head(second_terms, head_second.shape[0])
-    input_grad, early_bias_grad, early_wide_fn, early_deep_fn = block_backward(
-        late_input_grad + tapped_gradient, saved_early, silu_low, wide_early, deep_early, visible
-    )
-    early_wide_grad = reduce_wide(early_wide_fn, wide_weight.shape[1])
-    early_deep_grad = reduce_deep(early_deep_fn, deep_weight.shape[1])
-    wide_grad = jnp.stack([early_wide_grad, late_wide_grad])
+    )
+    input_grad, early_modulation_grad, early_row, early_rest_grad, early_deep_grad = (
+        block_backward(
+            late_input_grad + tapped_gradient, saved_early, wide_early, deep_early, visible
+        )
+    )
+    all_silu = gathered_terms(silu_low)
+    own_silu = lax.dynamic_slice_in_dim(
+        all_silu,
+        lax.axis_index("fsdp") * wide_weight.shape[1],
+        wide_weight.shape[1],
+        axis=1,
+    )
+    late_rows = gathered_terms(jnp.concatenate([late_row, head_row])[None])
+    early_rows = gathered_terms(early_row[None])
+
+    def modulation_weight_grad(rows):
+        return lax.dot_general(
+            own_silu,
+            rows[:, : 6 * MODEL_WIDTH].astype(jnp.bfloat16),
+            (((0,), (0,)), ((), ())),
+            preferred_element_type=jnp.float32,
+        )
+
+    bias_width = block_bias.shape[1]
+    wide_grad = jnp.stack(
+        [
+            jnp.concatenate([modulation_weight_grad(early_rows), early_rest_grad], axis=1),
+            jnp.concatenate([modulation_weight_grad(late_rows), late_rest_grad], axis=1),
+        ]
+    )
     deep_grad = jnp.stack([early_deep_grad, late_deep_grad])
-    wide_grad, deep_grad, first_weight_grad, second_weight_grad = (
-        lax.psum(wide_grad.astype(jnp.bfloat16), "rep").astype(jnp.float32),
-        lax.psum(deep_grad.astype(jnp.bfloat16), "rep").astype(jnp.float32),
-        lax.psum(first_weight_grad.astype(jnp.bfloat16), "rep").astype(jnp.float32),
-        lax.psum(second_weight_grad.astype(jnp.bfloat16), "rep").astype(jnp.float32),
-    )
-    block_bias_grad, head_bias_total = lax.psum(
-        (jnp.stack([early_bias_grad, late_bias_grad]), head_bias_grad), ("fsdp", "rep")
-    )
+    late_sum = jnp.sum(late_rows, axis=0)
+    block_bias_grad = jnp.stack([jnp.sum(early_rows, axis=0), late_sum[:bias_width]])
+    head_bias_total = late_sum[bias_width:]
     wide_m, wide_v, wide_new = adam_update(
         wide_weight, wide_grad, wide_mean, wide_square, matrix_rate, matrix_decay
     )

time: 3250 us -> 1480 us (0.46)
  waiting for transfers between devices: 2500 us -> 325 us
  local copies, waits for them, and re-layouts: 61.8 us -> 273 us
  starting transfers between devices: 1.36 us -> 192 us
  other arithmetic: 238 us -> 189 us
  between operations: 16.9 us -> 59.7 us
    unnamed x16 -> x6, waiting for transfers between devices: 1390 us -> 0.1 us
    reduce_scatter x4 -> x0, waiting for transfers between devices: 371 us -> none  [the longest x2 228 us: reduce_head(): lax.psum_scatter(term_fn(jnp.int32(0), lax.axis_size('fsdp') * row_count)...]
    all_gather x4, waiting for transfers between devices: 368 us -> 67.8 us  [the longest x2 67.8 us: fetch_block(): lax.all_gather(jnp.concatenate([rest, deep], axis=0), 'fsdp', axis=1, til...]
    ppermute x0 -> x193, waiting for transfers between devices: none -> 257 us  [the longest x154 248 us: ring_reduce(): total = lax.ppermute(total, 'fsdp', route)]
    psum x2 -> x0, waiting for transfers between devices: 247 us -> none  [the longest x1 171 us: per_device(): lax.psum(second_weight_grad.astype(jnp.bfloat16), 'rep').astype(jnp.float32)]
    ppermute x0 -> x193, starting transfers between devices: none -> 180 us  [the longest x154 168 us: ring_reduce(): total = lax.ppermute(total, 'fsdp', route)]
    concatenate x4 -> x12, other arithmetic: 107 us -> 7.82 us  [the longest x2 2.57 us: block_backward(): jnp.concatenate([query_grad.reshape(sequences, SEQ_LEN, MODEL_WIDTH), key...]
    all_gather x1, waiting for transfers between devices: 88.3 us -> 0.01 us  [per_device(): lax.all_gather(head_second.astype(jnp.bfloat16), 'fsdp', axis=0, tiled=True)]
  transfers between devices with their start and end apart: 14 -> 201, of which waited for: 12 -> 97; matrix products, arithmetic and copies ran while one was open for 19% -> 47% of each run, Pallas kernels for 0% -> 0%
where the time goes in v1:
time: 1480 us; the launch traced here: 1470 us
  matrix products  356 us (24%)
  waiting for transfers between devices  325 us (22%)
  local copies, waits for them, and re-layouts  273 us (18%)
  starting transfers between devices  192 us (13%)
  other arithmetic  189 us (13%)
  blocking collectives  71.1 us (5%)
  between operations  59.7 us (4%)
    ppermute x154, waiting for transfers between devices, ring_reduce(): total = lax.ppermute(total, 'fsdp', route)  248 us
    ppermute x154, starting transfers between devices, ring_reduce(): total = lax.ppermute(total, 'fsdp', route)  168 us
    unnamed x401, local copies, waits for them, and re-layouts  93.9 us
    dot_general x11, matrix products, paired_product(): lax.dot_general(left_both, right_both, (((0,), (0,)), ((), ())), preferre...  77.4 us
    all_gather x1, blocking collectives, gathered_terms(): return lax.all_gather(row, ('fsdp', 'rep'), axis=0, tiled=True)  71.1 us
    all_gather x2, waiting for transfers between devices, fetch_block(): lax.all_gather(jnp.concatenate([rest, deep], axis=0), 'fsdp', axis=1, til...  67.8 us
    convert_element_type x66, other arithmetic, ring_reduce(): (total.astype(jnp.float32) + own(hop + 1).astype(jnp.float32)).astype(jnp...  46.2 us
    sub x6, other arithmetic, adam_update(): weight - rate * (first_hat / (jnp.sqrt(second_hat) + adam_epsilon) + deca...  40.5 us
  transfers between devices with their start and end apart: 201, of which 97 were waited for; matrix products, arithmetic and copies ran while one was open for 47% of the time, Pallas kernels for 0%

profile of v1, /device:TPU:0, one launch (start us, length us, event | category | flops | bytes accessed | tf_op | source)
XLA Modules:
  0.0 1465.9 jit_solution(4547568303329232723)
XLA Ops:
  31.2 71.1 %all-gather.2 = bf16[32,1,1152]{2,1,0:T(2,128)(2,1)S(1)} all-gather(bf16[1,1,1152]{2,1,0:T(2,128)(2,1)S(1)} %bitcast.1012), channel_id=1, replica_groups=mesh['fsdp'=16,'rep'=2] {'fsdp','rep'}, dimensions={0}, use_global_device_ids=true | all-gather | bytes 76032 | tf_op jit(solution)/shard_map/all_gather | solution.py:110
  164.9 30.9 %all-gather.12.cloned.1.call-done = bf16[12,1152,1152]{2,1,0:T(8,128)(2,1)} async-done(((bf16[12,72,1152]{2,1,0:T(8,128)(2,1)}), bf16[12,1152,1152]{2,1,0:T(8,128)(2,1)}) %all-gather.12.cloned.1.call-update) | async-done | bytes 31850512 | tf_op jit(solution)/shard_map/all_gather | solution.py:120
  202.9 13.0 copy.317
  216.0 9.9 add_convert_fusion.1
  259.9 16.4 %fusion.455 = (bf16[4,1152,1152]{2,1,0:T(8,128)(2,1)}, bf16[4,1152,1152]{2,1,0:T(8,128)(2,1)}) fusion(bf16[12,1152,1152]{2,1,0:T(8,128)(2,1)} %all-gather.12.cloned.1.call-done), kind=kLoop, calls=%fused_computation.909 | loop fusion | bytes 42467328 | tf_op jit(solution)/shard_map/slice | solution.py:123
  276.4 15.1 %copy.318 = bf16[4,1152,1152]{1,2,0:T(8,128)(2,1)} copy(bf16[4,1152,1152]{2,1,0:T(8,128)(2,1)} %get-tuple-element.222) | data formatting | bytes 21233664
  291.5 11.3 copy.275
  312.6 11.9 fusion.451
  325.1 36.9 %all-gather.14.cloned.1.call-done = bf16[12,1152,1152]{2,1,0:T(8,128)(2,1)} async-done(((bf16[12,72,1152]{2,1,0:T(8,128)(2,1)}), bf16[12,1152,1152]{2,1,0:T(8,128)(2,1)}) %all-gather.14.cloned.1.call-update) | async-done | bytes 31850512 | tf_op jit(solution)/shard_map/all_gather | solution.py:120
  369.1 12.9 copy.319
  398.6 13.7 fusion.454
  424.1 16.1 %copy.320 = bf16[4,1152,1152]{1,2,0:T(8,128)(2,1)} copy(bf16[4,1152,1152]{2,1,0:T(8,128)(2,1)} %get-tuple-element.220) | data formatting | bytes 21233664
  463.0 13.0 fusion.461
  476.0 16.3 %convert_reduce_fusion = (f32[4608]{0:T(1024)}, bf16[448,4608]{1,0:T(8,128)(2,1)S(1)}, bf16[448,4608]{1,0:T(8,128)(2,1)}) fusion(f32[448,4608]{1,0:T(8,128)} %fusion.461, f32[4608]{0:T(1024)S(1)} %copy-done.134, bf16[448,1152]{1,0:T(8,128)(2,1)S(1)} %add_convert_fusion.3, bf16[1152,4608]{0,1:T(8,128)(2,1)} %bitcast.931), kind=kOutput, calls=%fused_computation.49 | convolution fusion | flops 4807945728 | bytes 28200960 | tf_op jit(solution)/shard_map/dot_general | solution.py:234
  492.3 11.9 multiply_reduce_fusion.2
  507.1 12.5 fusion.104
  527.4 15.0 %multiply_reduce_fusion.1 = (f32[16,448]{1,0:T(8,128)}, f32[16,448,448]{1,2,0:T(8,128)}) fusion(f32[16,448,448]{1,2,0:T(8,128)} %get-tuple-element.485, f32[16,448]{1,0:T(8,128)S(1)} %log_add_fusion.1, bf16[448,16,72]{0,2,1:T(8,128)(2,1)} %bitcast.913, bf16[1,448,3,16,72]{1,4,3,2,0:T(8,128)(2,1)} %bitcast.871), kind=kOutput, calls=%fused_computation.4 | convolution fusion | flops 472048640 | bytes 29941760 | tf_op jit(solution)/shard_map/while/body/eval_jaxpr/qhd,khd->hqk/dot_general | solution.py:176
  581.5 10.0 multiply_convert_fusion.4
  599.2 10.6 convert_reduce_fusion.3
  618.2 14.2 convert_reduce_fusion.1
  648.7 12.7 multiply_reduce_fusion
  1258.6 9.7 fusion.30
  1270.3 9.8 fusion.27
  1423.0 27.3 %multiply_subtract_fusion = (f32[2,72,16128]{2,1,0:T(8,128)}, f32[2,72,16128]{2,1,0:T(8,128)}, f32[2,72,16128]{2,1,0:T(8,128)}, f32[2,72,16128]{2,1,0:T(8,128)}) fusion(f32[2,72,16128]{2,1,0:T(8,128)} %param.50, f32[2,72,16128]{2,1,0:T(8,128)} %param.62, f32[2,72,16128]{2,1,0:T(8,128)} %param.56, f32[1,72,16128]{2,1,0:T(8,128)} %maximum_bitcast_fusion.1, ...), kind=kLoop, calls=%fused_computation.25 | loop fusion | flops 37158912 | bytes 74317824 | tf_op jit(solution)/shard_map/sub | solution.py:366
  (1103 shorter events, 983.7 us)
Async XLA Ops:
  7.2 188.6 %all-gather.12.cloned.1.call-start = ((), (), s32[]{:S(2)}) async-start(), calls=%async_computation.2 | async-start | bytes 33841152 | tf_op jit(solution)/shard_map/all_gather | solution.py:120
  17.9 344.1 %all-gather.14.cloned.1.call-start = ((), (), s32[]{:S(2)}) async-start(), calls=%async_computation.3 | async-start | bytes 33841152 | tf_op jit(solution)/shard_map/all_gather | solution.py:120
  20.5 552.9 %all-gather.16.cloned.1.call-start = ((), (), s32[]{:S(2)}) async-start(), calls=%async_computation.4 | async-start | bytes 5013504 | tf_op jit(solution)/shard_map/all_gather | solution.py:406
  22.1 81.5 %all-to-all-start = ((bf16[16,1,72]{2,1,0:T(2,128)(2,1)}), bf16[16,1,72]{2,1,0:T(2,128)(2,1)S(1)}, u32[]{:S(2)}, u32[]{:S(2)}) async-start(bf16[16,1,72]{2,1,0:T(2,128)(2,1)} %squeeze_transpose_reshape.4), calls=%async_computation | async-start | bytes 16384 | tf_op jit(solution)/shard_map/all_to_all | solution.py:137
  29.5 551.9 %all-gather.18.cloned.1.call-start = ((), (), s32[]{:S(2)}) async-start(), calls=%async_computation.5 | async-start | bytes 12255232 | tf_op jit(solution)/shard_map/all_gather | solution.py:407
  108.3 51.0 %all-to-all-start.1 = ((f32[16,1,2,6912]{3,2,1,0:T(2,128)}), f32[16,1,2,6912]{3,2,1,0:T(2,128)S(1)}, u32[]{:S(2)}, u32[]{:S(2)}) async-start(f32[16,1,2,6912]{3,2,1,0:T(2,128)} %copy.268), calls=%async_computation.1 | async-start | bytes 1769472 | tf_op jit(solution)/shard_map/all_to_all | solution.py:148
  112.1 1126.3 %all-gather.20.cloned.1.call-start = ((), (), s32[]{:S(2)}) async-start(), calls=%async_computation.6 | async-start | bytes 2128896 | tf_op jit(solution)/shard_map/all_gather | solution.py:110
  681.9 93.9 %collective-permute-start.140 = (bf16[448,1152]{1,0:T(8,128)(2,1)}, bf16[448,1152]{1,0:T(8,128)(2,1)}, u32[]{:S(2)}, u32[]{:S(2)}) collective-permute-start(bf16[448,1152]{1,0:T(8,128)(2,1)} %get-tuple-element.211), channel_id=1, source_target_pairs={{0,2},{2,0},{4,6},{6,4},{8,10},{10,8},{12,14},{14,12},{16,18},{18,... | collective-permute-start | bytes 3096584 | tf_op jit(solution)/shard_map/ppermute | solution.py:50
  713.7 641.6 %all-gather.22.cloned.1.call-start = ((), (), s32[]{:S(2)}) async-start(), calls=%async_computation.7 | async-start | bytes 2770944 | tf_op jit(solution)/shard_map/all_gather | solution.py:110
  733.9 41.5 %collective-permute-start.141 = (bf16[448,1024]{1,0:T(8,128)(2,1)}, bf16[448,1024]{1,0:T(8,128)(2,1)}, u32[]{:S(2)}, u32[]{:S(2)}) collective-permute-start(bf16[448,1024]{1,0:T(8,128)(2,1)} %get-tuple-element.371), channel_id=1, source_target_pairs={{0,2},{2,0},{4,6},{6,4},{8,10},{10,8},{12,14},{14,12},{16,18},{18,... | collective-permute-start | bytes 2752520 | tf_op jit(solution)/shard_map/ppermute | solution.py:50
  769.5 99.8 %collective-permute-start = (bf16[448,1152]{1,0:T(8,128)(2,1)}, bf16[448,1152]{1,0:T(8,128)(2,1)}, u32[]{:S(2)}, u32[]{:S(2)}) collective-permute-start(bf16[448,1152]{1,0:T(8,128)(2,1)} %fusion.99), channel_id=1, source_target_pairs={{0,2},{2,0},{4,6},{6,4},{8,10},{10,8},{12,14},{14,12},{16,18},{18,... | collective-permute-start | bytes 3096584 | tf_op jit(solution)/shard_map/ppermute | solution.py:50
  775.4 94.4 %collective-permute-start.1 = (bf16[448,1728]{1,0:T(8,128)(2,1)}, bf16[448,1728]{1,0:T(8,128)(2,1)}, u32[]{:S(2)}, u32[]{:S(2)}) collective-permute-start(bf16[448,1728]{1,0:T(8,128)(2,1)} %bitcast.70), channel_id=1, source_target_pairs={{0,2},{2,0},{4,6},{6,4},{8,10},{10,8},{12,14},{14,12},{16,18},{18,... | collective-permute-start | bytes 4644872 | tf_op jit(solution)/shard_map/ppermute | solution.py:50
  775.8 110.8 %collective-permute-start.53 = (bf16[448,1728]{1,0:T(8,128)(2,1)}, bf16[448,1728]{1,0:T(8,128)(2,1)}, u32[]{:S(2)}, u32[]{:S(2)}) collective-permute-start(bf16[448,1728]{1,0:T(8,128)(2,1)} %bitcast.175), channel_id=1, source_target_pairs={{0,2},{2,0},{4,6},{6,4},{8,10},{10,8},{12,14},{14,12},{16,18},{18,... | collective-permute-start | bytes 4644872 | tf_op jit(solution)/shard_map/ppermute | solution.py:50
  865.3 85.5 %collective-permute-start.158 = (bf16[448,2048]{1,0:T(8,128)(2,1)}, bf16[448,2048]{1,0:T(8,128)(2,1)}, u32[]{:S(2)}, u32[]{:S(2)}) collective-permute-start(bf16[448,2048]{1,0:T(8,128)(2,1)} %get-tuple-element.488), channel_id=1, source_target_pairs={{0,2},{2,0},{4,6},{6,4},{8,10},{10,8},{12,14},{14,12},{16,18},{18,... | collective-permute-start | bytes 5505032 | tf_op jit(solution)/shard_map/ppermute | solution.py:50
  869.3 75.0 %collective-permute-start.175 = (bf16[448,2048]{1,0:T(8,128)(2,1)}, bf16[448,2048]{1,0:T(8,128)(2,1)}, u32[]{:S(2)}, u32[]{:S(2)}) collective-permute-start(bf16[448,2048]{1,0:T(8,128)(2,1)} %get-tuple-element.490), channel_id=1, source_target_pairs={{0,2},{2,0},{4,6},{6,4},{8,10},{10,8},{12,14},{14,12},{16,18},{18,... | collective-permute-start | bytes 5505032 | tf_op jit(solution)/shard_map/ppermute | solution.py:50
  869.8 43.6 %collective-permute-start.145 = (bf16[72,1024]{1,0:T(8,128)(2,1)S(1)}, bf16[72,1024]{1,0:T(8,128)(2,1)}, u32[]{:S(2)}, u32[]{:S(2)}) collective-permute-start(bf16[72,1024]{1,0:T(8,128)(2,1)S(1)} %get-tuple-element.357), channel_id=1, source_target_pairs={{0,8},{2,10},{8,16},{10,18},{16,24},{18,26},{24,28},{26,30},{28,20... | collective-permute-start | bytes 442376 | tf_op jit(solution)/shard_map/ppermute | solution.py:87
  942.1 45.0 %collective-permute-start.35 = (bf16[448,2304]{1,0:T(8,128)(2,1)S(1)}, bf16[448,2304]{1,0:T(8,128)(2,1)S(1)}, u32[]{:S(2)}, u32[]{:S(2)}) collective-permute-start(bf16[448,2304]{1,0:T(8,128)(2,1)S(1)} %copy-done.57), channel_id=1, source_target_pairs={{0,2},{2,0},{4,6},{6,4},{8,10},{10,8},{12,14},{14,12},{16,18},{18,... | collective-permute-start | bytes 6193160 | tf_op jit(solution)/shard_map/ppermute | solution.py:50
  984.8 283.5 %collective-permute-start.123 = (bf16[448,576]{1,0:T(8,128)(2,1)}, bf16[448,576]{1,0:T(8,128)(2,1)}, u32[]{:S(2)}, u32[]{:S(2)}) collective-permute-start(bf16[448,576]{1,0:T(8,128)(2,1)} %get-tuple-element.425), channel_id=1, source_target_pairs={{0,2},{2,0},{4,6},{6,4},{8,10},{10,8},{12,14},{14,12},{16,18},{18,... | collective-permute-start | bytes 1548296 | tf_op jit(solution)/shard_map/ppermute | solution.py:50
  1034.6 223.2 %collective-permute-start.104 = (bf16[448,4608]{1,0:T(8,128)(2,1)}, bf16[448,4608]{1,0:T(8,128)(2,1)}, u32[]{:S(2)}, u32[]{:S(2)}) collective-permute-start(bf16[448,4608]{1,0:T(8,128)(2,1)} %get-tuple-element.481), channel_id=1, source_target_pairs={{0,2},{2,0},{4,6},{6,4},{8,10},{10,8},{12,14},{14,12},{16,18},{18,... | collective-permute-start | bytes 12386312 | tf_op jit(solution)/shard_map/ppermute | solution.py:50
  1082.9 187.1 %collective-permute-start.122 = (bf16[448,4608]{1,0:T(8,128)(2,1)}, bf16[448,4608]{1,0:T(8,128)(2,1)}, u32[]{:S(2)}, u32[]{:S(2)}) collective-permute-start(bf16[448,4608]{1,0:T(8,128)(2,1)} %get-tuple-element.223), channel_id=1, source_target_pairs={{0,2},{2,0},{4,6},{6,4},{8,10},{10,8},{12,14},{14,12},{16,18},{18,... | collective-permute-start | bytes 12386312 | tf_op jit(solution)/shard_map/ppermute | solution.py:50
  1254.0 65.2 %collective-permute-start.192 = (bf16[128,2816]{1,0:T(8,128)(2,1)S(1)}, bf16[128,2816]{1,0:T(8,128)(2,1)S(1)}, u32[]{:S(2)}, u32[]{:S(2)}) collective-permute-start(bf16[128,2816]{1,0:T(8,128)(2,1)S(1)} %copy-done.79), channel_id=1, source_target_pairs={{0,1},{1,0},{2,3},{3,2},{4,5},{5,4},{6,7},{7,6},{8,9},{9,8},{10,11... | collective-permute-start | bytes 2162696 | tf_op jit(solution)/shard_map/ppermute | solution.py:105
  1256.5 42.7 %collective-permute-start.42 = (bf16[72,2304]{1,0:T(8,128)(2,1)}, bf16[72,2304]{1,0:T(8,128)(2,1)}, u32[]{:S(2)}, u32[]{:S(2)}) collective-permute-start(bf16[72,2304]{1,0:T(8,128)(2,1)} %get-tuple-element.259), channel_id=1, source_target_pairs={{0,8},{2,10},{8,16},{10,18},{16,24},{18,26},{24,28},{26,30},{28,20... | collective-permute-start | bytes 995336 | tf_op jit(solution)/shard_map/ppermute | solution.py:87
  1257.8 43.0 %collective-permute-start.49 = (bf16[72,2304]{1,0:T(8,128)(2,1)}, bf16[72,2304]{1,0:T(8,128)(2,1)}, u32[]{:S(2)}, u32[]{:S(2)}) collective-permute-start(bf16[72,2304]{1,0:T(8,128)(2,1)} %get-tuple-element.258), channel_id=1, source_target_pairs={{0,4},{2,6},{8,0},{10,2},{16,8},{18,10},{24,16},{26,18},{28,24},{3... | collective-permute-start | bytes 995336 | tf_op jit(solution)/shard_map/ppermute | solution.py:87
  1325.7 62.7 %collective-permute-start.51 = (bf16[72,9216]{1,0:T(8,128)(2,1)}, bf16[72,9216]{1,0:T(8,128)(2,1)}, u32[]{:S(2)}, u32[]{:S(2)}) collective-permute-start(bf16[72,9216]{1,0:T(8,128)(2,1)} %pad_maximum_fusion.6), channel_id=1, source_target_pairs={{0,1},{1,0},{2,3},{3,2},{4,5},{5,4},{6,7},{7,6},{8,9},{9,8},{10,11... | collective-permute-start | bytes 3981320 | tf_op jit(solution)/shard_map/ppermute | solution.py:105
  (364 other events, 5251.1 us)
Sparse Core Ops, SparseCore 0:
  18.0 177.8 all-gather.11
  198.0 163.9 all-gather.13
  364.8 53.2 all-gather.15
  420.2 92.8 all-gather.17
  713.8 56.3 all-gather.19
  773.0 60.4 all-gather.21

commit v2 on v1

--- a/solution.py
+++ b/solution.py
@@ -1,7 +1,14 @@
+from functools import partial
+from typing import NamedTuple
+
 import jax
 import jax.numpy as jnp
 from jax import lax
+from jax.experimental import pallas as pl
+from jax.experimental.pallas import tpu as pltpu
 from jax.sharding import PartitionSpec as P
+
+MESH = pl.DeviceIdType.MESH
 
 MODEL_WIDTH = 1152
 HEADS = 16
@@ -41,8 +48,12 @@
     return [modulation[:, None, number * columns : (number + 1) * columns] for number in range(6)]
 
 
-def ring_order(chips):
-    return list(range(0, chips, 2)) + list(range(1, chips, 2))[::-1]
+def outer_rows(left, right):
+    flat_left = left.reshape(-1, left.shape[-1])
+    flat_right = right.reshape(-1, right.shape[-1])
+    return lax.dot_general(
+        flat_left, flat_right, (((0,), (0,)), ((), ())), preferred_element_type=jnp.float32
+    )
 
 
 def swap_cores(values):
@@ -50,60 +61,404 @@
     return lax.ppermute(values, "fsdp", [(place, place ^ 1) for place in range(count)])
 
 
-def paired_product(left, right):
+class Term(NamedTuple):
+    left: int
+    right: int
+    rows: int
+    row_from: int
+    columns: int
+    column_from: int
+    split: bool
+    way: int
+    start: int
+
+
+def ring_place(chip, chips):
+    return lax.div(chip, 2) + lax.rem(chip, 2) * (chips - 1 - 2 * lax.div(chip, 2))
+
+
+def ring_chip(place, chips):
+    upper = lax.div(place, (chips + 1) // 2)
+    return 2 * place + upper * (2 * (chips - 1 - place) + 1 - 2 * place)
+
+
+def reduce_body(terms, chips, lefts, rights, *refs):
+    refs = list(refs)
+
+    def take(count):
+        taken = refs[:count]
+        del refs[:count]
+        return taken
+
+    left_refs, right_refs = take(lefts), take(rights)
+    outs = take(len(terms))
+    own_left, own_right = take(lefts), take(rights)
+    sib_left, sib_right = take(lefts), take(rights)
+    landing, final = take(len(terms)), take(len(terms))
+    split_at = [number for number, term in enumerate(terms) if term.split]
+    give, got = take(len(split_at)), take(len(split_at))
+    load_sem, swap_send, swap_recv, ring_send, ring_recv = take(5)
+    give_send, got_recv, final_send, final_recv = take(4)
+
+    device = lax.axis_index("fsdp")
+    plane = lax.axis_index("rep")
+    core, chip = lax.rem(device, 2), lax.div(device, 2)
+    place = ring_place(chip, chips)
+    sibling = {"fsdp": device + 1 - 2 * core}
+    twin = {"rep": 1 - plane}
+    ways = [
+        {"fsdp": 2 * ring_chip(lax.rem(place + step, chips), chips) + core}
+        for step in (1, chips - 1)
+    ]
+
+    barrier = pltpu.get_barrier_semaphore()
+    partners = (ways[0], ways[1], sibling, twin)
+    for partner in partners:
+        pl.semaphore_signal(barrier, inc=1, device_id=partner, device_id_type=MESH)
+    pl.semaphore_wait(barrier, len(partners))
+
+    def remote(source, target, send_sem, recv_sem, partner):
+        return pltpu.make_async_remote_copy(
+            src_ref=source,
+            dst_ref=target,
+            send_sem=send_sem,
+            recv_sem=recv_sem,
+            device_id=partner,
+            device_id_type=MESH,
+        )
+
+    loads, swaps = {}, {}
+    for number in range(lefts):
+        ref = left_refs[number]
+        by_rows = len(ref.shape) == 4
+        mine = ref.at[:, core] if by_rows else ref
+        other = ref.at[:, 1 - core] if by_rows else ref
+        loads["l", number] = pltpu.make_async_copy(mine, own_left[number], load_sem.at[number])
+        swaps["l", number] = remote(
+            other, sib_left[number], swap_send.at[number], swap_recv.at[number], sibling
+        )
+    for number in range(rights):
+        ref, at = right_refs[number], lefts + number
+        width = own_right[number].shape[1]
+        if width == ref.shape[1]:
+            mine = other = ref
+        else:
+            mine = ref.at[:, pl.ds(pl.multiple_of(core * width, 128), width)]
+            other = ref.at[:, pl.ds(pl.multiple_of((1 - core) * width, 128), width)]
+        loads["r", number] = pltpu.make_async_copy(mine, own_right[number], load_sem.at[at])
+        swaps["r", number] = remote(
+            other, sib_right[number], swap_send.at[at], swap_recv.at[at], sibling
+        )
+    first_use = {}
+    for term in sorted(terms, key=lambda term: term.start - term.split):
+        for key in (("l", term.left), ("r", term.right)):
+            first_use.setdefault(key, term.start - term.split)
+    for key in first_use:
+        loads[key].start()
+        swaps[key].start()
+    for number, term in enumerate(terms):
+        landing[number][0] = jnp.zeros(landing[number].shape[1:], jnp.bfloat16)
+
+    def chunk(term, owner, part):
+        rows = pl.ds(term.row_from, term.rows)
+        from_column = term.column_from
+        if term.split:
+            from_column = pl.multiple_of(from_column + part * term.columns, 128)
+        columns = pl.ds(from_column, term.columns)
+        own = jnp.dot(
+            own_left[term.left][owner, rows, :],
+            own_right[term.right][:, columns],
+            preferred_element_type=jnp.float32,
+        )
+        return own + jnp.dot(
+            sib_left[term.left][owner, rows, :],
+            sib_right[term.right][:, columns],
+            preferred_element_type=jnp.float32,
+        )
+
+    def owner_at(term, hop):
+        back = hop + 1 if term.way == 0 else 2 * chips - 1 - hop
+        return ring_chip(lax.rem(place + 2 * chips - back, chips), chips)
+
+    def give_copy(at, hop):
+        return remote(
+            give[at].at[hop],
+            got[at].at[hop],
+            give_send.at[at, hop],
+            got_recv.at[at, hop],
+            twin,
+        )
+
+    def ring_copy(number, hop):
+        return remote(
+            landing[number].at[hop],
+            landing[number].at[hop + 1],
+            ring_send.at[number, hop],
+            ring_recv.at[number, hop + 1],
+            ways[terms[number].way],
+        )
+
+    def arrival(number, hop):
+        return remote(
+            landing[number].at[hop],
+            landing[number].at[hop],
+            ring_send.at[number, hop],
+            ring_recv.at[number, hop],
+            ways[terms[number].way],
+        )
+
+    def final_copy(number):
+        return remote(
+            landing[number].at[chips - 1],
+            final[number],
+            final_send.at[number],
+            final_recv.at[number],
+            twin,
+        )
+
+    def step(clock, carry):
+        for moment in sorted(set(first_use.values())):
+
+            @pl.when(clock == moment)
+            def _():
+                for key, use in first_use.items():
+                    if use == moment:
+                        loads[key].wait()
+                        swaps[key].wait_recv()
+
+        for at, number in enumerate(split_at):
+            term = terms[number]
+            later = clock - term.start + 1
+
+            @pl.when((later >= 0) & (later < chips))
+            def _():
+                give[at][later] = chunk(term, owner_at(term, later), 1 - plane).astype(
+                    jnp.bfloat16
+                )
+                give_copy(at, later).start()
+
+        for number, term in enumerate(terms):
+            hop = clock - term.start
+
+            @pl.when((hop >= 0) & (hop < chips))
+            def _():
+                total = chunk(term, owner_at(term, hop), plane)
+                if term.split:
+                    at = split_at.index(number)
+                    give_copy(at, hop).wait_recv()
+                    total = total + got[at][hop].astype(jnp.float32)
+
+                @pl.when(hop > 0)
+                def _():
+                    arrival(number, hop).wait_recv()
+
+                landing[number][hop] = (
+                    total + landing[number][hop].astype(jnp.float32)
+                ).astype(jnp.bfloat16)
+
+                @pl.when(hop < chips - 1)
+                def _():
+                    ring_copy(number, hop).start()
+
+                @pl.when(hop == chips - 1)
+                def _():
+                    final_copy(number).start()
+
+        return carry
+
+    lax.fori_loop(0, max(term.start for term in terms) + chips, step, 0)
+    for number, term in enumerate(terms):
+        final_copy(number).wait()
+        mine = landing[number][chips - 1].astype(jnp.float32)
+        other = final[number][...].astype(jnp.float32)
+        if term.split:
+            width = term.columns
+            outs[number][:, pl.ds(pl.multiple_of(plane * width, 128), width)] = mine
+            outs[number][:, pl.ds(pl.multiple_of((1 - plane) * width, 128), width)] = other
+        else:
+            outs[number][...] = mine + other
+
+    def settle(hop, carry):
+        for number in range(len(terms)):
+
+            @pl.when(hop < chips - 1)
+            def _():
+                ring_copy(number, hop).wait_send()
+
+        for at in range(len(split_at)):
+            give_copy(at, hop).wait_send()
+        return carry
+
+    lax.fori_loop(0, chips, settle, 0)
+    for key in first_use:
+        swaps[key].wait_send()
+
+
+def reduce_terms(terms, lefts, rights, identity):
+    chips = lefts[0].shape[0]
+    whole = {term.right for term in terms if lefts[term.left].ndim == 4}
+    left_parts = [
+        (left.shape[0],) + left.shape[-2:] for left in lefts
+    ]
+    right_parts = [
+        (right.shape[0], right.shape[1] if number in whole else right.shape[1] // 2)
+        for number, right in enumerate(rights)
+    ]
+
+    def vmem(shape):
+        return pltpu.VMEM(shape, jnp.bfloat16)
+
+    splits = [term for term in terms if term.split]
+    operands = len(lefts) + len(rights)
+    scratch = (
+        [vmem(shape) for shape in left_parts + right_parts] * 2
+        + [vmem((chips, term.rows, term.columns)) for term in terms]
+        + [vmem((term.rows, term.columns)) for term in terms]
+        + [vmem((chips, term.rows, term.columns)) for term in splits] * 2
+        + [pltpu.SemaphoreType.DMA((operands,))] * 3
+        + [pltpu.SemaphoreType.DMA((len(terms), chips))] * 2
+        + [pltpu.SemaphoreType.DMA((len(splits), chips))] * 2
+        + [pltpu.SemaphoreType.DMA((len(terms),))] * 2
+    )
+    return pl.pallas_call(
+        partial(reduce_body, terms, chips, len(lefts), len(rights)),
+        out_shape=[
+            jax.ShapeDtypeStruct((term.rows, term.columns * (1 + term.split)), jnp.float32)
+            for term in terms
+        ],
+        in_specs=[pl.BlockSpec(memory_space=pl.ANY)] * operands,
+        out_specs=[pl.BlockSpec(memory_space=pltpu.VMEM)] * len(terms),
+        scratch_shapes=scratch,
+        compiler_params=pltpu.CompilerParams(
+            collective_id=identity, has_side_effects=True, vmem_limit_bytes=60 * 1024 * 1024
+        ),
+    )(*lefts, *rights)
+
+
+def by_chip(values):
+    chips = lax.axis_size("fsdp") // 2
+    return values.T.reshape(chips, -1, values.shape[0])
+
+
+def by_device(values):
+    chips = lax.axis_size("fsdp") // 2
+    return values.T.reshape(chips, 2, -1, values.shape[0])
+
+
+def padded_halves(values, half):
+    tokens, columns = values.shape
+    halves = values.reshape(tokens, 2, columns // 2)
+    return jnp.pad(halves, ((0, 0), (0, 0), (0, half - columns // 2))).reshape(tokens, 2 * half)
+
+
+def join_cores(pieces):
     core = lax.axis_index("fsdp") % 2
-    half = right.shape[-1] // 2
-    kept = lax.dynamic_slice_in_dim(right, core * half, half, axis=1)
-    sent = lax.dynamic_slice_in_dim(right, (1 - core) * half, half, axis=1)
-    left_both = jnp.concatenate([left, swap_cores(left)], axis=0)
-    right_both = jnp.concatenate([kept, swap_cores(sent)], axis=0)
-    return lax.dot_general(
-        left_both, right_both, (((0,), (0,)), ((), ())), preferred_element_type=jnp.float32
-    ).astype(jnp.bfloat16)
-
-
-def ring_reduce(term):
+    both = jnp.concatenate(pieces, axis=1)
+    rows = both.shape[0] // 2
+    mine = lax.dynamic_slice_in_dim(both, core * rows, rows, axis=0)
+    sent = lax.dynamic_slice_in_dim(both, (1 - core) * rows, rows, axis=0)
+    other = swap_cores(sent)
+    low = jnp.where(core == 0, mine, other)
+    high = jnp.where(core == 0, other, mine)
+    joined, at = [], 0
+    for piece in pieces:
+        end = at + piece.shape[1]
+        joined += [low[:, at:end], high[:, at:end]]
+        at = end
+    return jnp.concatenate(joined, axis=1)
+
+
+def round_up(value, step):
+    return -(-value // step) * step
+
+
+def plain_sum(left, right):
+    total = lax.psum_scatter(
+        outer_rows(left, right).astype(jnp.bfloat16), "fsdp", scatter_dimension=0, tiled=True
+    )
+    return lax.psum(total.astype(jnp.float32), "rep")
+
+
+def kernels_fit(rows):
+    return 2 * rows % 16 == 0 and lax.axis_size("rep") == 2
+
+
+def sum_block_grads(
+    normed, triple_grad, attended, branch_grad, mixed, pre_grad, active, feed_grad, identity
+):
+    rows = MODEL_WIDTH // lax.axis_size("fsdp")
+    if not kernels_fit(rows):
+        wide = jnp.concatenate(
+            [
+                plain_sum(normed, triple_grad),
+                plain_sum(attended, branch_grad),
+                plain_sum(mixed, pre_grad),
+            ],
+            axis=1,
+        )
+        return (wide, plain_sum(active, feed_grad))
+    triple_half = round_up(triple_grad.shape[1] // 2, 256)
+    branch_half = round_up(branch_grad.shape[1] // 2, 128)
+    pre_half = pre_grad.shape[1] // 2
+    plain_part = 8 * 128
+    pre_part = (pre_half - plain_part) // 2
+    deep_rows = active.shape[1] // lax.axis_size("fsdp") // 2
+    terms = (
+        Term(0, 0, 2 * rows, 0, triple_half // 2, 0, True, 0, 1),
+        Term(2, 2, 2 * rows, 0, pre_part, plain_part, True, 1, 1),
+        Term(3, 3, deep_rows, 0, MODEL_WIDTH, 0, False, 0, 1),
+        Term(3, 3, deep_rows, deep_rows, MODEL_WIDTH, 0, False, 1, 1),
+        Term(1, 1, 2 * rows, 0, branch_half, 0, False, 0, 2),
+        Term(2, 2, 2 * rows, 0, plain_part, 0, False, 1, 2),
+    )
+    triple, pre_late, deep_low, deep_high, branch, pre_early = reduce_terms(
+        terms,
+        [by_chip(normed), by_chip(attended), by_chip(mixed), by_device(active)],
+        [
+            padded_halves(triple_grad, triple_half),
+            padded_halves(branch_grad, branch_half),
+            pre_grad,
+            feed_grad,
+        ],
+        identity,
+    )
+    wide = join_cores(
+        [
+            triple[:, : triple_grad.shape[1] // 2],
+            branch[:, : branch_grad.shape[1] // 2],
+            jnp.concatenate([pre_early, pre_late], axis=1),
+        ]
+    )
+    return (wide, jnp.concatenate([deep_low, deep_high], axis=0))
+
+
+def sum_head_grads(tapped, first_grad, first, second_grad, second, projected_grad, identity):
     count = lax.axis_size("fsdp")
-    chips = count // 2
-    device = lax.axis_index("fsdp")
-    chip, core = device // 2, device % 2
-    order = ring_order(chips)
-    order_table = jnp.array(order, jnp.int32)
-    place = jnp.array([order.index(number) for number in range(chips)], jnp.int32)[chip]
-    parts = term.reshape(chips, 2, term.shape[0] // count, term.shape[1])
-    totals = []
-    for way, step in ((0, 1), (1, -1)):
-        route = [
-            (2 * order[spot] + side, 2 * order[(spot + step) % chips] + side)
-            for spot in range(chips)
-            for side in range(2)
-        ]
-
-        def own(hops):
-            return parts[order_table[(place - step * hops) % chips], way]
-
-        total = own(1)
-        for hop in range(1, chips):
-            total = lax.ppermute(total, "fsdp", route)
-            total = (total.astype(jnp.float32) + own(hop + 1).astype(jnp.float32)).astype(
-                jnp.bfloat16
-            )
-        totals.append(total)
-    stacked = jnp.stack(totals)
-    mine = stacked[core]
-    other = swap_cores(stacked[1 - core])
-    both = jnp.concatenate([mine, other, mine], axis=1)
-    return lax.dynamic_slice_in_dim(
-        both, core * term.shape[1], 2 * term.shape[1], axis=1
-    )
-
-
-def sum_copies(values):
-    copies = lax.axis_size("rep")
-    total = values.astype(jnp.float32)
-    if copies == 2:
-        return total + lax.ppermute(values, "rep", [(0, 1), (1, 0)]).astype(jnp.float32)
-    return lax.psum(total, "rep")
+    rows, head_rows = tapped.shape[1] // count, first.shape[1] // count
+    if not kernels_fit(rows):
+        return (
+            plain_sum(tapped, first_grad),
+            jnp.concatenate(
+                [plain_sum(first, second_grad), plain_sum(second, projected_grad)], axis=1
+            ),
+        )
+    half, last = first_grad.shape[1] // 2, projected_grad.shape[1] // 2
+    terms = (
+        Term(1, 1, 2 * head_rows, 0, half // 2, 0, True, 1, 1),
+        Term(0, 0, 2 * rows, 0, half, 0, False, 0, 1),
+        Term(2, 2, 2 * head_rows, 0, last - 128, 128, False, 1, 1),
+        Term(2, 2, 2 * head_rows, 0, 128, 0, False, 0, 1),
+    )
+    second_out, first_out, third_late, third_early = reduce_terms(
+        terms,
+        [by_chip(tapped), by_chip(first), by_chip(second)],
+        [first_grad, second_grad, projected_grad],
+        identity,
+    )
+    return (
+        join_cores([first_out]),
+        join_cores([second_out, jnp.concatenate([third_early, third_late], axis=1)]),
+    )
 
 
 def gathered_terms(row):
@@ -111,18 +466,15 @@
 
 
 def fetch_block(wide_shard, deep_shard):
-    rows = wide_shard.shape[0]
-    count = lax.axis_size("fsdp")
     rest = wide_shard[:, 6 * MODEL_WIDTH :].astype(jnp.bfloat16)
-    groups = rest.shape[1] // MODEL_WIDTH
-    rest = rest.reshape(rows, groups, MODEL_WIDTH).transpose(1, 0, 2)
-    deep = deep_shard.astype(jnp.bfloat16).reshape(-1, rows, MODEL_WIDTH)
-    whole = lax.all_gather(
-        jnp.concatenate([rest, deep], axis=0), "fsdp", axis=1, tiled=True
-    )
-    deep_whole = whole[groups:].reshape(-1, count, rows, MODEL_WIDTH)
-    deep_whole = deep_whole.transpose(1, 0, 2, 3).reshape(-1, MODEL_WIDTH)
-    return (whole[:groups], deep_whole)
+    whole = lax.all_gather(rest, "fsdp", axis=0, tiled=True)
+    deep = lax.all_gather(deep_shard.astype(jnp.bfloat16), "fsdp", axis=0, tiled=True)
+    split = (
+        whole[:, : 3 * MODEL_WIDTH],
+        whole[:, 3 * MODEL_WIDTH : 4 * MODEL_WIDTH],
+        whole[:, 4 * MODEL_WIDTH :],
+    )
+    return (split, deep)
 
 
 def plane_modulation(silu_low, wide_weight, block_bias):
@@ -165,33 +517,36 @@
     return (attended, largest + jnp.log(totals))
 
 
-def attention_backward(inputs):
-    queries, keys_in, values_in, visible, log_total, upstream = inputs
+def attention_scores_backward(queries, keys_in, values_in, visible, log_total, upstream):
     factor = queries.shape[-1] ** (-0.5)
     scores = (
-        jnp.einsum("qhd,khd->hqk", queries, keys_in, preferred_element_type=jnp.float32) * factor
-    )
-    scores = jnp.where(visible[None, None, :], scores, masked_score)
+        jnp.einsum("sqhd,skhd->shqk", queries, keys_in, preferred_element_type=jnp.float32)
+        * factor
+    )
+    scores = jnp.where(visible[:, None, None, :], scores, masked_score)
     chances = jnp.exp(scores - log_total)
     chance_grad = jnp.einsum(
-        "qhd,khd->hqk", upstream, values_in, preferred_element_type=jnp.float32
-    )
-    value_grad = jnp.einsum(
-        "hqk,qhd->khd", chances.astype(jnp.bfloat16), upstream, preferred_element_type=jnp.float32
+        "sqhd,skhd->shqk", upstream, values_in, preferred_element_type=jnp.float32
     )
     centre = jnp.sum(chance_grad * chances, axis=-1, keepdims=True)
     score_grad = (chances * (chance_grad - centre)).astype(jnp.bfloat16)
+    return (chances.astype(jnp.bfloat16), score_grad)
+
+
+def attention_products_backward(queries, keys_in, chances_low, score_grad, upstream):
+    factor = queries.shape[-1] ** (-0.5)
+    value_grad = jnp.einsum(
+        "shqk,sqhd->skhd", chances_low, upstream, preferred_element_type=jnp.float32
+    )
     query_grad = (
-        jnp.einsum("hqk,khd->qhd", score_grad, keys_in, preferred_element_type=jnp.float32) * factor
+        jnp.einsum("shqk,skhd->sqhd", score_grad, keys_in, preferred_element_type=jnp.float32)
+        * factor
     )
     key_grad = (
-        jnp.einsum("hqk,qhd->khd", score_grad, queries, preferred_element_type=jnp.float32) * factor
+        jnp.einsum("shqk,sqhd->skhd", score_grad, queries, preferred_element_type=jnp.float32)
+        * factor
     )
     return (query_grad, key_grad, value_grad)
-
-
-def joined(groups):
-    return groups.transpose(1, 0, 2).reshape(groups.shape[1], -1)
 
 
 def block_forward(hidden, modulation, wide_matrix, deep_matrix, bias, visible):
@@ -257,7 +612,7 @@
     return (result, saved)
 
 
-def block_backward(upstream, saved, wide_matrix, deep_matrix, visible):
+def block_backward(upstream, saved, wide_matrix, deep_matrix, visible, identity):
     (
         hidden,
         modulation,
@@ -303,9 +658,12 @@
     ).astype(jnp.bfloat16)
     pieces = triple.reshape(sequences, SEQ_LEN, 3, HEADS, HEAD_DIM)
     heads_grad = attended_grad.reshape(sequences, SEQ_LEN, HEADS, HEAD_DIM)
-    query_grad, key_grad, value_grad = lax.map(
-        attention_backward,
-        (pieces[:, :, 0], pieces[:, :, 1], pieces[:, :, 2], visible, log_total, heads_grad),
+    queries, keys_in, values_in = pieces[:, :, 0], pieces[:, :, 1], pieces[:, :, 2]
+    chances_low, score_grad = attention_scores_backward(
+        queries, keys_in, values_in, visible, log_total, heads_grad
+    )
+    query_grad, key_grad, value_grad = attention_products_backward(
+        queries, keys_in, chances_low, score_grad, heads_grad
     )
     triple_gradient = jnp.concatenate(
         [
@@ -349,13 +707,18 @@
     def flat(values):
         return values.reshape(-1, values.shape[-1])
 
-    deep_grad = ring_reduce(paired_product(flat(active_low), flat(feedforward_gradient)))
-    pre_grad = ring_reduce(paired_product(flat(mixed_low), flat(preactivation_gradient)))
-    branch_grad = ring_reduce(paired_product(flat(attended_low), flat(branch_gradient)))
-    triple_grad = ring_reduce(paired_product(flat(normed_low), flat(triple_gradient)))
-    rest_grad = sum_copies(jnp.concatenate([triple_grad, branch_grad, pre_grad], axis=1))
-    deep_grad = sum_copies(deep_grad)
-    return (hidden_grad, modulation_grad, bias_row, rest_grad, deep_grad)
+    weight_grads = sum_block_grads(
+        flat(normed_low),
+        flat(triple_gradient),
+        flat(attended_low),
+        flat(branch_gradient),
+        flat(mixed_low),
+        flat(preactivation_gradient),
+        flat(active_low),
+        flat(feedforward_gradient),
+        identity,
+    )
+    return (hidden_grad, modulation_grad, bias_row, weight_grads)
 
 
 def adam_update(weight, grad, first, second, rate, decay):
@@ -398,15 +761,33 @@
     visible = jnp.arange(SEQ_LEN, dtype=jnp.int32)[None, :] < lengths[:, None]
     wide_early, deep_early = fetch_block(wide_weight[0], deep_weight[0])
     modulation_early, modulation_late = plane_modulation(silu_low, wide_weight, block_bias)
-    wide_early = [joined(wide_early[:3]), wide_early[3], joined(wide_early[4:])]
     tapped, saved_early = block_forward(
         hidden, modulation_early, wide_early, deep_early, block_bias[0], visible
     )
+    wide_late, deep_late = fetch_block(wide_weight[1], deep_weight[1])
     first_matrix, second_w = (
         lax.all_gather(head_first.astype(jnp.bfloat16), "fsdp", axis=0, tiled=True),
         lax.all_gather(head_second.astype(jnp.bfloat16), "fsdp", axis=0, tiled=True),
     )
-    tapped_low = tapped.astype(jnp.bfloat16)
+    final, saved_late = block_forward(
+        tapped, modulation_late, wide_late, deep_late, block_bias[1], visible
+    )
+    raw_targets = targets.astype(jnp.float32).reshape(sequences, SEQ_LEN, PZ)
+    target_unit = raw_targets * lax.rsqrt(
+        jnp.sum(raw_targets * raw_targets, axis=-1, keepdims=True) + norm_epsilon
+    )
+
+    def alignment(values):
+        unit = values * lax.rsqrt(jnp.sum(values * values, axis=-1, keepdims=True) + norm_epsilon)
+        return jnp.sum(unit * target_unit, axis=-1)
+
+    upstream = cotangent.astype(jnp.float32).reshape(sequences, SEQ_LEN, MODEL_WIDTH)
+    late_input_grad, late_modulation_grad, late_row, late_grads = block_backward(
+        upstream, saved_late, wide_late, deep_late, visible, 0
+    )
+    tapped_low, late_input_grad = lax.optimization_barrier(
+        (tapped.astype(jnp.bfloat16), late_input_grad)
+    )
     first_pre = (
         jnp.dot(tapped_low, first_matrix, preferred_element_type=jnp.float32) + head_bias[:PH]
     )
@@ -419,24 +800,6 @@
     projected = (
         jnp.dot(second_low, second_w[:, PH:], preferred_element_type=jnp.float32)
         + head_bias[2 * PH :]
-    )
-    wide_late, deep_late = fetch_block(wide_weight[1], deep_weight[1])
-    wide_late = [joined(wide_late[:3]), wide_late[3], joined(wide_late[4:])]
-    final, saved_late = block_forward(
-        tapped, modulation_late, wide_late, deep_late, block_bias[1], visible
-    )
-    raw_targets = targets.astype(jnp.float32).reshape(sequences, SEQ_LEN, PZ)
-    target_unit = raw_targets * lax.rsqrt(
-        jnp.sum(raw_targets * raw_targets, axis=-1, keepdims=True) + norm_epsilon
-    )
-
-    def alignment(values):
-        unit = values * lax.rsqrt(jnp.sum(values * values, axis=-1, keepdims=True) + norm_epsilon)
-        return jnp.sum(unit * target_unit, axis=-1)
-
-    upstream = cotangent.astype(jnp.float32).reshape(sequences, SEQ_LEN, MODEL_WIDTH)
-    late_input_grad, late_modulation_grad, late_row, late_rest_grad, late_deep_grad = (
-        block_backward(upstream, saved_late, wide_late, deep_late, visible)
     )
     projected_grad = jax.vjp(alignment, projected)[1](-repa_weight * visible.astype(jnp.float32))[
         0
@@ -460,34 +823,37 @@
         ]
     )
 
+
     def flat(values):
         return values.reshape(-1, values.shape[-1])
 
-    first_weight_grad = sum_copies(
-        ring_reduce(paired_product(flat(tapped_low), flat(first_gradient)))
-    )
-    second_weight_grad = sum_copies(
-        jnp.concatenate(
-            [
-                ring_reduce(paired_product(flat(first_low), flat(second_grad))),
-                ring_reduce(paired_product(flat(second_low), flat(projected_grad))),
-            ],
-            axis=1,
-        )
-    )
-    input_grad, early_modulation_grad, early_row, early_rest_grad, early_deep_grad = (
-        block_backward(
-            late_input_grad + tapped_gradient, saved_early, wide_early, deep_early, visible
-        )
-    )
-    all_silu = gathered_terms(silu_low)
+    first_weight_grad, second_weight_grad = sum_head_grads(
+        flat(tapped_low),
+        flat(first_gradient),
+        flat(first_low),
+        flat(second_grad),
+        flat(second_low),
+        flat(projected_grad),
+        1,
+    )
+    input_grad, early_modulation_grad, early_row, early_grads = block_backward(
+        late_input_grad + tapped_gradient,
+        saved_early,
+        wide_early,
+        deep_early,
+        visible,
+        2,
+    )
+    late_rows = gathered_terms(
+        jnp.concatenate([silu_low.astype(jnp.float32)[0], late_row, head_row])[None]
+    )
     own_silu = lax.dynamic_slice_in_dim(
-        all_silu,
+        late_rows,
         lax.axis_index("fsdp") * wide_weight.shape[1],
         wide_weight.shape[1],
         axis=1,
-    )
-    late_rows = gathered_terms(jnp.concatenate([late_row, head_row])[None])
+    ).astype(jnp.bfloat16)
+    late_rows = late_rows[:, MODEL_WIDTH:]
     early_rows = gathered_terms(early_row[None])
 
     def modulation_weight_grad(rows):
@@ -501,11 +867,17 @@
     bias_width = block_bias.shape[1]
     wide_grad = jnp.stack(
         [
-            jnp.concatenate([modulation_weight_grad(early_rows), early_rest_grad], axis=1),
-            jnp.concatenate([modulation_weight_grad(late_rows), late_rest_grad], axis=1),
+            jnp.concatenate(
+                [modulation_weight_grad(early_rows), early_grads[0]],
+                axis=1,
+            ),
+            jnp.concatenate(
+                [modulation_weight_grad(late_rows), late_grads[0]],
+                axis=1,
+            ),
         ]
     )
-    deep_grad = jnp.stack([early_deep_grad, late_deep_grad])
+    deep_grad = jnp.stack([early_grads[1], late_grads[1]])
     late_sum = jnp.sum(late_rows, axis=0)
     block_bias_grad = jnp.stack([jnp.sum(early_rows, axis=0), late_sum[:bias_width]])
     head_bias_total = late_sum[bias_width:]

time: 1480 us -> 1360 us (0.919)
  Pallas kernels: 0 us -> 418 us
  starting transfers between devices: 192 us -> 12 us
  local copies, waits for them, and re-layouts: 273 us -> 178 us
  blocking collectives: 71.1 us -> 0 us
  other arithmetic: 189 us -> 120 us
  matrix products: 356 us -> 289 us
  between operations: 59.7 us -> 16.8 us
    pallas_call x0 -> x3, Pallas kernels: none -> 418 us  [reduce_terms(): pl.pallas_call(partial(reduce_body, terms, chips, len(lefts), len(rights)...]
    ppermute x160 -> x0, waiting for transfers between devices: 256 us -> none  [the longest x154 248 us: ring_reduce(): total = lax.ppermute(total, 'fsdp', route)]
    ppermute x160 -> x0, starting transfers between devices: 176 us -> none  [the longest x154 168 us: ring_reduce(): total = lax.ppermute(total, 'fsdp', route)]
    all_gather x2 -> x4, waiting for transfers between devices: 67.8 us -> 224 us  [the longest x2 156 us: fetch_block(): whole = lax.all_gather(rest, 'fsdp', axis=0, tiled=True)]
    dot_general x19 -> x8, matrix products: 126 us -> 51.9 us  [the longest x2 26.7 us: attention_scores_backward(): jnp.einsum('sqhd,skhd->shqk', upstream, values_in, preferred_element_type...]
    all_gather x1 -> x0, blocking collectives: 71.1 us -> none  [gathered_terms(): return lax.all_gather(row, ('fsdp', 'rep'), axis=0, tiled=True)]
    unnamed x401 -> x307, local copies, waits for them, and re-layouts: 93.9 us -> 47 us
    convert_element_type x73 -> x5, other arithmetic: 65.3 us -> 19.4 us  [the longest x2 15 us: attention_scores_backward(): score_grad = (chances * (chance_grad - centre)).astype(jnp.bfloat16)]
  transfers between devices with their start and end apart: 201 -> 14, of which waited for: 97 -> 8; matrix products, arithmetic and copies ran while one was open for 47% -> 28% of each run, Pallas kernels for 0% -> 31%
where the time goes in v2:
time: 1360 us; the launch traced here: 1350 us
  Pallas kernels  418 us (31%)
  waiting for transfers between devices  321 us (24%)
  matrix products  289 us (21%)
  local copies, waits for them, and re-layouts  178 us (13%)
  other arithmetic  120 us (9%)
  between operations  16.8 us (1%)
    pallas_call x3, Pallas kernels, reduce_terms(): pl.pallas_call(partial(reduce_body, terms, chips, len(lefts), len(rights)...  418 us
    all_gather x2, waiting for transfers between devices, fetch_block(): whole = lax.all_gather(rest, 'fsdp', axis=0, tiled=True)  156 us
    all_gather x2, waiting for transfers between devices, fetch_block(): lax.all_gather(deep_shard.astype(jnp.bfloat16), 'fsdp', axis=0, tiled=True)  68 us
    unnamed x307, local copies, waits for them, and re-layouts  47 us
    sub x6, other arithmetic, adam_update(): weight - rate * (first_hat / (jnp.sqrt(second_hat) + adam_epsilon) + deca...  40.5 us
    all_gather x1, waiting for transfers between devices, per_device(): lax.all_gather(head_second.astype(jnp.bfloat16), 'fsdp', axis=0, tiled=True)  40.2 us
    all_to_all x1, waiting for transfers between devices, plane_modulation(): back = lax.all_to_all(partial, 'fsdp', 0, 0, tiled=True)  29.5 us
    dot_general x2, matrix products, block_backward(): jnp.einsum('xjn,mn->xjm', feedforward_gradient, deep_matrix, preferred_el...  28.2 us
  transfers between devices with their start and end apart: 14, of which 8 were waited for; matrix products, arithmetic and copies ran while one was open for 28% of the time, Pallas kernels for 31%

profile of v2, /device:TPU:0, one launch (start us, length us, event | category | flops | bytes accessed | tf_op | source)
XLA Modules:
  0.0 1354.8 jit_solution(15714550915942218623)
XLA Ops:
  50.6 29.5 %all-to-all-done.1 = f32[16,1,2,6912]{3,2,1,0:T(2,128)S(1)} async-done(((f32[16,1,2,6912]{3,2,1,0:T(2,128)}), f32[16,1,2,6912]{3,2,1,0:T(2,128)S(1)}, u32[]{:S(2)}, u32[]{:S(2)}) %all-to-all-start.1) | async-done | bytes 884768 | tf_op jit(solution)/shard_map/all_to_all | solution.py:500
  83.6 59.1 %all-gather.15.cloned.1.call-done = bf16[1152,9216]{1,0:T(8,128)(2,1)} async-done(((bf16[72,9216]{1,0:T(8,128)(2,1)}), bf16[1152,9216]{1,0:T(8,128)(2,1)}) %all-gather.15.cloned.1.call-update) | async-done | bytes 21233680 | tf_op jit(solution)/shard_map/all_gather | solution.py:470
  186.8 13.9 %fusion.42 = (bf16[4608,448]{0,1:T(8,128)(2,1)}, f32[448,4608]{1,0:T(8,128)}) fusion(f32[4608]{0:T(1024)S(1)} %copy-done.96, bf16[1152,9216]{1,0:T(8,128)(2,1)} %all-gather.15.cloned.1.call-done, f32[448,1152]{1,0:T(8,128)S(1)} %get-tuple-element.194, f32[1152]{0:T(1024)S(1)} %copy-done.82, f32[1152]{0:T(1024)S(1)} %copy-done.84, f32[448]{0:T(512)S(1)} %fusion.196, ...), kind=kOutput, calls=%fused_computation.64 | convolution fusion | flops 4779565056 | bytes 25098752 | tf_op jit(solution)/shard_map/dot_general | solution.py:589
  200.7 37.4 %all-gather.23.cloned.1.call-done = bf16[1,4608,1152]{2,1,0:T(8,128)(2,1)} async-done(((bf16[1,288,1152]{2,1,0:T(8,128)(2,1)}), bf16[1,4608,1152]{2,1,0:T(8,128)(2,1)}) %all-gather.23.cloned.1.call-update) | async-done | bytes 10616848 | tf_op jit(solution)/shard_map/all_gather | solution.py:471
  238.1 11.6 fusion.117
  251.9 96.6 %all-gather.17.cloned.1.call-done = bf16[1152,9216]{1,0:T(8,128)(2,1)} async-done(((bf16[72,9216]{1,0:T(8,128)(2,1)}), bf16[1152,9216]{1,0:T(8,128)(2,1)}) %all-gather.17.cloned.1.call-update) | async-done | bytes 21233680 | tf_op jit(solution)/shard_map/all_gather | solution.py:470
  363.9 10.1 fusion.235
  396.5 12.9 fusion.50
  409.4 30.6 %all-gather.25.cloned.1.call-done = bf16[1,4608,1152]{2,1,0:T(8,128)(2,1)} async-done(((bf16[1,288,1152]{2,1,0:T(8,128)(2,1)}), bf16[1,4608,1152]{2,1,0:T(8,128)(2,1)}) %all-gather.25.cloned.1.call-update) | async-done | bytes 10616848 | tf_op jit(solution)/shard_map/all_gather | solution.py:471
  440.0 13.9 %convert_reduce_fusion.1 = (f32[4608]{0:T(1024)}, bf16[448,4608]{1,0:T(8,128)(2,1)S(1)}) fusion(f32[448,4608]{1,0:T(8,128)} %get-tuple-element.247, bf16[448,1152]{1,0:T(8,128)(2,1)S(1)} %copy-done.30, bf16[1,4608,1152]{2,1,0:T(8,128)(2,1)} %all-gather.25.cloned.1.call-done), kind=kOutput, calls=%fused_computation.74 | convolution fusion | flops 4801752576 | bytes 24053760 | tf_op jit(solution)/shard_map/xjn,mn->xjm/dot_general | solution.py:636
  453.8 11.9 multiply_reduce_fusion.3
  477.9 15.1 %multiply_reduce_fusion.1 = (f32[16,448]{1,0:T(8,128)}, f32[16,448,448]{1,2,0:T(8,128)}) fusion(f32[16,448,448]{1,2,0:T(8,128)} %get-tuple-element.228, f32[16,448]{1,0:T(8,128)S(1)} %log_add_fusion.1, bf16[448,16,72]{0,2,1:T(8,128)(2,1)} %bitcast.321, bf16[1,448,3,16,72]{1,4,3,2,0:T(8,128)(2,1)} %bitcast.306), kind=kOutput, calls=%fused_computation.4 | convolution fusion | flops 472048640 | bytes 29941760 | tf_op jit(solution)/shard_map/sqhd,skhd->shqk/dot_general | solution.py:528
  513.4 10.3 multiply_reduce_fusion.5
  527.0 14.2 %fusion.147 = (bf16[1152]{0:T(1024)(128)(2,1)}, bf16[1152]{0:T(1024)(128)(2,1)}, f32[1,448,1152]{2,1,0:T(8,128)}, bf16[448,1152]{1,0:T(8,128)(2,1)}) fusion(bf16[448,1152]{1,0:T(8,128)(2,1)S(1)} %copy-done.35, f32[448,1152]{1,0:T(8,128)S(1)} %copy-done.128, f32[448,1152]{1,0:T(8,128)S(1)} %copy-done.15, f32[448]{0:T(512)S(1)} %copy-done.110, ...), kind=kOutput, calls=%fused_computation.205 | convolution fusion | flops 4781627392 | bytes 31278080 | tf_op jit(solution)/shard_map/dot_general | solution.py:594
  548.9 40.2 %all-gather.21.cloned.1.call-done = bf16[2048,2816]{1,0:T(8,128)(2,1)} async-done(((bf16[128,2816]{1,0:T(8,128)(2,1)}), bf16[2048,2816]{1,0:T(8,128)(2,1)}) %all-gather.21.cloned.1.call-update) | async-done | bytes 11534352 | tf_op jit(solution)/shard_map/all_gather | solution.py:770
  589.2 10.3 fusion.106
  621.7 14.3 %convert_reduce_fusion = (f32[4608]{0:T(1024)}, bf16[448,4608]{1,0:T(8,128)(2,1)S(1)}) fusion(f32[448,4608]{1,0:T(8,128)} %get-tuple-element.251, bf16[448,1152]{1,0:T(8,128)(2,1)S(1)} %get-tuple-element.207.refs_7_, bf16[1,4608,1152]{2,1,0:T(8,128)(2,1)} %all-gather.23.cloned.1.call-done), kind=kOutput, calls=%fused_computation.73 | convolution fusion | flops 4801752576 | bytes 24053760 | tf_op jit(solution)/shard_map/xjn,mn->xjm/dot_general | solution.py:636
  636.1 11.9 multiply_reduce_fusion.2
  665.0 11.6 multiply_reduce_fusion
  772.9 162.9 %shard_map.423 = (f32[144,1792]{1,0:T(8,128)}, f32[144,1280]{1,0:T(8,128)}, f32[144,1152]{1,0:T(8,128)}, f32[144,1152]{1,0:T(8,128)}, f32[144,640]{1,0:T(8,128)}, /*index=5*/f32[144,1024]{1,0:T(8,128)}) custom-call(bf16[8,144,448]{2,1,0:T(8,128)(2,1)} %bitcast.340, bf16[8,144,448]{2,1,0:T(8,128)(2,1)} %bitcast.353, bf16[8,144,448]{2,1,0:T(8,128)(2,1)} %bitcast.342, ...), custom_call_target="tpu_custom_call" | custom-call | tf_op jit(solution)/shard_map/pallas_call | solution.py:323
  968.8 162.7 %shard_map.422 = (f32[144,1792]{1,0:T(8,128)}, f32[144,1280]{1,0:T(8,128)}, f32[144,1152]{1,0:T(8,128)}, f32[144,1152]{1,0:T(8,128)}, f32[144,640]{1,0:T(8,128)}, /*index=5*/f32[144,1024]{1,0:T(8,128)}) custom-call(bf16[8,144,448]{2,1,0:T(8,128)(2,1)} %bitcast.339, bf16[8,144,448]{2,1,0:T(8,128)(2,1)} %bitcast.351, bf16[8,144,448]{2,1,0:T(8,128)(2,1)} %bitcast.341, ...), custom_call_target="tpu_custom_call" | custom-call | tf_op jit(solution)/shard_map/pallas_call | solution.py:323
  1145.3 92.2 %shard_map.424 = (f32[256,1024]{1,0:T(8,128)}, f32[144,1024]{1,0:T(8,128)}, f32[256,256]{1,0:T(8,128)}, f32[256,128]{1,0:T(8,128)}) custom-call(bf16[8,144,448]{2,1,0:T(8,128)(2,1)} %bitcast.343, bf16[8,256,448]{2,1,0:T(8,128)(2,1)} %bitcast.329, bf16[8,256,448]{2,1,0:T(8,128)(2,1)} %bitcast.330, bf16[448,2048]{1,0:T(8,128)(2,1)} %copy-done.47, ...), custom_call_target="tpu_custom_call" | custom-call | tf_op jit(solution)/shard_map/pallas_call | solution.py:323
  1277.8 23.1 %all-gather.27.cloned.1.call-done = f32[32,1,22144]{2,1,0:T(1,128)} async-done(((f32[1,1,22144]{2,1,0:T(1,128)}), f32[32,1,22144]{2,1,0:T(1,128)}) %all-gather.27.cloned.1.call-update) | async-done | bytes 2834448 | tf_op jit(solution)/shard_map/all_gather | solution.py:465
  1319.1 27.4 %multiply_subtract_fusion = (f32[2,72,16128]{2,1,0:T(8,128)}, f32[2,72,16128]{2,1,0:T(8,128)}, f32[2,72,16128]{2,1,0:T(8,128)}, f32[2,72,16128]{2,1,0:T(8,128)}) fusion(f32[2,72,16128]{2,1,0:T(8,128)} %param.28, f32[2,72,16128]{2,1,0:T(8,128)} %param.40, f32[2,72,16128]{2,1,0:T(8,128)} %param.34, f32[1,72,16128]{2,1,0:T(8,128)} %bitcast.313, ...), kind=kLoop, calls=%fused_computation.41 | loop fusion | flops 37158912 | bytes 74317824 | tf_op jit(solution)/shard_map/sub | solution.py:729
  (508 shorter events, 414.3 us)
Async XLA Ops:
  7.2 135.5 %all-gather.15.cloned.1.call-start = ((), (), s32[]{:S(2)}) async-start(), calls=%async_computation.2 | async-start | bytes 22560768 | tf_op jit(solution)/shard_map/all_gather | solution.py:470
  15.4 222.7 %all-gather.23.cloned.1.call-start = ((), (), s32[]{:S(2)}) async-start(), calls=%async_computation.6 | async-start | bytes 11280384 | tf_op jit(solution)/shard_map/all_gather | solution.py:471
  17.8 330.8 %all-gather.17.cloned.1.call-start = ((), (), s32[]{:S(2)}) async-start(), calls=%async_computation.3 | async-start | bytes 22560768 | tf_op jit(solution)/shard_map/all_gather | solution.py:470
  20.5 419.5 %all-gather.25.cloned.1.call-start = ((), (), s32[]{:S(2)}) async-start(), calls=%async_computation.7 | async-start | bytes 11280384 | tf_op jit(solution)/shard_map/all_gather | solution.py:471
  21.1 520.2 %all-gather.19.cloned.1.call-start = ((), (), s32[]{:S(2)}) async-start(), calls=%async_computation.4 | async-start | bytes 5013504 | tf_op jit(solution)/shard_map/all_gather | solution.py:769
  23.3 13.8 %all-to-all-start = ((bf16[16,1,72]{2,1,0:T(2,128)(2,1)}), bf16[16,1,72]{2,1,0:T(2,128)(2,1)S(1)}, u32[]{:S(2)}, u32[]{:S(2)}) async-start(bf16[16,1,72]{2,1,0:T(2,128)(2,1)} %squeeze_transpose_reshape.4), calls=%async_computation | async-start | bytes 16384 | tf_op jit(solution)/shard_map/all_to_all | solution.py:489
  30.6 558.5 %all-gather.21.cloned.1.call-start = ((), (), s32[]{:S(2)}) async-start(), calls=%async_computation.5 | async-start | bytes 12255232 | tf_op jit(solution)/shard_map/all_gather | solution.py:770
  41.7 38.3 %all-to-all-start.1 = ((f32[16,1,2,6912]{3,2,1,0:T(2,128)}), f32[16,1,2,6912]{3,2,1,0:T(2,128)S(1)}, u32[]{:S(2)}, u32[]{:S(2)}) async-start(f32[16,1,2,6912]{3,2,1,0:T(2,128)} %copy.128), calls=%async_computation.1 | async-start | bytes 1769472 | tf_op jit(solution)/shard_map/all_to_all | solution.py:500
  45.5 1227.6 %all-gather.29.cloned.1.call-start = ((), (), s32[]{:S(2)}) async-start(), calls=%async_computation.9 | async-start | bytes 2128896 | tf_op jit(solution)/shard_map/all_gather | solution.py:465
  48.9 93.8 %copy-start.90 = (f32[448]{0:T(512)}, f32[448]{0:T(512)S(1)}, u32[]{:S(2)}) copy-start(f32[448]{0:T(512)S(1)} %broadcast_multiply_fusion.3) | copy-start | bytes 5380
  49.4 93.3 %copy-start.105 = (f32[448]{0:T(512)}, f32[448]{0:T(512)S(1)}, u32[]{:S(2)}) copy-start(f32[448]{0:T(512)S(1)} %fusion.195) | copy-start | bytes 5380
  81.1 61.6 %copy-start.70 = (f32[1152]{0:T(1024)}, f32[1152]{0:T(1024)S(1)}, u32[]{:S(2)}) copy-start(f32[1152]{0:T(1024)S(1)} %get-tuple-element.146) | copy-start | bytes 13828
  81.1 61.6 %copy-start.74 = (f32[1152]{0:T(1024)}, f32[1152]{0:T(1024)S(1)}, u32[]{:S(2)}) copy-start(f32[1152]{0:T(1024)S(1)} %get-tuple-element.145) | copy-start | bytes 13828
  81.1 168.6 %copy-start.72 = (f32[1152]{0:T(1024)}, f32[1152]{0:T(1024)S(1)}, u32[]{:S(2)}) copy-start(f32[1152]{0:T(1024)S(1)} %get-tuple-element.142) | copy-start | bytes 13828
  251.3 97.2 %copy-start.86 = (f32[1152]{0:T(1024)S(1)}, f32[1152]{0:T(1024)}, u32[]{:S(2)}) copy-start(f32[1152]{0:T(1024)} %get-tuple-element.139) | copy-start | bytes 13828
  251.3 97.2 %copy-start.87 = (f32[1152]{0:T(1024)S(1)}, f32[1152]{0:T(1024)}, u32[]{:S(2)}) copy-start(f32[1152]{0:T(1024)} %get-tuple-element.140) | copy-start | bytes 13828
  251.3 97.2 %copy-start.108 = (f32[3456]{0:T(1024)S(1)}, f32[3456]{0:T(1024)}, u32[]{:S(2)}) copy-start(f32[3456]{0:T(1024)} %get-tuple-element.220) | copy-start | bytes 41476
  251.9 106.0 %copy-start.103 = (f32[448]{0:T(512)}, f32[448]{0:T(512)S(1)}, u32[]{:S(2)}) copy-start(f32[448]{0:T(512)S(1)} %multiply_reduce_fusion.10) | copy-start | bytes 5380
  251.9 105.9 %copy-start.113 = (f32[448]{0:T(512)}, f32[448]{0:T(512)S(1)}, u32[]{:S(2)}) copy-start(f32[448]{0:T(512)S(1)} %fusion.197) | copy-start | bytes 5380
  723.5 577.3 %all-gather.27.cloned.1.call-start = ((), (), s32[]{:S(2)}) async-start(), calls=%async_computation.8 | async-start | bytes 2923008 | tf_op jit(solution)/shard_map/all_gather | solution.py:465
  942.5 318.8 %collective-permute-start.1 = (f32[72,4608]{1,0:T(8,128)}, f32[72,4608]{1,0:T(8,128)}, u32[]{:S(2)}, u32[]{:S(2)}) collective-permute-start(f32[72,4608]{1,0:T(8,128)} %constant_dynamic-slice_fusion.2), channel_id=1, source_target_pairs={{0,2},{2,0},{4,6},{6,4},{8,10},{10,8},{12,14},{14,12},{16,18},{18,... | collective-permute-start | bytes 3981320 | tf_op jit(solution)/shard_map/ppermute | solution.py:61
  1135.4 131.1 %collective-permute-start = (f32[72,4608]{1,0:T(8,128)}, f32[72,4608]{1,0:T(8,128)}, u32[]{:S(2)}, u32[]{:S(2)}) collective-permute-start(f32[72,4608]{1,0:T(8,128)} %constant_dynamic-slice_fusion.3), channel_id=1, source_target_pairs={{0,2},{2,0},{4,6},{6,4},{8,10},{10,8},{12,14},{14,12},{16,18},{18,... | collective-permute-start | bytes 3981320 | tf_op jit(solution)/shard_map/ppermute | solution.py:61
  1239.3 14.1 %collective-permute-start.2 = (f32[72,1024]{1,0:T(8,128)}, f32[72,1024]{1,0:T(8,128)}, u32[]{:S(2)}, u32[]{:S(2)}) collective-permute-start(f32[72,1024]{1,0:T(8,128)} %constant_dynamic-slice_fusion.1), channel_id=1, source_target_pairs={{0,2},{2,0},{4,6},{6,4},{8,10},{10,8},{12,14},{14,12},{16,18},{18,... | collective-permute-start | bytes 884744 | tf_op jit(solution)/shard_map/ppermute | solution.py:61
  1242.7 13.4 collective-permute-start.3
  (129 other events, 1194.6 us)
Sparse Core Ops, SparseCore 0:
  15.5 127.1 all-gather.14
  145.5 92.4 all-gather.22
  240.3 108.2 all-gather.16
  351.3 88.6 all-gather.24
  442.7 51.4 all-gather.18
  496.3 92.8 all-gather.20
  723.6 56.4 all-gather.28
  1243.4 57.4 all-gather.26

commit v3 on v2

--- a/solution.py
+++ b/solution.py
@@ -143,8 +143,9 @@
         if width == ref.shape[1]:
             mine = other = ref
         else:
-            mine = ref.at[:, pl.ds(pl.multiple_of(core * width, 128), width)]
-            other = ref.at[:, pl.ds(pl.multiple_of((1 - core) * width, 128), width)]
+            second = ref.shape[1] - width
+            mine = ref.at[:, pl.ds(pl.multiple_of(core * second, 128), width)]
+            other = ref.at[:, pl.ds(pl.multiple_of((1 - core) * second, 128), width)]
         loads["r", number] = pltpu.make_async_copy(mine, own_right[number], load_sem.at[at])
         swaps["r", number] = remote(
             other, sib_right[number], swap_send.at[at], swap_recv.at[at], sibling
@@ -294,6 +295,10 @@
         swaps[key].wait_send()
 
 
+def core_columns(columns):
+    return -(-columns // 256) * 128
+
+
 def reduce_terms(terms, lefts, rights, identity):
     chips = lefts[0].shape[0]
     whole = {term.right for term in terms if lefts[term.left].ndim == 4}
@@ -301,7 +306,7 @@
         (left.shape[0],) + left.shape[-2:] for left in lefts
     ]
     right_parts = [
-        (right.shape[0], right.shape[1] if number in whole else right.shape[1] // 2)
+        (right.shape[0], right.shape[1] if number in whole else core_columns(right.shape[1]))
         for number, right in enumerate(rights)
     ]
 
@@ -335,6 +340,202 @@
     )(*lefts, *rights)
 
 
+class Piece(NamedTuple):
+    source: int
+    rows: int
+    columns: int
+    row_core: int
+    row_plane: int
+    column_from: int
+    column_core: int
+    column_plane: int
+    split: bool
+    long_way: int
+
+
+def gather_body(pieces, chips, count, *refs):
+    sources, outs = refs[:count], refs[count : 2 * count]
+    ring_send, ring_recv, pass_send, pass_recv, twin_send, twin_recv, own_sem = refs[2 * count :]
+    device = lax.axis_index("fsdp")
+    plane = lax.axis_index("rep")
+    core, chip = lax.rem(device, 2), lax.div(device, 2)
+    place = ring_place(chip, chips)
+    sibling = {"fsdp": device + 1 - 2 * core}
+    twin = {"rep": 1 - plane}
+
+    def chip_back(way, hops):
+        back = hops if way == 0 else chips - hops
+        return ring_chip(lax.rem(place + chips - back, chips), chips)
+
+    ways = [{"fsdp": 2 * chip_back(1 - way, 1) + core} for way in range(2)]
+
+    barrier = pltpu.get_barrier_semaphore()
+    partners = (ways[0], ways[1], sibling, twin)
+    for partner in partners:
+        pl.semaphore_signal(barrier, inc=1, device_id=partner, device_id_type=MESH)
+    pl.semaphore_wait(barrier, len(partners))
+
+    keep = [
+        pltpu.make_async_copy(
+            sources[number],
+            outs[number].at[
+                pl.ds(
+                    pl.multiple_of(chip * sources[number].shape[0], 16), sources[number].shape[0]
+                ),
+                :,
+            ],
+            own_sem.at[number],
+        )
+        for number in range(count)
+    ]
+    for copy in keep:
+        copy.start()
+
+    def window(piece, ref, base, of_core, of_plane):
+        row = base + of_core * piece.row_core + of_plane * piece.row_plane
+        column = (
+            piece.column_from + of_core * piece.column_core + of_plane * piece.column_plane
+        )
+        return ref.at[
+            pl.ds(pl.multiple_of(row, 16), piece.rows),
+            pl.ds(pl.multiple_of(column, 128), piece.columns),
+        ]
+
+    def landed(number, owner, of_core, of_plane):
+        piece = pieces[number]
+        height = sources[piece.source].shape[0]
+        return window(piece, outs[piece.source], owner * height, of_core, of_plane)
+
+    def remote(source, target, sems, index, partner):
+        return pltpu.make_async_remote_copy(
+            src_ref=source,
+            dst_ref=target,
+            send_sem=sems[0].at[index],
+            recv_sem=sems[1].at[index],
+            device_id=partner,
+            device_id_type=MESH,
+        )
+
+    hops = [
+        [chips // 2 if piece.long_way == way else (chips - 1) // 2 for way in range(2)]
+        for piece in pieces
+    ]
+    splits = [number for number, piece in enumerate(pieces) if piece.split]
+    sent = []
+
+    def send(copy):
+        copy.start()
+        sent.append(copy)
+
+    for number, piece in enumerate(pieces):
+        for way in range(2):
+            send(
+                remote(
+                    window(piece, sources[piece.source], 0, core, plane),
+                    landed(number, chip, core, plane),
+                    (ring_send, ring_recv),
+                    (number, way, 0),
+                    ways[way],
+                )
+            )
+
+    def ring_arrivals(hop):
+        for number, piece in enumerate(pieces):
+            for way in range(2):
+                if hop > hops[number][way]:
+                    continue
+                block = landed(number, chip_back(way, hop), core, plane)
+                remote(
+                    block, block, (ring_send, ring_recv), (number, way, hop - 1), ways[way]
+                ).wait_recv()
+                if hop < hops[number][way]:
+                    send(
+                        remote(
+                            block, block, (ring_send, ring_recv), (number, way, hop), ways[way]
+                        )
+                    )
+                send(
+                    remote(
+                        block, block, (pass_send, pass_recv), (number, way, hop - 1), sibling
+                    )
+                )
+                if piece.split:
+                    at = splits.index(number)
+                    send(
+                        remote(block, block, (twin_send, twin_recv), (at, way, hop - 1), twin)
+                    )
+
+    def twin_arrivals(hop):
+        for at, number in enumerate(splits):
+            for way in range(2):
+                if hop > hops[number][way]:
+                    continue
+                block = landed(number, chip_back(way, hop), core, 1 - plane)
+                remote(
+                    block, block, (twin_send, twin_recv), (at, way, hop - 1), twin
+                ).wait_recv()
+                send(
+                    remote(
+                        block,
+                        block,
+                        (pass_send, pass_recv),
+                        (len(pieces) + at, way, hop - 1),
+                        sibling,
+                    )
+                )
+
+    for hop in range(1, chips // 2 + 1):
+        ring_arrivals(hop)
+        if hop > 1:
+            twin_arrivals(hop - 1)
+    twin_arrivals(chips // 2)
+    for number in range(len(pieces) + len(splits)):
+        at = number if number < len(pieces) else splits[number - len(pieces)]
+        of_plane = plane if number < len(pieces) else 1 - plane
+        for way in range(2):
+            for hop in range(1, hops[at][way] + 1):
+                block = landed(at, chip_back(way, hop), 1 - core, of_plane)
+                remote(
+                    block, block, (pass_send, pass_recv), (number, way, hop - 1), sibling
+                ).wait_recv()
+    for copy in sent:
+        copy.wait_send()
+    for copy in keep:
+        copy.wait()
+
+
+def gather_pieces(pieces, sources, identity):
+    chips = lax.axis_size("fsdp") // 2
+    splits = sum(piece.split for piece in pieces)
+    hops = chips // 2
+
+    def sems(number):
+        return [pltpu.SemaphoreType.DMA((number, 2, hops))] * 2
+
+    return pl.pallas_call(
+        partial(gather_body, pieces, chips, len(sources)),
+        out_shape=[
+            jax.ShapeDtypeStruct((chips * source.shape[0], source.shape[1]), source.dtype)
+            for source in sources
+        ],
+        in_specs=[pl.BlockSpec(memory_space=pl.ANY)] * len(sources),
+        out_specs=[pl.BlockSpec(memory_space=pl.ANY)] * len(sources),
+        scratch_shapes=sems(len(pieces))
+        + sems(len(pieces) + splits)
+        + sems(splits)
+        + [pltpu.SemaphoreType.DMA((len(sources),))],
+        compiler_params=pltpu.CompilerParams(collective_id=identity, has_side_effects=True),
+    )(*sources)
+
+
+def chip_rows(shard):
+    other = swap_cores(shard)
+    core = lax.axis_index("fsdp") % 2
+    return jnp.where(
+        core == 0, jnp.concatenate([shard, other]), jnp.concatenate([other, shard])
+    )
+
+
 def by_chip(values):
     chips = lax.axis_size("fsdp") // 2
     return values.T.reshape(chips, -1, values.shape[0])
@@ -345,15 +546,9 @@
     return values.T.reshape(chips, 2, -1, values.shape[0])
 
 
-def padded_halves(values, half):
-    tokens, columns = values.shape
-    halves = values.reshape(tokens, 2, columns // 2)
-    return jnp.pad(halves, ((0, 0), (0, 0), (0, half - columns // 2))).reshape(tokens, 2 * half)
-
-
 def join_cores(pieces):
     core = lax.axis_index("fsdp") % 2
-    both = jnp.concatenate(pieces, axis=1)
+    both = jnp.concatenate([piece for piece, _ in pieces], axis=1)
     rows = both.shape[0] // 2
     mine = lax.dynamic_slice_in_dim(both, core * rows, rows, axis=0)
     sent = lax.dynamic_slice_in_dim(both, (1 - core) * rows, rows, axis=0)
@@ -361,15 +556,12 @@
     low = jnp.where(core == 0, mine, other)
     high = jnp.where(core == 0, other, mine)
     joined, at = [], 0
-    for piece in pieces:
+    for piece, columns in pieces:
         end = at + piece.shape[1]
-        joined += [low[:, at:end], high[:, at:end]]
+        twice = 2 * piece.shape[1] - columns
+        joined += [low[:, at:end], high[:, at + twice : end]]
         at = end
     return jnp.concatenate(joined, axis=1)
-
-
-def round_up(value, step):
-    return -(-value // step) * step
 
 
 def plain_sum(left, right):
@@ -397,36 +589,31 @@
             axis=1,
         )
         return (wide, plain_sum(active, feed_grad))
-    triple_half = round_up(triple_grad.shape[1] // 2, 256)
-    branch_half = round_up(branch_grad.shape[1] // 2, 128)
-    pre_half = pre_grad.shape[1] // 2
+    triple_half = core_columns(triple_grad.shape[1])
+    branch_half = core_columns(branch_grad.shape[1])
+    pre_half = core_columns(pre_grad.shape[1])
     plain_part = 8 * 128
     pre_part = (pre_half - plain_part) // 2
     deep_rows = active.shape[1] // lax.axis_size("fsdp") // 2
     terms = (
-        Term(0, 0, 2 * rows, 0, triple_half // 2, 0, True, 0, 1),
+        Term(3, 3, deep_rows, 0, MODEL_WIDTH, 0, False, 0, 0),
+        Term(3, 3, deep_rows, deep_rows, MODEL_WIDTH, 0, False, 1, 0),
         Term(2, 2, 2 * rows, 0, pre_part, plain_part, True, 1, 1),
-        Term(3, 3, deep_rows, 0, MODEL_WIDTH, 0, False, 0, 1),
-        Term(3, 3, deep_rows, deep_rows, MODEL_WIDTH, 0, False, 1, 1),
-        Term(1, 1, 2 * rows, 0, branch_half, 0, False, 0, 2),
+        Term(0, 0, 2 * rows, 0, triple_half // 2, 0, True, 0, 2),
         Term(2, 2, 2 * rows, 0, plain_part, 0, False, 1, 2),
-    )
-    triple, pre_late, deep_low, deep_high, branch, pre_early = reduce_terms(
+        Term(1, 1, 2 * rows, 0, branch_half, 0, False, 0, 3),
+    )
+    deep_low, deep_high, pre_late, triple, pre_early, branch = reduce_terms(
         terms,
         [by_chip(normed), by_chip(attended), by_chip(mixed), by_device(active)],
-        [
-            padded_halves(triple_grad, triple_half),
-            padded_halves(branch_grad, branch_half),
-            pre_grad,
-            feed_grad,
-        ],
+        [triple_grad, branch_grad, pre_grad, feed_grad],
         identity,
     )
     wide = join_cores(
         [
-            triple[:, : triple_grad.shape[1] // 2],
-            branch[:, : branch_grad.shape[1] // 2],
-            jnp.concatenate([pre_early, pre_late], axis=1),
+            (triple, triple_grad.shape[1]),
+            (branch, branch_grad.shape[1]),
+            (jnp.concatenate([pre_early, pre_late], axis=1), pre_grad.shape[1]),
         ]
     )
     return (wide, jnp.concatenate([deep_low, deep_high], axis=0))
@@ -456,19 +643,53 @@
         identity,
     )
     return (
-        join_cores([first_out]),
-        join_cores([second_out, jnp.concatenate([third_early, third_late], axis=1)]),
-    )
+        join_cores([(first_out, first_grad.shape[1])]),
+        join_cores(
+            [
+                (second_out, second_grad.shape[1]),
+                (jnp.concatenate([third_early, third_late], axis=1), projected_grad.shape[1]),
+            ]
+        ),
+    )
+
+
+def pack_body(*refs):
+    out, at = refs[-1], 0
+    for ref in refs[:-1]:
+        width = ref.shape[1]
+        out[:, at : at + width] = ref[...].astype(jnp.float32)
+        at += width
+
+
+def pack_rows(pieces):
+    rows = pieces[0].shape[0]
+    width = sum(piece.shape[1] for piece in pieces)
+    return pl.pallas_call(
+        pack_body, out_shape=jax.ShapeDtypeStruct((rows, width), jnp.float32)
+    )(*pieces)
 
 
 def gathered_terms(row):
     return lax.all_gather(row, ("fsdp", "rep"), axis=0, tiled=True)
 
 
-def fetch_block(wide_shard, deep_shard):
+def fetch_block(wide_shard, deep_shard, identity):
     rest = wide_shard[:, 6 * MODEL_WIDTH :].astype(jnp.bfloat16)
-    whole = lax.all_gather(rest, "fsdp", axis=0, tiled=True)
-    deep = lax.all_gather(deep_shard.astype(jnp.bfloat16), "fsdp", axis=0, tiled=True)
+    low = deep_shard.astype(jnp.bfloat16)
+    rows = rest.shape[0]
+    if identity is not None and kernels_fit(rows):
+        unit = MODEL_WIDTH
+        deep_rows = low.shape[0] // 2
+        pieces = (
+            Piece(0, 2 * rows, unit, 0, 0, 2 * unit, 4 * unit, unit, True, 0),
+            Piece(1, deep_rows, unit, 2 * deep_rows, deep_rows, 0, 0, 0, True, 1),
+            Piece(0, 2 * rows, unit, 0, 0, 0, 4 * unit, 0, False, 0),
+            Piece(0, 2 * rows, unit, 0, 0, unit, 4 * unit, 0, False, 1),
+        )
+        whole, deep = gather_pieces(pieces, [chip_rows(rest), chip_rows(low)], identity)
+    else:
+        whole = lax.all_gather(rest, "fsdp", axis=0, tiled=True)
+        deep = lax.all_gather(low, "fsdp", axis=0, tiled=True)
     split = (
         whole[:, : 3 * MODEL_WIDTH],
         whole[:, 3 * MODEL_WIDTH : 4 * MODEL_WIDTH],
@@ -502,54 +723,127 @@
     return [total[:, block] + block_bias[block, : 6 * MODEL_WIDTH] for block in range(2)]
 
 
-def attention_forward(inputs):
-    queries, keys_in, values_in, visible = inputs
-    factor = queries.shape[-1] ** (-0.5)
-    scores = (
-        jnp.einsum("qhd,khd->hqk", queries, keys_in, preferred_element_type=jnp.float32) * factor
-    )
-    scores = jnp.where(visible[None, None, :], scores, masked_score)
-    largest = jnp.max(scores, axis=-1, keepdims=True)
-    expanded = jnp.exp(scores - largest)
-    totals = jnp.sum(expanded, axis=-1, keepdims=True)
-    weights = (expanded / totals).astype(jnp.bfloat16)
-    attended = jnp.einsum("hqk,khd->qhd", weights, values_in, preferred_element_type=jnp.float32)
-    return (attended, largest + jnp.log(totals))
-
-
-def attention_scores_backward(queries, keys_in, values_in, visible, log_total, upstream):
-    factor = queries.shape[-1] ** (-0.5)
-    scores = (
-        jnp.einsum("sqhd,skhd->shqk", queries, keys_in, preferred_element_type=jnp.float32)
-        * factor
-    )
-    scores = jnp.where(visible[:, None, None, :], scores, masked_score)
-    chances = jnp.exp(scores - log_total)
-    chance_grad = jnp.einsum(
-        "sqhd,skhd->shqk", upstream, values_in, preferred_element_type=jnp.float32
-    )
-    centre = jnp.sum(chance_grad * chances, axis=-1, keepdims=True)
-    score_grad = (chances * (chance_grad - centre)).astype(jnp.bfloat16)
-    return (chances.astype(jnp.bfloat16), score_grad)
-
-
-def attention_products_backward(queries, keys_in, chances_low, score_grad, upstream):
-    factor = queries.shape[-1] ** (-0.5)
-    value_grad = jnp.einsum(
-        "shqk,sqhd->skhd", chances_low, upstream, preferred_element_type=jnp.float32
-    )
-    query_grad = (
-        jnp.einsum("shqk,skhd->sqhd", score_grad, keys_in, preferred_element_type=jnp.float32)
-        * factor
-    )
-    key_grad = (
-        jnp.einsum("shqk,sqhd->skhd", score_grad, queries, preferred_element_type=jnp.float32)
-        * factor
-    )
-    return (query_grad, key_grad, value_grad)
-
-
-def block_forward(hidden, modulation, wide_matrix, deep_matrix, bias, visible):
+HEAD_WINDOW = 256
+
+
+def head_window(head, width):
+    first = head * HEAD_DIM
+    at = min(first // 128 * 128, width - HEAD_WINDOW)
+    lane = lax.broadcasted_iota(jnp.int32, (1, HEAD_WINDOW), 1)
+    return at, (lane >= first - at) & (lane < first - at + HEAD_DIM)
+
+
+def only(mine, values):
+    return jnp.where(mine, values, jnp.zeros_like(values))
+
+
+def against(left, right):
+    return lax.dot_general(
+        left, right, (((1,), (1,)), ((), ())), preferred_element_type=jnp.float32
+    )
+
+
+def attend_body(lengths_ref, triple_ref, attended_ref, log_ref, total_ref):
+    tokens, width = attended_ref.shape
+    length = lengths_ref[pl.program_id(0)]
+    seen = lax.broadcasted_iota(jnp.int32, (tokens, 1), 0) < length
+    total_ref[...] = jnp.zeros_like(total_ref)
+    for head in range(HEADS):
+        at, mine = head_window(head, width)
+        window = pl.ds(at, HEAD_WINDOW)
+        keys = only(mine, triple_ref[:, pl.ds(width + at, HEAD_WINDOW)])
+        values = only(mine, triple_ref[:, pl.ds(2 * width + at, HEAD_WINDOW)])
+        scores = against(keys, triple_ref[:, window]) * HEAD_DIM ** (-0.5)
+        scores = jnp.where(seen, scores, masked_score)
+        largest = jnp.max(scores, axis=0, keepdims=True)
+        expanded = jnp.exp(scores - largest)
+        sums = jnp.sum(expanded, axis=0, keepdims=True)
+        weights = (expanded * (1.0 / sums)).astype(jnp.bfloat16)
+        total_ref[:, window] += lax.dot_general(
+            weights, values, (((0,), (0,)), ((), ())), preferred_element_type=jnp.float32
+        )
+        log_ref[head : head + 1, :] = largest + jnp.log(sums)
+    attended_ref[...] = total_ref[...].astype(jnp.bfloat16)
+
+
+def attention_forward(triple, lengths):
+    sequences, tokens, columns = triple.shape
+    width = columns // 3
+    return pl.pallas_call(
+        attend_body,
+        grid=(sequences,),
+        out_shape=[
+            jax.ShapeDtypeStruct((sequences, tokens, width), jnp.bfloat16),
+            jax.ShapeDtypeStruct((sequences, HEADS, tokens), jnp.float32),
+        ],
+        in_specs=[
+            pl.BlockSpec(memory_space=pltpu.SMEM),
+            pl.BlockSpec((None, tokens, columns), lambda number: (number, 0, 0)),
+        ],
+        out_specs=[
+            pl.BlockSpec((None, tokens, width), lambda number: (number, 0, 0)),
+            pl.BlockSpec((None, HEADS, tokens), lambda number: (number, 0, 0)),
+        ],
+        scratch_shapes=[pltpu.VMEM((tokens, width), jnp.float32)],
+        compiler_params=pltpu.CompilerParams(vmem_limit_bytes=48 * 1024 * 1024),
+    )(lengths, triple)
+
+
+def attend_back_body(lengths_ref, triple_ref, log_ref, upstream_ref, grad_ref, total_ref):
+    tokens, width = upstream_ref.shape
+    length = lengths_ref[pl.program_id(0)]
+    factor = HEAD_DIM ** (-0.5)
+    seen = lax.broadcasted_iota(jnp.int32, (tokens, 1), 0) < length
+    total_ref[...] = jnp.zeros_like(total_ref)
+    for head in range(HEADS):
+        at, mine = head_window(head, width)
+        query_at, key_at, value_at = (
+            pl.ds(group * width + at, HEAD_WINDOW) for group in range(3)
+        )
+        queries = only(mine, triple_ref[:, query_at])
+        keys = only(mine, triple_ref[:, key_at])
+        values = only(mine, triple_ref[:, value_at])
+        upstream = only(mine, upstream_ref[:, pl.ds(at, HEAD_WINDOW)])
+        scores = against(keys, queries) * factor
+        chances = jnp.where(seen, jnp.exp(scores - log_ref[head : head + 1, :]), 0.0)
+        chance_grad = against(values, upstream)
+        centre = jnp.sum(chance_grad * chances, axis=0, keepdims=True)
+        score_grad = (chances * (chance_grad - centre)).astype(jnp.bfloat16)
+        total_ref[:, value_at] += jnp.dot(
+            chances.astype(jnp.bfloat16), upstream, preferred_element_type=jnp.float32
+        )
+        total_ref[:, key_at] += factor * jnp.dot(
+            score_grad, queries, preferred_element_type=jnp.float32
+        )
+        total_ref[:, query_at] += factor * lax.dot_general(
+            score_grad, keys, (((0,), (0,)), ((), ())), preferred_element_type=jnp.float32
+        )
+    grad_ref[...] = total_ref[...].astype(jnp.bfloat16)
+
+
+def attention_backward(triple, logs, upstream, lengths):
+    sequences, tokens, columns = triple.shape
+
+    def spec(width):
+        return pl.BlockSpec((None, tokens, width), lambda number: (number, 0, 0))
+
+    return pl.pallas_call(
+        attend_back_body,
+        grid=(sequences,),
+        out_shape=jax.ShapeDtypeStruct((sequences, tokens, columns), jnp.bfloat16),
+        in_specs=[
+            pl.BlockSpec(memory_space=pltpu.SMEM),
+            spec(columns),
+            pl.BlockSpec((None, HEADS, tokens), lambda number: (number, 0, 0)),
+            spec(columns // 3),
+        ],
+        out_specs=spec(columns),
+        scratch_shapes=[pltpu.VMEM((tokens, columns), jnp.float32)],
+        compiler_params=pltpu.CompilerParams(vmem_limit_bytes=48 * 1024 * 1024),
+    )(lengths, triple, logs, upstream)
+
+
+def block_forward(hidden, modulation, wide_matrix, deep_matrix, bias, lengths):
     sequences = hidden.shape[0]
     offset_first, factor_first, gate_first, offset_second, factor_second, gate_second = (
         split_modulation(modulation)
@@ -570,11 +864,7 @@
         )
         + triple_bias
     ).astype(jnp.bfloat16)
-    pieces = triple.reshape(sequences, SEQ_LEN, 3, HEADS, HEAD_DIM)
-    attended, log_total = lax.map(
-        attention_forward, (pieces[:, :, 0], pieces[:, :, 1], pieces[:, :, 2], visible)
-    )
-    attended_low = attended.reshape(sequences, SEQ_LEN, MODEL_WIDTH).astype(jnp.bfloat16)
+    attended_low, log_total = attention_forward(triple, lengths)
     branch = (
         jnp.dot(
             attended_low,
@@ -612,7 +902,7 @@
     return (result, saved)
 
 
-def block_backward(upstream, saved, wide_matrix, deep_matrix, visible, identity):
+def block_backward(upstream, saved, wide_matrix, deep_matrix, lengths):
     (
         hidden,
         modulation,
@@ -656,23 +946,7 @@
         wide_matrix[1],
         preferred_element_type=jnp.float32,
     ).astype(jnp.bfloat16)
-    pieces = triple.reshape(sequences, SEQ_LEN, 3, HEADS, HEAD_DIM)
-    heads_grad = attended_grad.reshape(sequences, SEQ_LEN, HEADS, HEAD_DIM)
-    queries, keys_in, values_in = pieces[:, :, 0], pieces[:, :, 1], pieces[:, :, 2]
-    chances_low, score_grad = attention_scores_backward(
-        queries, keys_in, values_in, visible, log_total, heads_grad
-    )
-    query_grad, key_grad, value_grad = attention_products_backward(
-        queries, keys_in, chances_low, score_grad, heads_grad
-    )
-    triple_gradient = jnp.concatenate(
-        [
-            query_grad.reshape(sequences, SEQ_LEN, MODEL_WIDTH),
-            key_grad.reshape(sequences, SEQ_LEN, MODEL_WIDTH),
-            value_grad.reshape(sequences, SEQ_LEN, MODEL_WIDTH),
-        ],
-        axis=-1,
-    ).astype(jnp.bfloat16)
+    triple_gradient = attention_backward(triple, log_total, attended_grad, lengths)
     normed_grad = jnp.einsum(
         "tbr,ar->tba",
         triple_gradient,
@@ -682,43 +956,45 @@
     first_back = jax.vjp(modulate, hidden, offset_first, factor_first)[1]
     hidden_part, offset_first_grad, factor_first_grad = first_back(normed_grad)
     hidden_grad = middle_grad + hidden_part
-    modulation_grad = jnp.concatenate(
-        [
-            offset_first_grad[:, 0],
-            factor_first_grad[:, 0],
+    def column_sum(values):
+        return jnp.sum(values, axis=(0, 1), dtype=jnp.float32)[None]
+
+    triple_sum = column_sum(triple_gradient)
+    row_pieces = [
+        piece.reshape(1, -1).astype(jnp.bfloat16)
+        for piece in (
+            offset_first_grad,
+            factor_first_grad,
             gate_first_grad,
-            offset_second_grad[:, 0],
-            factor_second_grad[:, 0],
+            offset_second_grad,
+            factor_second_grad,
             gate_second_grad,
-        ],
-        axis=-1,
-    ).astype(jnp.bfloat16)
-    bias_row = jnp.concatenate(
-        [
-            modulation_grad.astype(jnp.float32).sum(axis=0),
-            jnp.sum(triple_gradient[..., :MODEL_WIDTH], axis=(0, 1), dtype=jnp.float32),
-            jnp.sum(triple_gradient[..., 2 * MODEL_WIDTH :], axis=(0, 1), dtype=jnp.float32),
-            jnp.sum(branch_gradient, axis=(0, 1), dtype=jnp.float32),
-            jnp.sum(preactivation_gradient, axis=(0, 1), dtype=jnp.float32),
-            jnp.sum(feedforward_gradient, axis=(0, 1), dtype=jnp.float32),
-        ]
-    )
+        )
+    ] + [
+        triple_sum[:, :MODEL_WIDTH],
+        triple_sum[:, 2 * MODEL_WIDTH :],
+        column_sum(branch_gradient),
+        column_sum(preactivation_gradient),
+        column_sum(feedforward_gradient),
+    ]
 
     def flat(values):
         return values.reshape(-1, values.shape[-1])
 
-    weight_grads = sum_block_grads(
-        flat(normed_low),
-        flat(triple_gradient),
-        flat(attended_low),
-        flat(branch_gradient),
-        flat(mixed_low),
-        flat(preactivation_gradient),
-        flat(active_low),
-        flat(feedforward_gradient),
-        identity,
-    )
-    return (hidden_grad, modulation_grad, bias_row, weight_grads)
+    factors = [
+        flat(values)
+        for values in (
+            normed_low,
+            triple_gradient,
+            attended_low,
+            branch_gradient,
+            mixed_low,
+            preactivation_gradient,
+            active_low,
+            feedforward_gradient,
+        )
+    ]
+    return (hidden_grad, row_pieces, factors)
 
 
 def adam_update(weight, grad, first, second, rate, decay):
@@ -759,18 +1035,18 @@
     hidden = tokens.astype(jnp.float32).reshape(sequences, SEQ_LEN, MODEL_WIDTH)
     silu_low = jax.nn.silu(condition.astype(jnp.float32)).astype(jnp.bfloat16)
     visible = jnp.arange(SEQ_LEN, dtype=jnp.int32)[None, :] < lengths[:, None]
-    wide_early, deep_early = fetch_block(wide_weight[0], deep_weight[0])
+    wide_early, deep_early = fetch_block(wide_weight[0], deep_weight[0], 3)
     modulation_early, modulation_late = plane_modulation(silu_low, wide_weight, block_bias)
     tapped, saved_early = block_forward(
-        hidden, modulation_early, wide_early, deep_early, block_bias[0], visible
-    )
-    wide_late, deep_late = fetch_block(wide_weight[1], deep_weight[1])
+        hidden, modulation_early, wide_early, deep_early, block_bias[0], lengths
+    )
+    wide_late, deep_late = fetch_block(wide_weight[1], deep_weight[1], None)
     first_matrix, second_w = (
         lax.all_gather(head_first.astype(jnp.bfloat16), "fsdp", axis=0, tiled=True),
         lax.all_gather(head_second.astype(jnp.bfloat16), "fsdp", axis=0, tiled=True),
     )
     final, saved_late = block_forward(
-        tapped, modulation_late, wide_late, deep_late, block_bias[1], visible
+        tapped, modulation_late, wide_late, deep_late, block_bias[1], lengths
     )
     raw_targets = targets.astype(jnp.float32).reshape(sequences, SEQ_LEN, PZ)
     target_unit = raw_targets * lax.rsqrt(
@@ -782,8 +1058,8 @@
         return jnp.sum(unit * target_unit, axis=-1)
 
     upstream = cotangent.astype(jnp.float32).reshape(sequences, SEQ_LEN, MODEL_WIDTH)
-    late_input_grad, late_modulation_grad, late_row, late_grads = block_backward(
-        upstream, saved_late, wide_late, deep_late, visible, 0
+    late_input_grad, late_row, late_factors = block_backward(
+        upstream, saved_late, wide_late, deep_late, lengths
     )
     tapped_low, late_input_grad = lax.optimization_barrier(
         (tapped.astype(jnp.bfloat16), late_input_grad)
@@ -815,46 +1091,50 @@
     tapped_gradient = jnp.einsum(
         "ejk,rk->ejr", first_gradient, first_matrix, preferred_element_type=jnp.float32
     )
-    head_row = jnp.concatenate(
-        [
-            jnp.sum(first_gradient, axis=(0, 1), dtype=jnp.float32),
-            jnp.sum(second_grad, axis=(0, 1), dtype=jnp.float32),
-            jnp.sum(projected_grad, axis=(0, 1), dtype=jnp.float32),
-        ]
-    )
-
+
+    def column_sum(values):
+        return jnp.sum(values, axis=(0, 1), dtype=jnp.float32)[None]
 
     def flat(values):
         return values.reshape(-1, values.shape[-1])
 
-    first_weight_grad, second_weight_grad = sum_head_grads(
+    input_grad, early_row, early_factors = block_backward(
+        late_input_grad + tapped_gradient, saved_early, wide_early, deep_early, lengths
+    )
+    row = pack_rows(
+        [silu_low]
+        + early_row
+        + late_row
+        + [column_sum(first_gradient), column_sum(second_grad), column_sum(projected_grad)]
+    )
+    row, early_factors, late_factors, first_gradient = lax.optimization_barrier(
+        (row, early_factors, late_factors, first_gradient)
+    )
+    rows = gathered_terms(row)
+    late_grads = sum_block_grads(*late_factors, 0)
+    head_factors = (
         flat(tapped_low),
         flat(first_gradient),
         flat(first_low),
         flat(second_grad),
         flat(second_low),
         flat(projected_grad),
-        1,
-    )
-    input_grad, early_modulation_grad, early_row, early_grads = block_backward(
-        late_input_grad + tapped_gradient,
-        saved_early,
-        wide_early,
-        deep_early,
-        visible,
-        2,
-    )
-    late_rows = gathered_terms(
-        jnp.concatenate([silu_low.astype(jnp.float32)[0], late_row, head_row])[None]
-    )
+    )
+    late_grads, head_factors = lax.optimization_barrier((late_grads, head_factors))
+    first_weight_grad, second_weight_grad = sum_head_grads(*head_factors, 1)
+    rows, early_factors, first_weight_grad = lax.optimization_barrier(
+        (rows, early_factors, first_weight_grad)
+    )
+    early_grads = sum_block_grads(*early_factors, 2)
     own_silu = lax.dynamic_slice_in_dim(
-        late_rows,
+        rows,
         lax.axis_index("fsdp") * wide_weight.shape[1],
         wide_weight.shape[1],
         axis=1,
     ).astype(jnp.bfloat16)
-    late_rows = late_rows[:, MODEL_WIDTH:]
-    early_rows = gathered_terms(early_row[None])
+    bias_width = block_bias.shape[1]
+    early_rows = rows[:, MODEL_WIDTH : MODEL_WIDTH + bias_width]
+    late_rows = rows[:, MODEL_WIDTH + bias_width : MODEL_WIDTH + 2 * bias_width]
 
     def modulation_weight_grad(rows):
         return lax.dot_general(
@@ -864,7 +1144,6 @@
             preferred_element_type=jnp.float32,
         )
 
-    bias_width = block_bias.shape[1]
     wide_grad = jnp.stack(
         [
             jnp.concatenate(
@@ -878,9 +1157,9 @@
         ]
     )
     deep_grad = jnp.stack([early_grads[1], late_grads[1]])
-    late_sum = jnp.sum(late_rows, axis=0)
-    block_bias_grad = jnp.stack([jnp.sum(early_rows, axis=0), late_sum[:bias_width]])
-    head_bias_total = late_sum[bias_width:]
+    row_sum = jnp.sum(rows, axis=0)[MODEL_WIDTH:]
+    block_bias_grad = row_sum[: 2 * bias_width].reshape(2, bias_width)
+    head_bias_total = row_sum[2 * bias_width :]
     wide_m, wide_v, wide_new = adam_update(
         wide_weight, wide_grad, wide_mean, wide_square, matrix_rate, matrix_decay
     )

time: 1360 us -> 1130 us (0.83)
  waiting for transfers between devices: 321 us -> 38.3 us
  Pallas kernels: 418 us -> 683 us
  matrix products: 289 us -> 192 us
  local copies, waits for them, and re-layouts: 178 us -> 97.9 us
  other arithmetic: 120 us -> 77.1 us
    pallas_call x0 -> x6, Pallas kernels: none -> 257 us  [the longest x1 213 us: gather_pieces(): pl.pallas_call(partial(gather_body, pieces, chips, len(sources)), out_sha...]
    all_gather x2 -> x1, waiting for transfers between devices: 156 us -> 0.02 us  [fetch_block(): whole = lax.all_gather(rest, 'fsdp', axis=0, tiled=True)]
    dot_general x12 -> x0, matrix products: 85.8 us -> none  [the longest x2 26.7 us: attention_scores_backward(): jnp.einsum('sqhd,skhd->shqk', upstream, values_in, preferred_element_type...]
    all_gather x2 -> x1, waiting for transfers between devices: 68 us -> 0.01 us  [fetch_block(): deep = lax.all_gather(low, 'fsdp', axis=0, tiled=True)]
    convert_element_type x9 -> x12, local copies, waits for them, and re-layouts: 42.6 us -> 7.15 us  [block_backward(): piece.reshape(1, -1).astype(jnp.bfloat16)]
    all_to_all x1, waiting for transfers between devices: 29.5 us -> 0.01 us  [plane_modulation(): back = lax.all_to_all(partial, 'fsdp', 0, 0, tiled=True)]
    reduce_sum x12 -> x8, other arithmetic: 29.5 us -> 5.38 us  [the longest x7 4.82 us: column_sum(): return jnp.sum(values, axis=(0, 1), dtype=jnp.float32)[None]]
    all_gather x2 -> x1, waiting for transfers between devices: 23.1 us -> 0.01 us  [gathered_terms(): return lax.all_gather(row, ('fsdp', 'rep'), axis=0, tiled=True)]
  transfers between devices with their start and end apart: 14 -> 13, of which waited for: 8 -> 2; matrix products, arithmetic and copies ran while one was open for 28% -> 17% of each run, Pallas kernels for 31% -> 31%
where the time goes in v3:
time: 1130 us; the launch traced here: 1120 us
  Pallas kernels  683 us (60%)
  matrix products  192 us (17%)
  local copies, waits for them, and re-layouts  97.9 us (9%)
  other arithmetic  77.1 us (7%)
  waiting for transfers between devices  38.3 us (3%)
  between operations  16.5 us (1%)
  starting transfers between devices  14.6 us (1%)
    pallas_call x3, Pallas kernels, reduce_terms(): pl.pallas_call(partial(reduce_body, terms, chips, len(lefts), len(rights)...  426 us
    pallas_call x1, Pallas kernels, gather_pieces(): pl.pallas_call(partial(gather_body, pieces, chips, len(sources)), out_sha...  213 us
    sub x6, other arithmetic, adam_update(): weight - rate * (first_hat / (jnp.sqrt(second_hat) + adam_epsilon) + deca...  37.6 us
    all_gather x1, waiting for transfers between devices, per_device(): lax.all_gather(head_second.astype(jnp.bfloat16), 'fsdp', axis=0, tiled=True)  37.2 us
    unnamed x251, local copies, waits for them, and re-layouts  34.8 us
    pallas_call x2, Pallas kernels, attention_backward(): pl.pallas_call(attend_back_body, grid=(sequences,), out_shape=jax.ShapeDt...  27.8 us
    dot_general x2, matrix products, block_backward(): jnp.einsum('xjn,mn->xjm', feedforward_gradient, deep_matrix, preferred_el...  27.3 us
    dot_general x2, matrix products, block_forward(): jnp.dot(mixed_low, wide_matrix[2], preferred_element_type=jnp.float32)  24.1 us
  transfers between devices with their start and end apart: 13, of which 2 were waited for; matrix products, arithmetic and copies ran while one was open for 17% of the time, Pallas kernels for 31%

profile of v3, /device:TPU:0, one launch (start us, length us, event | category | flops | bytes accessed | tf_op | source)
XLA Modules:
  0.0 1119.5 jit_solution(17863013772904542893)
XLA Ops:
  20.0 7.4 all-to-all-start
  52.3 213.1 %shard_map.422 = (bf16[1152,9216]{1,0:T(8,128)(2,1)}, bf16[4608,1152]{1,0:T(8,128)(2,1)}) custom-call(bf16[144,9216]{1,0:T(8,128)(2,1)} %maximum_select_fusion.refs_0_, bf16[576,1152]{1,0:T(8,128)(2,1)} %maximum_select_fusion.1.refs_1_), custom_call_target="tpu_custom_call" | custom-call | tf_op jit(solution)/shard_map/pallas_call | solution.py:515
  267.4 9.2 fusion.51.triple_ref
  276.7 7.1 shard_map.423
  289.7 11.9 %multiply_convert_fusion.1 = (bf16[448,4608]{1,0:T(8,128)(2,1)S(1)}, f32[448,4608]{1,0:T(8,128)}) fusion(f32[4608]{0:T(1024)S(1)} %get-tuple-element.175, bf16[448,1152]{1,0:T(8,128)(2,1)S(1)} %add_convert_fusion.5, bf16[1152,9216]{1,0:T(8,128)(2,1)} %get-tuple-element.86), kind=kOutput, calls=%fused_computation.39 | convolution fusion | flops 4776984576 | bytes 24053760 | tf_op jit(solution)/shard_map/dot_general | solution.py:879
  301.7 9.9 convolution_add_fusion
  318.8 8.2 fusion.54.triple_ref
  327.0 7.1 shard_map.424
  341.0 12.2 %multiply_convert_fusion = (bf16[448,4608]{1,0:T(8,128)(2,1)}, f32[448,4608]{1,0:T(8,128)}) fusion(f32[4608]{0:T(1024)S(1)} %get-tuple-element.174, bf16[448,1152]{1,0:T(8,128)(2,1)S(1)} %add_convert_fusion.3, bf16[1152,9216]{1,0:T(8,128)(2,1)} %all-gather.8.cloned.1.call-done), kind=kOutput, calls=%fused_computation.38 | convolution fusion | flops 4776984576 | bytes 24053760 | tf_op jit(solution)/shard_map/dot_general | solution.py:879
  353.2 13.9 %convert_reduce_fusion = (f32[4608]{0:T(1024)}, bf16[448,4608]{1,0:T(8,128)(2,1)S(1)}) fusion(f32[448,4608]{1,0:T(8,128)} %get-tuple-element.267, bf16[448,1152]{1,0:T(8,128)(2,1)} %get-tuple-element.110.refs_7_, bf16[1,4608,1152]{2,1,0:T(8,128)(2,1)} %all-gather.14.cloned.1.call-done), kind=kOutput, calls=%fused_computation.36 | convolution fusion | flops 4801752576 | bytes 24053760 | tf_op jit(solution)/shard_map/xjn,mn->xjm/dot_general | solution.py:926
  367.1 12.1 %multiply_reduce_fusion = (bf16[1152]{0:T(1024)(128)(2,1)}, f32[448]{0:T(512)S(1)}, bf16[1152]{0:T(1024)(128)(2,1)}, f32[448,1152]{1,0:T(8,128)S(1)}) fusion(f32[448,1152]{1,0:T(8,128)S(1)} %get-tuple-element.228, f32[448]{0:T(512)S(1)} %fusion.133, f32[448]{0:T(512)S(1)} %broadcast_multiply_fusion, f32[1152]{0:T(1024)S(1)} %get-tuple-element.178, ...), kind=kOutput, calls=%fused_computation.137 | convolution fusion | flops 4760466944 | bytes 18888960 | tf_op jit(solution)/shard_map/qvm,am->qva/dot_general | solution.py:932
  385.4 13.9 %shard_map.425 = bf16[1,448,3456]{2,1,0:T(8,128)(2,1)S(1)} custom-call(s32[1]{0:T(128)} %copy.130.lengths_ref, bf16[1,448,3456]{2,1,0:T(8,128)(2,1)} %copy-done.4, f32[1,16,448]{2,1,0:T(8,128)S(1)} %get-tuple-element.90.log_ref, bf16[1,448,1152]{2,1,0:T(8,128)(2,1)S(1)} %fusion.75.upstream_ref), custom_call_target="tpu_custom_call" | custom-call | tf_op jit(solution)/shard_map/pallas_call | solution.py:830
  399.3 8.9 multiply_reduce_fusion.2
  411.1 13.0 %fusion.92 = (bf16[1152]{0:T(1024)(128)(2,1)S(1)}, bf16[1152]{0:T(1024)(128)(2,1)S(1)}, f32[1,448,1152]{2,1,0:T(8,128)}, bf16[448,1152]{1,0:T(8,128)(2,1)}) fusion(bf16[448,1152]{1,0:T(8,128)(2,1)S(1)} %copy-done.36, f32[448,1152]{1,0:T(8,128)S(1)} %copy-done.114, f32[448,1152]{1,0:T(8,128)S(1)} %get-tuple-element.224, f32[448]{0:T(512)S(1)} %negate_multiply_fusion.3, ...), kind=kOutput, calls=%fused_computation.127 | convolution fusion | flops 4763047936 | bytes 27149312 | tf_op jit(solution)/shard_map/dot_general | solution.py:884
  431.2 37.2 %all-gather.12.cloned.1.call-done = bf16[2048,2816]{1,0:T(8,128)(2,1)} async-done(((bf16[128,2816]{1,0:T(8,128)(2,1)}), bf16[2048,2816]{1,0:T(8,128)(2,1)}) %all-gather.12.cloned.1.call-update) | async-done | bytes 11534352 | tf_op jit(solution)/shard_map/all_gather | solution.py:1046
  481.1 10.6 convert_reduce_fusion.5
  497.8 13.4 %convert_reduce_fusion.1 = (f32[4608]{0:T(1024)S(1)}, bf16[448,4608]{1,0:T(8,128)(2,1)S(1)}) fusion(f32[448,4608]{1,0:T(8,128)} %get-tuple-element.264, bf16[448,1152]{1,0:T(8,128)(2,1)S(1)} %get-tuple-element.133.refs_7_, bf16[4608,1152]{1,0:T(8,128)(2,1)} %get-tuple-element.88), kind=kOutput, calls=%fused_computation.37 | convolution fusion | flops 4801752576 | bytes 24053760 | tf_op jit(solution)/shard_map/xjn,mn->xjm/dot_general | solution.py:926
  511.3 11.3 %multiply_reduce_fusion.3 = (bf16[1152]{0:T(1024)(128)(2,1)S(1)}, f32[448]{0:T(512)S(1)}, bf16[1152]{0:T(1024)(128)(2,1)S(1)}, f32[448,1152]{1,0:T(8,128)S(1)}) fusion(f32[448,1152]{1,0:T(8,128)S(1)} %copy-done.13, f32[448]{0:T(512)S(1)} %copy-done.101, f32[448]{0:T(512)S(1)} %copy-done.96, f32[1152]{0:T(1024)S(1)} %copy-done.85, ...), kind=kOutput, calls=%fused_computation.142 | convolution fusion | flops 4760466944 | bytes 18888960 | tf_op jit(solution)/shard_map/qvm,am->qva/dot_general | solution.py:932
  529.3 14.0 %shard_map.426 = bf16[1,448,3456]{2,1,0:T(8,128)(2,1)S(1)} custom-call(s32[1]{0:T(128)} %copy.130.lengths_ref, bf16[1,448,3456]{2,1,0:T(8,128)(2,1)} %copy-done.3, f32[1,16,448]{2,1,0:T(8,128)S(1)} %get-tuple-element.93.log_ref, bf16[1,448,1152]{2,1,0:T(8,128)(2,1)S(1)} %fusion.76.upstream_ref), custom_call_target="tpu_custom_call" | custom-call | tf_op jit(solution)/shard_map/pallas_call | solution.py:830
  543.3 8.8 fusion.90
  581.5 159.8 %shard_map.428 = (f32[144,1152]{1,0:T(8,128)}, f32[144,1152]{1,0:T(8,128)}, f32[144,1280]{1,0:T(8,128)}, f32[144,1792]{1,0:T(8,128)}, f32[144,1024]{1,0:T(8,128)}, /*index=5*/f32[144,640]{1,0:T(8,128)}) custom-call(bf16[8,144,448]{2,1,0:T(8,128)(2,1)} %bitcast.178, bf16[8,144,448]{2,1,0:T(8,128)(2,1)} %bitcast.180, bf16[8,144,448]{2,1,0:T(8,128)(2,1)} %bitcast.182, ...), custom_call_target="tpu_custom_call" | custom-call | tf_op jit(solution)/shard_map/pallas_call | solution.py:328
  764.3 106.4 %shard_map.429 = (f32[256,1024]{1,0:T(8,128)}, f32[144,1024]{1,0:T(8,128)}, f32[256,256]{1,0:T(8,128)}, f32[256,128]{1,0:T(8,128)}) custom-call(bf16[8,144,448]{2,1,0:T(8,128)(2,1)} %bitcast.184, bf16[8,256,448]{2,1,0:T(8,128)(2,1)} %bitcast.175, bf16[8,256,448]{2,1,0:T(8,128)(2,1)} %bitcast.176, bf16[448,2048]{1,0:T(8,128)(2,1)} %copy-done.58, ...), custom_call_target="tpu_custom_call" | custom-call | tf_op jit(solution)/shard_map/pallas_call | solution.py:328
  902.2 160.0 %shard_map.430 = (f32[144,1152]{1,0:T(8,128)}, f32[144,1152]{1,0:T(8,128)}, f32[144,1280]{1,0:T(8,128)}, f32[144,1792]{1,0:T(8,128)}, f32[144,1024]{1,0:T(8,128)}, /*index=5*/f32[144,640]{1,0:T(8,128)}) custom-call(bf16[8,144,448]{2,1,0:T(8,128)(2,1)} %bitcast.179, bf16[8,144,448]{2,1,0:T(8,128)(2,1)} %bitcast.181, bf16[8,144,448]{2,1,0:T(8,128)(2,1)} %bitcast.183, ...), custom_call_target="tpu_custom_call" | custom-call | tf_op jit(solution)/shard_map/pallas_call | solution.py:328
  1087.5 25.2 %multiply_subtract_fusion = (f32[2,72,16128]{2,1,0:T(8,128)}, f32[2,72,16128]{2,1,0:T(8,128)}, f32[2,72,16128]{2,1,0:T(8,128)}, f32[2,72,16128]{2,1,0:T(8,128)}) fusion(f32[2,72,16128]{2,1,0:T(8,128)} %param.28, f32[2,72,16128]{2,1,0:T(8,128)} %param.40, f32[2,72,16128]{2,1,0:T(8,128)} %param.34, f32[1,72,16128]{2,1,0:T(8,128)S(1)} %maximum_bitcast_fusion, ...), kind=kLoop, calls=%fused_computation.19 | loop fusion | flops 37158912 | bytes 74317824 | tf_op jit(solution)/shard_map/sub | solution.py:1005
  (425 shorter events, 208.5 us)
Async XLA Ops:
  7.2 310.7 %all-gather.8.cloned.1.call-start = ((), (), s32[]{:S(2)}) async-start(), calls=%async_computation.2 | async-start | bytes 22560768 | tf_op jit(solution)/shard_map/all_gather | solution.py:691
  15.4 337.8 %all-gather.14.cloned.1.call-start = ((), (), s32[]{:S(2)}) async-start(), calls=%async_computation.5 | async-start | bytes 11280384 | tf_op jit(solution)/shard_map/all_gather | solution.py:692
  17.8 406.3 %all-gather.10.cloned.1.call-start = ((), (), s32[]{:S(2)}) async-start(), calls=%async_computation.3 | async-start | bytes 5013504 | tf_op jit(solution)/shard_map/all_gather | solution.py:1045
  20.0 13.8 %all-to-all-start = ((bf16[16,1,72]{2,1,0:T(2,128)(2,1)}), bf16[16,1,72]{2,1,0:T(2,128)(2,1)S(1)}, u32[]{:S(2)}, u32[]{:S(2)}) async-start(bf16[16,1,72]{2,1,0:T(2,128)(2,1)} %squeeze_transpose_reshape.4), calls=%async_computation | async-start | bytes 16384 | tf_op jit(solution)/shard_map/all_to_all | solution.py:710
  27.3 441.0 %all-gather.12.cloned.1.call-start = ((), (), s32[]{:S(2)}) async-start(), calls=%async_computation.4 | async-start | bytes 12255232 | tf_op jit(solution)/shard_map/all_gather | solution.py:1046
  30.0 18.5 %collective-permute-start = (bf16[72,9216]{1,0:T(8,128)(2,1)}, bf16[72,9216]{1,0:T(8,128)(2,1)}, u32[]{:S(2)}, u32[]{:S(2)}) collective-permute-start(bf16[72,9216]{1,0:T(8,128)(2,1)} %slice.344), channel_id=1, source_target_pairs={{0,2},{2,0},{4,6},{6,4},{8,10},{10,8},{12,14},{14,12},{16,18},{18,... | collective-permute-start | bytes 3981320 | tf_op jit(solution)/shard_map/ppermute | solution.py:61
  30.4 14.9 %collective-permute-start.1 = (bf16[288,1152]{1,0:T(8,128)(2,1)}, bf16[288,1152]{1,0:T(8,128)(2,1)}, u32[]{:S(2)}, u32[]{:S(2)}) collective-permute-start(bf16[288,1152]{1,0:T(8,128)(2,1)} %get-tuple-element.247), channel_id=1, source_target_pairs={{0,2},{2,0},{4,6},{6,4},{8,10},{10,8},{12,14},{14,12},{16,18},{18,... | collective-permute-start | bytes 1990664 | tf_op jit(solution)/shard_map/ppermute | solution.py:61
  32.3 233.6 %copy-start.90 = (f32[448]{0:T(512)}, f32[448]{0:T(512)S(1)}, u32[]{:S(2)}) copy-start(f32[448]{0:T(512)S(1)} %broadcast_multiply_fusion.3) | copy-start | bytes 5380
  32.8 233.2 %copy-start.93 = (f32[448]{0:T(512)}, f32[448]{0:T(512)S(1)}, u32[]{:S(2)}) copy-start(f32[448]{0:T(512)S(1)} %fusion.130) | copy-start | bytes 5380
  38.5 226.9 %all-to-all-start.1 = ((f32[16,1,2,6912]{3,2,1,0:T(2,128)}), f32[16,1,2,6912]{3,2,1,0:T(2,128)S(1)}, u32[]{:S(2)}, u32[]{:S(2)}) async-start(f32[16,1,2,6912]{3,2,1,0:T(2,128)} %copy.85), calls=%async_computation.1 | async-start | bytes 1769472 | tf_op jit(solution)/shard_map/all_to_all | solution.py:721
  44.5 839.3 %all-gather.16.cloned.1.call-start = ((), (), s32[]{:S(2)}) async-start(), calls=%async_computation.6 | async-start | bytes 5051904 | tf_op jit(solution)/shard_map/all_gather | solution.py:673
  265.9 17.9 %copy-start.86 = (f32[1152]{0:T(1024)}, f32[1152]{0:T(1024)S(1)}, u32[]{:S(2)}) copy-start(f32[1152]{0:T(1024)S(1)} %get-tuple-element.187) | copy-start | bytes 13828
  265.9 23.4 %copy-start.84 = (f32[1152]{0:T(1024)}, f32[1152]{0:T(1024)S(1)}, u32[]{:S(2)}) copy-start(f32[1152]{0:T(1024)S(1)} %get-tuple-element.184) | copy-start | bytes 13828
  265.9 45.7 %copy-start.88 = (f32[1152]{0:T(1024)}, f32[1152]{0:T(1024)S(1)}, u32[]{:S(2)}) copy-start(f32[1152]{0:T(1024)S(1)} %get-tuple-element.182) | copy-start | bytes 13828
  288.9 22.7 %copy-start.12 = (f32[448,1152]{1,0:T(8,128)}, f32[448,1152]{1,0:T(8,128)S(1)}, u32[]{:S(2)}) copy-start(f32[448,1152]{1,0:T(8,128)S(1)} %get-tuple-element.230) | copy-start | bytes 6193156
  424.1 44.3 %copy-start.107 = (f32[2048]{0:T(1024)S(1)}, f32[2048]{0:T(1024)}, u32[]{:S(2)}) copy-start(f32[2048]{0:T(1024)} %get-tuple-element.252) | copy-start | bytes 24580
  431.2 44.2 %copy-start.59 = (bf16[448,2048]{1,0:T(8,128)(2,1)}, bf16[448,2048]{1,0:T(8,128)(2,1)S(1)}, u32[]{:S(2)}) copy-start(bf16[448,2048]{1,0:T(8,128)(2,1)S(1)} %get-tuple-element.119) | copy-start | bytes 5505028
  555.4 14.7 %copy-start.39 = (bf16[448,1152]{1,0:T(8,128)(2,1)S(1)}, bf16[448,1152]{1,0:T(8,128)(2,1)}, u32[]{:S(2)}) copy-start(bf16[448,1152]{1,0:T(8,128)(2,1)} %copy-done.38) | copy-start | bytes 3096580
  555.4 16.3 %copy-start.8 = (bf16[1,448,1152]{2,1,0:T(8,128)(2,1)S(1)}, bf16[1,448,1152]{2,1,0:T(8,128)(2,1)}, u32[]{:S(2)}) copy-start(bf16[1,448,1152]{2,1,0:T(8,128)(2,1)} %copy-done.7) | copy-start | bytes 3096580
  749.7 3.3 collective-permute-start.2
  871.9 5.9 collective-permute-start.3
  875.3 3.4 collective-permute-start.5
  887.1 180.3 %copy-start.69 = (f32[38272]{0:T(1024)}, f32[38272]{0:T(1024)S(1)}, u32[]{:S(2)}) copy-start(f32[38272]{0:T(1024)S(1)} %get-tuple-element.233) | copy-start | bytes 459268
  1067.4 13.7 %collective-permute-start.4 = (f32[72,4736]{1,0:T(8,128)}, f32[72,4736]{1,0:T(8,128)}, u32[]{:S(2)}, u32[]{:S(2)}) collective-permute-start(f32[72,4736]{1,0:T(8,128)} %constant_dynamic-slice_fusion.1), channel_id=1, source_target_pairs={{0,2},{2,0},{4,6},{6,4},{8,10},{10,8},{12,14},{14,12},{16,18},{18,... | collective-permute-start | bytes 4091912 | tf_op jit(solution)/shard_map/ppermute | solution.py:61
  (106 other events, 655.1 us)
Sparse Core Ops, SparseCore 0:
  15.5 201.2 all-gather.7
  219.1 99.8 all-gather.13
  321.9 51.3 all-gather.9
  375.4 92.8 all-gather.11
  743.8 72.7 all-gather.15

commit v4 on v3

--- a/solution.py
+++ b/solution.py
@@ -9,6 +9,7 @@
 from jax.sharding import PartitionSpec as P
 
 MESH = pl.DeviceIdType.MESH
+GIVE_SLOTS = 3
 
 MODEL_WIDTH = 1152
 HEADS = 16
@@ -71,6 +72,9 @@
     split: bool
     way: int
     start: int
+    out: int
+    out_row: int
+    out_column: int
 
 
 def ring_place(chip, chips):
@@ -82,7 +86,7 @@
     return 2 * place + upper * (2 * (chips - 1 - place) + 1 - 2 * place)
 
 
-def reduce_body(terms, chips, lefts, rights, *refs):
+def reduce_body(terms, chips, lefts, rights, out_count, *refs):
     refs = list(refs)
 
     def take(count):
@@ -91,7 +95,7 @@
         return taken
 
     left_refs, right_refs = take(lefts), take(rights)
-    outs = take(len(terms))
+    outs = take(out_count)
     own_left, own_right = take(lefts), take(rights)
     sib_left, sib_right = take(lefts), take(rights)
     landing, final = take(len(terms)), take(len(terms))
@@ -99,6 +103,7 @@
     give, got = take(len(split_at)), take(len(split_at))
     load_sem, swap_send, swap_recv, ring_send, ring_recv = take(5)
     give_send, got_recv, final_send, final_recv = take(4)
+    stage, stage_sem, share_send, share_recv = take(4)
 
     device = lax.axis_index("fsdp")
     plane = lax.axis_index("rep")
@@ -183,7 +188,7 @@
 
     def give_copy(at, hop):
         return remote(
-            give[at].at[hop],
+            give[at].at[lax.rem(hop, GIVE_SLOTS)],
             got[at].at[hop],
             give_send.at[at, hop],
             got_recv.at[at, hop],
@@ -231,9 +236,13 @@
             term = terms[number]
             later = clock - term.start + 1
 
+            @pl.when((later >= GIVE_SLOTS) & (later < chips))
+            def _():
+                give_copy(at, later - GIVE_SLOTS).wait_send()
+
             @pl.when((later >= 0) & (later < chips))
             def _():
-                give[at][later] = chunk(term, owner_at(term, later), 1 - plane).astype(
+                give[at][lax.rem(later, GIVE_SLOTS)] = chunk(term, owner_at(term, later), 1 - plane).astype(
                     jnp.bfloat16
                 )
                 give_copy(at, later).start()
@@ -268,16 +277,61 @@
         return carry
 
     lax.fori_loop(0, max(term.start for term in terms) + chips, step, 0)
+    stores, shares = [], []
+
+    def store(term, values, from_column):
+        slot = len(stores) % 2
+        if len(stores) >= 2:
+            stores[-2]()
+        stage[slot, : term.rows, : term.columns] = values
+        columns = pl.ds(from_column, term.columns)
+        if len(left_refs[term.left].shape) == 4:
+            copy = pltpu.make_async_copy(
+                stage.at[slot, pl.ds(0, term.rows), pl.ds(0, term.columns)],
+                outs[term.out].at[0, pl.ds(term.out_row, term.rows), columns],
+                stage_sem.at[slot],
+            )
+            copy.start()
+            stores.append(copy.wait)
+            return
+        half = term.rows // 2
+
+        def rows_of(owner):
+            return stage.at[
+                slot, pl.ds(pl.multiple_of(owner * half, 8), half), pl.ds(0, term.columns)
+            ]
+
+        target = outs[term.out].at[core, :, columns]
+        copy = pltpu.make_async_copy(rows_of(core), target, stage_sem.at[slot])
+        at = len(shares)
+        share = remote(
+            rows_of(1 - core), target, share_send.at[at], share_recv.at[at], sibling
+        )
+        copy.start()
+        share.start()
+
+        def settle_store():
+            copy.wait()
+            share.wait_send()
+
+        stores.append(settle_store)
+        arrived = outs[term.out].at[1 - core, :, columns]
+        shares.append(remote(arrived, arrived, share_send.at[at], share_recv.at[at], sibling))
+
     for number, term in enumerate(terms):
         final_copy(number).wait()
         mine = landing[number][chips - 1].astype(jnp.float32)
         other = final[number][...].astype(jnp.float32)
         if term.split:
-            width = term.columns
-            outs[number][:, pl.ds(pl.multiple_of(plane * width, 128), width)] = mine
-            outs[number][:, pl.ds(pl.multiple_of((1 - plane) * width, 128), width)] = other
+            for part, values in ((plane, mine), (1 - plane, other)):
+                from_column = term.out_column + part * term.columns
+                store(term, values, pl.multiple_of(from_column, 128))
         else:
-            outs[number][...] = mine + other
+            store(term, mine + other, term.out_column)
+    for settle_store in stores[-2:]:
+        settle_store()
+    for share in shares:
+        share.wait_recv()
 
     def settle(hop, carry):
         for number in range(len(terms)):
@@ -287,7 +341,11 @@
                 ring_copy(number, hop).wait_send()
 
         for at in range(len(split_at)):
-            give_copy(at, hop).wait_send()
+
+            @pl.when(hop >= chips - GIVE_SLOTS)
+            def _():
+                give_copy(at, hop).wait_send()
+
         return carry
 
     lax.fori_loop(0, chips, settle, 0)
@@ -319,23 +377,38 @@
         [vmem(shape) for shape in left_parts + right_parts] * 2
         + [vmem((chips, term.rows, term.columns)) for term in terms]
         + [vmem((term.rows, term.columns)) for term in terms]
-        + [vmem((chips, term.rows, term.columns)) for term in splits] * 2
+        + [vmem((GIVE_SLOTS, term.rows, term.columns)) for term in splits]
+        + [vmem((chips, term.rows, term.columns)) for term in splits]
         + [pltpu.SemaphoreType.DMA((operands,))] * 3
         + [pltpu.SemaphoreType.DMA((len(terms), chips))] * 2
         + [pltpu.SemaphoreType.DMA((len(splits), chips))] * 2
         + [pltpu.SemaphoreType.DMA((len(terms),))] * 2
-    )
+        + [
+            pltpu.VMEM(
+                (2, max(term.rows for term in terms), max(term.columns for term in terms)),
+                jnp.float32,
+            ),
+            pltpu.SemaphoreType.DMA((2,)),
+        ]
+        + [pltpu.SemaphoreType.DMA((len(terms) + len(splits),))] * 2
+    )
+    heights, widths, halves = {}, {}, {}
+    for term in terms:
+        out, width = term.out, term.columns * (1 + term.split)
+        halves[out] = 1 if lefts[term.left].ndim == 4 else 2
+        heights[out] = max(heights.get(out, 0), (term.out_row + term.rows) // halves[out])
+        widths[out] = max(widths.get(out, 0), term.out_column + width)
     return pl.pallas_call(
-        partial(reduce_body, terms, chips, len(lefts), len(rights)),
+        partial(reduce_body, terms, chips, len(lefts), len(rights), len(heights)),
         out_shape=[
-            jax.ShapeDtypeStruct((term.rows, term.columns * (1 + term.split)), jnp.float32)
-            for term in terms
+            jax.ShapeDtypeStruct((halves[out], heights[out], widths[out]), jnp.float32)
+            for out in range(len(heights))
         ],
         in_specs=[pl.BlockSpec(memory_space=pl.ANY)] * operands,
-        out_specs=[pl.BlockSpec(memory_space=pltpu.VMEM)] * len(terms),
+        out_specs=[pl.BlockSpec(memory_space=pl.ANY)] * len(heights),
         scratch_shapes=scratch,
         compiler_params=pltpu.CompilerParams(
-            collective_id=identity, has_side_effects=True, vmem_limit_bytes=60 * 1024 * 1024
+            collective_id=identity, has_side_effects=True, vmem_limit_bytes=62 * 1024 * 1024
         ),
     )(*lefts, *rights)
 
@@ -546,22 +619,14 @@
     return values.T.reshape(chips, 2, -1, values.shape[0])
 
 
-def join_cores(pieces):
-    core = lax.axis_index("fsdp") % 2
-    both = jnp.concatenate([piece for piece, _ in pieces], axis=1)
-    rows = both.shape[0] // 2
-    mine = lax.dynamic_slice_in_dim(both, core * rows, rows, axis=0)
-    sent = lax.dynamic_slice_in_dim(both, (1 - core) * rows, rows, axis=0)
-    other = swap_cores(sent)
-    low = jnp.where(core == 0, mine, other)
-    high = jnp.where(core == 0, other, mine)
+def join_cores(both, columns):
     joined, at = [], 0
-    for piece, columns in pieces:
-        end = at + piece.shape[1]
-        twice = 2 * piece.shape[1] - columns
-        joined += [low[:, at:end], high[:, at + twice : end]]
+    for width in columns:
+        end = at + core_columns(width)
+        twice = 2 * core_columns(width) - width
+        joined += [both[0, :, at:end], both[1, :, at + twice : end]]
         at = end
-    return jnp.concatenate(joined, axis=1)
+    return joined
 
 
 def plain_sum(left, right):
@@ -575,97 +640,73 @@
     return 2 * rows % 16 == 0 and lax.axis_size("rep") == 2
 
 
-def sum_block_grads(
-    normed, triple_grad, attended, branch_grad, mixed, pre_grad, active, feed_grad, identity
-):
-    rows = MODEL_WIDTH // lax.axis_size("fsdp")
+def sum_grads(factors, first=None, second=None, third=None, identity=0):
+    (normed, attended, mixed, active), (triple_grad, branch_grad, pre_grad, feed_grad) = factors
+    count = lax.axis_size("fsdp")
+    rows = MODEL_WIDTH // count
+    extra = [pair for pair in (first, second, third) if pair is not None]
     if not kernels_fit(rows):
-        wide = jnp.concatenate(
-            [
-                plain_sum(normed, triple_grad),
-                plain_sum(attended, branch_grad),
-                plain_sum(mixed, pre_grad),
-            ],
-            axis=1,
-        )
-        return (wide, plain_sum(active, feed_grad))
+        wide = [
+            plain_sum(left.reshape(-1, left.shape[-1]).T, right)
+            for left, right in zip((normed, attended, mixed, active), factors[1])
+        ]
+        return (wide[:3], wide[3], [plain_sum(*pair) for pair in extra])
     triple_half = core_columns(triple_grad.shape[1])
     branch_half = core_columns(branch_grad.shape[1])
     pre_half = core_columns(pre_grad.shape[1])
     plain_part = 8 * 128
     pre_part = (pre_half - plain_part) // 2
-    deep_rows = active.shape[1] // lax.axis_size("fsdp") // 2
-    terms = (
-        Term(3, 3, deep_rows, 0, MODEL_WIDTH, 0, False, 0, 0),
-        Term(3, 3, deep_rows, deep_rows, MODEL_WIDTH, 0, False, 1, 0),
-        Term(2, 2, 2 * rows, 0, pre_part, plain_part, True, 1, 1),
-        Term(0, 0, 2 * rows, 0, triple_half // 2, 0, True, 0, 2),
-        Term(2, 2, 2 * rows, 0, plain_part, 0, False, 1, 2),
-        Term(1, 1, 2 * rows, 0, branch_half, 0, False, 0, 3),
-    )
-    deep_low, deep_high, pre_late, triple, pre_early, branch = reduce_terms(
-        terms,
-        [by_chip(normed), by_chip(attended), by_chip(mixed), by_device(active)],
-        [triple_grad, branch_grad, pre_grad, feed_grad],
-        identity,
-    )
-    wide = join_cores(
-        [
-            (triple, triple_grad.shape[1]),
-            (branch, branch_grad.shape[1]),
-            (jnp.concatenate([pre_early, pre_late], axis=1), pre_grad.shape[1]),
-        ]
-    )
-    return (wide, jnp.concatenate([deep_low, deep_high], axis=0))
-
-
-def sum_head_grads(tapped, first_grad, first, second_grad, second, projected_grad, identity):
-    count = lax.axis_size("fsdp")
-    rows, head_rows = tapped.shape[1] // count, first.shape[1] // count
-    if not kernels_fit(rows):
-        return (
-            plain_sum(tapped, first_grad),
-            jnp.concatenate(
-                [plain_sum(first, second_grad), plain_sum(second, projected_grad)], axis=1
-            ),
-        )
-    half, last = first_grad.shape[1] // 2, projected_grad.shape[1] // 2
-    terms = (
-        Term(1, 1, 2 * head_rows, 0, half // 2, 0, True, 1, 1),
-        Term(0, 0, 2 * rows, 0, half, 0, False, 0, 1),
-        Term(2, 2, 2 * head_rows, 0, last - 128, 128, False, 1, 1),
-        Term(2, 2, 2 * head_rows, 0, 128, 0, False, 0, 1),
-    )
-    second_out, first_out, third_late, third_early = reduce_terms(
-        terms,
-        [by_chip(tapped), by_chip(first), by_chip(second)],
-        [first_grad, second_grad, projected_grad],
-        identity,
-    )
-    return (
-        join_cores([(first_out, first_grad.shape[1])]),
-        join_cores(
-            [
-                (second_out, second_grad.shape[1]),
-                (jnp.concatenate([third_early, third_late], axis=1), projected_grad.shape[1]),
-            ]
-        ),
-    )
+    deep_rows = active.shape[2] // 2
+    pre_at = triple_half + branch_half
+    terms = [
+        Term(3, 3, deep_rows, 0, MODEL_WIDTH, 0, False, 0, 0, 1, 0, 0),
+        Term(3, 3, deep_rows, deep_rows, MODEL_WIDTH, 0, False, 1, 0, 1, deep_rows, 0),
+        Term(2, 2, 2 * rows, 0, pre_part, plain_part, True, 1, 1, 0, 0, pre_at + plain_part),
+        Term(0, 0, 2 * rows, 0, triple_half // 2, 0, True, 0, 2, 0, 0, 0),
+        Term(2, 2, 2 * rows, 0, plain_part, 0, False, 1, 2, 0, 0, pre_at),
+        Term(1, 1, 2 * rows, 0, branch_half, 0, False, 0, 3, 0, 0, triple_half),
+    ]
+    lefts = [normed, attended, mixed, active]
+    rights = [triple_grad, branch_grad, pre_grad, feed_grad]
+    columns = []
+    for pair, ways in ((first, "s"), (second, "ps"), (third, "p")):
+        if pair is None:
+            continue
+        at, out = len(lefts), 2 + len(columns)
+        lefts.append(by_chip(pair[0]))
+        rights.append(pair[1])
+        height, half = lefts[-1].shape[1], core_columns(pair[1].shape[1])
+        if ways == "s":
+            terms.append(Term(at, at, height, 0, half // 2, 0, True, 0, 1, out, 0, 0))
+        elif ways == "p":
+            terms.append(Term(at, at, height, 0, half, 0, False, 1, 1, out, 0, 0))
+        else:
+            half = half // 2
+            terms.append(Term(at, at, height, 0, half, 0, False, 0, 1, out, 0, 0))
+            terms.append(Term(at, at, height, 0, half // 2, half, True, 1, 1, out, 0, half))
+        columns.append(pair[1].shape[1])
+    outs = reduce_terms(tuple(terms), lefts, rights, identity)
+    wide = join_cores(outs[0], [triple_grad.shape[1], branch_grad.shape[1], pre_grad.shape[1]])
+    rest = [
+        jnp.concatenate(join_cores(out, [width]), axis=1)
+        for out, width in zip(outs[2:], columns)
+    ]
+    return (wide, outs[1][0], rest)
 
 
 def pack_body(*refs):
     out, at = refs[-1], 0
     for ref in refs[:-1]:
         width = ref.shape[1]
-        out[:, at : at + width] = ref[...].astype(jnp.float32)
+        out[:, at : at + width] = ref[...].astype(jnp.bfloat16).astype(out.dtype)
         at += width
 
 
-def pack_rows(pieces):
+def pack_rows(pieces, dtype):
     rows = pieces[0].shape[0]
     width = sum(piece.shape[1] for piece in pieces)
     return pl.pallas_call(
-        pack_body, out_shape=jax.ShapeDtypeStruct((rows, width), jnp.float32)
+        pack_body, out_shape=jax.ShapeDtypeStruct((rows, width), dtype)
     )(*pieces)
 
 
@@ -677,14 +718,13 @@
     rest = wide_shard[:, 6 * MODEL_WIDTH :].astype(jnp.bfloat16)
     low = deep_shard.astype(jnp.bfloat16)
     rows = rest.shape[0]
-    if identity is not None and kernels_fit(rows):
+    if kernels_fit(rows):
         unit = MODEL_WIDTH
         deep_rows = low.shape[0] // 2
         pieces = (
-            Piece(0, 2 * rows, unit, 0, 0, 2 * unit, 4 * unit, unit, True, 0),
+            Piece(0, 2 * rows, unit, 0, 0, 0, 4 * unit, unit, True, 0),
             Piece(1, deep_rows, unit, 2 * deep_rows, deep_rows, 0, 0, 0, True, 1),
-            Piece(0, 2 * rows, unit, 0, 0, 0, 4 * unit, 0, False, 0),
-            Piece(0, 2 * rows, unit, 0, 0, unit, 4 * unit, 0, False, 1),
+            Piece(0, 2 * rows, unit, 0, 0, 2 * unit, 4 * unit, unit, True, 1),
         )
         whole, deep = gather_pieces(pieces, [chip_rows(rest), chip_rows(low)], identity)
     else:
@@ -696,6 +736,22 @@
         whole[:, 4 * MODEL_WIDTH :],
     )
     return (split, deep)
+
+
+def fetch_block_and(wide_shard, deep_shard, other_shard):
+    rest = jnp.concatenate(
+        [other_shard.astype(jnp.bfloat16), wide_shard[:, 6 * MODEL_WIDTH :].astype(jnp.bfloat16)],
+        axis=1,
+    )
+    whole = lax.all_gather(rest, "fsdp", axis=0, tiled=True)
+    deep = lax.all_gather(deep_shard.astype(jnp.bfloat16), "fsdp", axis=0, tiled=True)
+    at = other_shard.shape[1]
+    split = (
+        whole[:, at : at + 3 * MODEL_WIDTH],
+        whole[:, at + 3 * MODEL_WIDTH : at + 4 * MODEL_WIDTH],
+        whole[:, at + 4 * MODEL_WIDTH :],
+    )
+    return (split, deep, whole[:, :at])
 
 
 def plane_modulation(silu_low, wide_weight, block_bias):
@@ -922,7 +978,7 @@
         split_modulation(modulation)
     )
     feedforward_gradient = (upstream * gate_second).astype(jnp.bfloat16)
-    gate_second_grad = jnp.sum(upstream * feed_out, axis=1)
+    gate_second_grad = jnp.sum(upstream * feed_out, axis=1, keepdims=True)
     activation_gradient = jnp.einsum(
         "xjn,mn->xjm", feedforward_gradient, deep_matrix, preferred_element_type=jnp.float32
     )
@@ -938,7 +994,7 @@
     second_back = jax.vjp(modulate, middle, offset_second, factor_second)[1]
     middle_part, offset_second_grad, factor_second_grad = second_back(mixed_grad)
     middle_grad = upstream + middle_part
-    gate_first_grad = jnp.sum(middle_grad * branch, axis=1)
+    gate_first_grad = jnp.sum(middle_grad * branch, axis=1, keepdims=True)
     branch_gradient = (middle_grad * gate_first).astype(jnp.bfloat16)
     attended_grad = jnp.einsum(
         "tbr,ar->tba",
@@ -957,11 +1013,11 @@
     hidden_part, offset_first_grad, factor_first_grad = first_back(normed_grad)
     hidden_grad = middle_grad + hidden_part
     def column_sum(values):
-        return jnp.sum(values, axis=(0, 1), dtype=jnp.float32)[None]
+        return jnp.sum(values, axis=(0, 1), dtype=jnp.float32, keepdims=True)[0]
 
     triple_sum = column_sum(triple_gradient)
     row_pieces = [
-        piece.reshape(1, -1).astype(jnp.bfloat16)
+        piece.reshape(1, -1)
         for piece in (
             offset_first_grad,
             factor_first_grad,
@@ -981,19 +1037,18 @@
     def flat(values):
         return values.reshape(-1, values.shape[-1])
 
-    factors = [
+    entering = [by_chip(flat(values)) for values in (normed_low, attended_low, mixed_low)]
+    entering.append(by_device(flat(active_low)))
+    returning = [
         flat(values)
         for values in (
-            normed_low,
             triple_gradient,
-            attended_low,
             branch_gradient,
-            mixed_low,
             preactivation_gradient,
-            active_low,
             feedforward_gradient,
         )
     ]
+    factors = (entering, returning)
     return (hidden_grad, row_pieces, factors)
 
 
@@ -1040,11 +1095,10 @@
     tapped, saved_early = block_forward(
         hidden, modulation_early, wide_early, deep_early, block_bias[0], lengths
     )
-    wide_late, deep_late = fetch_block(wide_weight[1], deep_weight[1], None)
-    first_matrix, second_w = (
-        lax.all_gather(head_first.astype(jnp.bfloat16), "fsdp", axis=0, tiled=True),
-        lax.all_gather(head_second.astype(jnp.bfloat16), "fsdp", axis=0, tiled=True),
-    )
+    wide_late, deep_late, first_matrix = fetch_block_and(
+        wide_weight[1], deep_weight[1], head_first
+    )
+    second_w = lax.all_gather(head_second.astype(jnp.bfloat16), "fsdp", axis=0, tiled=True)
     final, saved_late = block_forward(
         tapped, modulation_late, wide_late, deep_late, block_bias[1], lengths
     )
@@ -1061,8 +1115,8 @@
     late_input_grad, late_row, late_factors = block_backward(
         upstream, saved_late, wide_late, deep_late, lengths
     )
-    tapped_low, late_input_grad = lax.optimization_barrier(
-        (tapped.astype(jnp.bfloat16), late_input_grad)
+    tapped_low, late_input_grad, late_factors = lax.optimization_barrier(
+        (tapped.astype(jnp.bfloat16), late_input_grad, late_factors)
     )
     first_pre = (
         jnp.dot(tapped_low, first_matrix, preferred_element_type=jnp.float32) + head_bias[:PH]
@@ -1093,48 +1147,50 @@
     )
 
     def column_sum(values):
-        return jnp.sum(values, axis=(0, 1), dtype=jnp.float32)[None]
+        return jnp.sum(values, axis=(0, 1), dtype=jnp.float32, keepdims=True)[0]
 
     def flat(values):
         return values.reshape(-1, values.shape[-1])
 
+    late_packed = pack_rows(
+        [silu_low]
+        + late_row
+        + [column_sum(first_gradient), column_sum(second_grad), column_sum(projected_grad)],
+        jnp.bfloat16,
+    )
+    late_packed, late_input_grad = lax.optimization_barrier((late_packed, late_input_grad))
+    late_rows = gathered_terms(late_packed)
     input_grad, early_row, early_factors = block_backward(
         late_input_grad + tapped_gradient, saved_early, wide_early, deep_early, lengths
     )
-    row = pack_rows(
-        [silu_low]
-        + early_row
-        + late_row
-        + [column_sum(first_gradient), column_sum(second_grad), column_sum(projected_grad)]
-    )
-    row, early_factors, late_factors, first_gradient = lax.optimization_barrier(
-        (row, early_factors, late_factors, first_gradient)
-    )
-    rows = gathered_terms(row)
-    late_grads = sum_block_grads(*late_factors, 0)
-    head_factors = (
-        flat(tapped_low),
-        flat(first_gradient),
-        flat(first_low),
-        flat(second_grad),
-        flat(second_low),
-        flat(projected_grad),
-    )
-    late_grads, head_factors = lax.optimization_barrier((late_grads, head_factors))
-    first_weight_grad, second_weight_grad = sum_head_grads(*head_factors, 1)
-    rows, early_factors, first_weight_grad = lax.optimization_barrier(
-        (rows, early_factors, first_weight_grad)
-    )
-    early_grads = sum_block_grads(*early_factors, 2)
+    early_packed = pack_rows(early_row, jnp.float32)
+    first_pair = [flat(tapped_low), flat(first_gradient)]
+    second_pair = [flat(first_low), flat(second_grad)]
+    third_pair = [flat(second_low), flat(projected_grad)]
+    early_packed, late_rows, early_factors, late_factors, second_pair = (
+        lax.optimization_barrier(
+            (early_packed, late_rows, early_factors, late_factors, second_pair)
+        )
+    )
+    early_rows = gathered_terms(early_packed)
+    late_wide_grad, late_deep_grad, (first_weight_grad, third_weight_grad) = sum_grads(
+        late_factors, first=first_pair, third=third_pair, identity=0
+    )
+    early_rows, early_factors, late_deep_grad = lax.optimization_barrier(
+        (early_rows, early_factors, late_deep_grad)
+    )
+    early_wide_grad, early_deep_grad, (second_weight_grad,) = sum_grads(
+        early_factors, second=second_pair, identity=1
+    )
+    second_weight_grad = jnp.concatenate([second_weight_grad, third_weight_grad], axis=1)
     own_silu = lax.dynamic_slice_in_dim(
-        rows,
+        late_rows,
         lax.axis_index("fsdp") * wide_weight.shape[1],
         wide_weight.shape[1],
         axis=1,
-    ).astype(jnp.bfloat16)
+    )
+    late_rows = late_rows[:, MODEL_WIDTH:]
     bias_width = block_bias.shape[1]
-    early_rows = rows[:, MODEL_WIDTH : MODEL_WIDTH + bias_width]
-    late_rows = rows[:, MODEL_WIDTH + bias_width : MODEL_WIDTH + 2 * bias_width]
 
     def modulation_weight_grad(rows):
         return lax.dot_general(
@@ -1147,19 +1203,20 @@
     wide_grad = jnp.stack(
         [
             jnp.concatenate(
-                [modulation_weight_grad(early_rows), early_grads[0]],
+                [modulation_weight_grad(early_rows)] + early_wide_grad,
                 axis=1,
             ),
             jnp.concatenate(
-                [modulation_weight_grad(late_rows), late_grads[0]],
+                [modulation_weight_grad(late_rows)] + late_wide_grad,
                 axis=1,
             ),
         ]
     )
-    deep_grad = jnp.stack([early_grads[1], late_grads[1]])
-    row_sum = jnp.sum(rows, axis=0)[MODEL_WIDTH:]
-    block_bias_grad = row_sum[: 2 * bias_width].reshape(2, bias_width)
-    head_bias_total = row_sum[2 * bias_width :]
+    deep_grad = jnp.stack([early_deep_grad, late_deep_grad])
+    late_sum = jnp.sum(late_rows, axis=0, dtype=jnp.float32)
+    early_sum = jnp.sum(early_rows, axis=0, dtype=jnp.float32)
+    block_bias_grad = jnp.stack([early_sum, late_sum[:bias_width]])
+    head_bias_total = late_sum[bias_width:]
     wide_m, wide_v, wide_new = adam_update(
         wide_weight, wide_grad, wide_mean, wide_square, matrix_rate, matrix_decay
     )

time: 1130 us -> 1050 us (0.929)
  Pallas kernels: 683 us -> 627 us
  waiting for transfers between devices: 38.3 us -> 19.6 us
    all_gather x1, waiting for transfers between devices: 37.2 us -> 2.39 us  [per_device(): lax.all_gather(head_second.astype(jnp.bfloat16), 'fsdp', axis=0, tiled=True)]
    pallas_call x1, Pallas kernels: 213 us -> 184 us  [gather_pieces(): pl.pallas_call(partial(gather_body, pieces, chips, len(sources)), out_sha...]
    pallas_call x3 -> x2, Pallas kernels: 426 us -> 399 us  [reduce_terms(): pl.pallas_call(partial(reduce_body, terms, chips, len(lefts), len(rights)...]
    transpose x2 -> x0, local copies, waits for them, and re-layouts: 13 us -> none  [by_device(): return values.T.reshape(chips, 2, -1, values.shape[0])]
    unnamed x251 -> x194, local copies, waits for them, and re-layouts: 34.8 us -> 28.1 us
  transfers between devices with their start and end apart: 13 -> 9, of which waited for: 2 -> 3; matrix products, arithmetic and copies ran while one was open for 17% -> 22% of each run, Pallas kernels for 31% -> 41%
where the time goes in v4:
time: 1050 us; the launch traced here: 1040 us
  Pallas kernels  627 us (60%)
  matrix products  196 us (19%)
  local copies, waits for them, and re-layouts  89.4 us (9%)
  other arithmetic  74.6 us (7%)
  waiting for transfers between devices  19.6 us (2%)
  between operations  16.2 us (2%)
  starting transfers between devices  14.6 us (1%)
    pallas_call x2, Pallas kernels, reduce_terms(): pl.pallas_call(partial(reduce_body, terms, chips, len(lefts), len(rights)...  399 us
    pallas_call x1, Pallas kernels, gather_pieces(): pl.pallas_call(partial(gather_body, pieces, chips, len(sources)), out_sha...  184 us
    sub x6, other arithmetic, adam_update(): weight - rate * (first_hat / (jnp.sqrt(second_hat) + adam_epsilon) + deca...  41.2 us
    unnamed x194, local copies, waits for them, and re-layouts  28.1 us
    pallas_call x2, Pallas kernels, attention_backward(): pl.pallas_call(attend_back_body, grid=(sequences,), out_shape=jax.ShapeDt...  27.2 us
    dot_general x2, matrix products, block_backward(): jnp.einsum('xjn,mn->xjm', feedforward_gradient, deep_matrix, preferred_el...  26.7 us
    dot_general x2, matrix products, block_forward(): jnp.dot(active_low, deep_matrix, preferred_element_type=jnp.float32)  26.6 us
    dot_general x2, matrix products, block_forward(): jnp.dot(mixed_low, wide_matrix[2], preferred_element_type=jnp.float32)  24.7 us
  transfers between devices with their start and end apart: 9, of which 3 were waited for; matrix products, arithmetic and copies ran while one was open for 22% of the time, Pallas kernels for 41%

profile of v4, /device:TPU:0, one launch (start us, length us, event | category | flops | bytes accessed | tf_op | source)
XLA Modules:
  0.0 1037.7 jit_solution(6601172514729495097)
XLA Ops:
  20.3 7.4 all-to-all-start
  53.5 183.6 %shard_map.422 = (bf16[1152,9216]{1,0:T(8,128)(2,1)}, bf16[4608,1152]{1,0:T(8,128)(2,1)}) custom-call(bf16[144,9216]{1,0:T(8,128)(2,1)} %maximum_select_fusion.refs_0_, bf16[576,1152]{1,0:T(8,128)(2,1)} %maximum_select_fusion.1.refs_1_), custom_call_target="tpu_custom_call" | custom-call | tf_op jit(solution)/shard_map/pallas_call | solution.py:588
  238.2 8.5 fusion.67.triple_ref
  259.1 12.1 %fusion.42 = (bf16[4608,448]{0,1:T(8,128)(2,1)}, f32[448,4608]{1,0:T(8,128)S(1)}) fusion(f32[4608]{0:T(1024)S(1)} %get-tuple-element.165, bf16[1152,9216]{1,0:T(8,128)(2,1)} %get-tuple-element.81, f32[448,1152]{1,0:T(8,128)S(1)} %get-tuple-element.222, f32[1152]{0:T(1024)S(1)} %get-tuple-element.173, f32[1152]{0:T(1024)S(1)} %get-tuple-element.174, ...), kind=kOutput, calls=%fused_computation.54 | convolution fusion | flops 4779565056 | bytes 25098752 | tf_op jit(solution)/shard_map/dot_general | solution.py:935
  271.3 13.2 %fusion.99 = f32[448,1152]{1,0:T(8,128)S(1)} fusion(bf16[4608,1152]{1,0:T(8,128)(2,1)} %get-tuple-element.83, f32[448,4608]{1,0:T(8,128)S(1)} %get-tuple-element.273, f32[1152]{0:T(1024)S(1)} %get-tuple-element.160), kind=kOutput, calls=%fused_computation.116 | convolution fusion | flops 4775436288 | bytes 20943360 | tf_op jit(solution)/shard_map/dot_general | solution.py:940
  295.9 8.4 fusion.70.triple_ref
  317.8 12.6 %fusion.34 = (bf16[4608,448]{0,1:T(8,128)(2,1)}, f32[448,4608]{1,0:T(8,128)}) fusion(f32[4608]{0:T(1024)S(1)} %get-tuple-element.164, bf16[1152,11264]{1,0:T(8,128)(2,1)} %all-gather.9.cloned.1.call-done, f32[448,1152]{1,0:T(8,128)S(1)} %get-tuple-element.220, f32[1152]{0:T(1024)S(1)} %get-tuple-element.167, f32[1152]{0:T(1024)S(1)} %get-tuple-element.168, ...), kind=kOutput, calls=%fused_computation.46 | convolution fusion | flops 4779565056 | bytes 25098752 | tf_op jit(solution)/shard_map/dot_general | solution.py:935
  330.4 9.3 all-gather.13.cloned.1.call-done
  339.7 13.3 %convert_reduce_fusion.1 = (f32[4608]{0:T(1024)S(1)}, bf16[448,4608]{1,0:T(8,128)(2,1)S(1)}) fusion(f32[448,4608]{1,0:T(8,128)} %get-tuple-element.261, bf16[448,1152]{1,0:T(8,128)(2,1)S(1)} %copy-done.22, bf16[1,4608,1152]{2,1,0:T(8,128)(2,1)} %all-gather.13.cloned.1.call-done), kind=kOutput, calls=%fused_computation.56 | convolution fusion | flops 4801752576 | bytes 24053760 | tf_op jit(solution)/shard_map/xjn,mn->xjm/dot_general | solution.py:982
  353.1 11.3 %multiply_reduce_fusion.3 = (f32[1152]{0:T(1024)S(1)}, f32[448]{0:T(512)S(1)}, f32[1152]{0:T(1024)S(1)}, f32[448,1152]{1,0:T(8,128)S(1)}) fusion(f32[448,1152]{1,0:T(8,128)S(1)} %copy-done.18, f32[448]{0:T(512)S(1)} %fusion.174, f32[448]{0:T(512)S(1)} %broadcast_multiply_fusion, f32[1152]{0:T(1024)S(1)} %get-tuple-element.168, ...), kind=kOutput, calls=%fused_computation.183 | convolution fusion | flops 4760466944 | bytes 18893568 | tf_op jit(solution)/shard_map/qvm,am->qva/dot_general | solution.py:988
  369.9 13.7 %shard_map.425 = bf16[1,448,3456]{2,1,0:T(8,128)(2,1)S(1)} custom-call(s32[1]{0:T(128)} %copy.126.lengths_ref, bf16[1,448,3456]{2,1,0:T(8,128)(2,1)} %copy-done.3, f32[1,16,448]{2,1,0:T(8,128)S(1)} %get-tuple-element.85.log_ref, bf16[1,448,1152]{2,1,0:T(8,128)(2,1)S(1)} %fusion.114.upstream_ref), custom_call_target="tpu_custom_call" | custom-call | tf_op jit(solution)/shard_map/pallas_call | solution.py:886
  383.6 8.9 multiply_reduce_fusion.2
  395.6 13.4 %fusion.131 = (f32[1152]{0:T(1024)S(1)}, f32[1152]{0:T(1024)S(1)}, f32[1,448,1152]{2,1,0:T(8,128)}, bf16[448,1152]{1,0:T(8,128)(2,1)}) fusion(bf16[448,1152]{1,0:T(8,128)(2,1)S(1)} %copy-done.27, f32[448,1152]{1,0:T(8,128)S(1)} %copy-done.89, f32[448,1152]{1,0:T(8,128)S(1)} %get-tuple-element.218, f32[448]{0:T(512)S(1)} %negate_multiply_fusion.3, ...), kind=kOutput, calls=%fused_computation.164 | convolution fusion | flops 4781627392 | bytes 31282688 | tf_op jit(solution)/shard_map/dot_general | solution.py:940
  425.5 7.2 multiply_convert_fusion.5
  435.2 9.1 fusion.95
  451.2 8.0 convert_reduce_fusion.5
  467.2 13.3 %convert_reduce_fusion = (f32[4608]{0:T(1024)S(1)}, bf16[448,4608]{1,0:T(8,128)(2,1)S(1)}) fusion(f32[448,4608]{1,0:T(8,128)} %copy-done.90, bf16[448,1152]{1,0:T(8,128)(2,1)S(1)} %get-tuple-element.127.refs_8_, bf16[4608,1152]{1,0:T(8,128)(2,1)} %get-tuple-element.83), kind=kOutput, calls=%fused_computation.55 | convolution fusion | flops 4801752576 | bytes 24053760 | tf_op jit(solution)/shard_map/xjn,mn->xjm/dot_general | solution.py:982
  480.7 11.3 %multiply_reduce_fusion = (f32[1152]{0:T(1024)S(1)}, f32[448]{0:T(512)S(1)}, f32[1152]{0:T(1024)S(1)}, f32[448,1152]{1,0:T(8,128)S(1)}) fusion(f32[448,1152]{1,0:T(8,128)S(1)} %copy-done.9, f32[448]{0:T(512)S(1)} %copy-done.81, f32[448]{0:T(512)S(1)} %copy-done.77, f32[1152]{0:T(1024)S(1)} %copy-done.69, ...), kind=kOutput, calls=%fused_computation.175 | convolution fusion | flops 4760466944 | bytes 18893568 | tf_op jit(solution)/shard_map/qvm,am->qva/dot_general | solution.py:988
  500.9 13.6 %shard_map.427 = bf16[1,448,3456]{2,1,0:T(8,128)(2,1)S(1)} custom-call(s32[1]{0:T(128)} %copy.126.lengths_ref, bf16[1,448,3456]{2,1,0:T(8,128)(2,1)} %copy-done.2, f32[1,16,448]{2,1,0:T(8,128)S(1)} %get-tuple-element.89.log_ref, bf16[1,448,1152]{2,1,0:T(8,128)(2,1)S(1)} %copy-done.4), custom_call_target="tpu_custom_call" | custom-call | tf_op jit(solution)/shard_map/pallas_call | solution.py:886
  514.6 9.0 fusion.129
  548.4 7.8 all-gather.15.cloned.1.call-done
  563.5 203.9 %shard_map.429 = (f32[2,72,4736]{2,1,0:T(8,128)}, f32[1,288,1152]{2,1,0:T(8,128)}, f32[2,72,1024]{2,1,0:T(8,128)}, f32[2,128,384]{2,1,0:T(8,128)}) custom-call(bf16[8,144,448]{2,1,0:T(8,128)(2,1)} %bitcast.229, bf16[8,144,448]{2,1,0:T(8,128)(2,1)} %bitcast.230, bf16[8,144,448]{2,1,0:T(8,128)(2,1)} %bitcast.231, bf16[8,2,288,448]{3,2,1,0:T(8,128)(2,1)} %bitcast.218, ...), custom_call_target="tpu_custom_call" | custom-call | tf_op jit(solution)/shard_map/pallas_call | solution.py:401
  785.7 194.6 %shard_map.430 = (f32[2,72,4736]{2,1,0:T(8,128)}, f32[1,288,1152]{2,1,0:T(8,128)}, f32[2,128,1024]{2,1,0:T(8,128)}) custom-call(bf16[8,144,448]{2,1,0:T(8,128)(2,1)} %bitcast.232, bf16[8,144,448]{2,1,0:T(8,128)(2,1)} %bitcast.228, bf16[8,144,448]{2,1,0:T(8,128)(2,1)} %bitcast.233, bf16[8,2,288,448]{3,2,1,0:T(8,128)(2,1)} %bitcast.219, ...), custom_call_target="tpu_custom_call" | custom-call | tf_op jit(solution)/shard_map/pallas_call | solution.py:401
  991.6 28.0 %multiply_subtract_fusion = (f32[2,72,16128]{2,1,0:T(8,128)}, f32[2,72,16128]{2,1,0:T(8,128)}, f32[2,72,16128]{2,1,0:T(8,128)}, f32[2,72,16128]{2,1,0:T(8,128)}) fusion(f32[2,72,16128]{2,1,0:T(8,128)} %param.28, f32[2,72,16128]{2,1,0:T(8,128)} %param.40, f32[2,72,16128]{2,1,0:T(8,128)} %param.34, f32[1,72,16128]{2,1,0:T(8,128)} %bitcast.72, ...), kind=kLoop, calls=%fused_computation.21 | loop fusion | flops 37158912 | bytes 74317824 | tf_op jit(solution)/shard_map/sub | solution.py:1060
  (342 shorter events, 199.9 us)
Async XLA Ops:
  7.2 288.6 %all-gather.9.cloned.1.call-start = ((), (), s32[]{:S(2)}) async-start(), calls=%async_computation.2 | async-start | bytes 27574272 | tf_op jit(solution)/shard_map/all_gather | solution.py:746
  16.6 323.1 %all-gather.13.cloned.1.call-start = ((), (), s32[]{:S(2)}) async-start(), calls=%async_computation.4 | async-start | bytes 11280384 | tf_op jit(solution)/shard_map/all_gather | solution.py:747
  20.3 14.3 %all-to-all-start = ((bf16[16,1,72]{2,1,0:T(2,128)(2,1)}), bf16[16,1,72]{2,1,0:T(2,128)(2,1)S(1)}, u32[]{:S(2)}, u32[]{:S(2)}) async-start(bf16[16,1,72]{2,1,0:T(2,128)(2,1)} %squeeze_transpose_reshape.4), calls=%async_computation | async-start | bytes 16384 | tf_op jit(solution)/shard_map/all_to_all | solution.py:766
  27.7 407.4 %all-gather.11.cloned.1.call-start = ((), (), s32[]{:S(2)}) async-start(), calls=%async_computation.3 | async-start | bytes 12255232 | tf_op jit(solution)/shard_map/all_gather | solution.py:1101
  30.3 19.1 %collective-permute-start = (bf16[72,9216]{1,0:T(8,128)(2,1)}, bf16[72,9216]{1,0:T(8,128)(2,1)}, u32[]{:S(2)}, u32[]{:S(2)}) collective-permute-start(bf16[72,9216]{1,0:T(8,128)(2,1)} %slice.353), channel_id=1, source_target_pairs={{0,2},{2,0},{4,6},{6,4},{8,10},{10,8},{12,14},{14,12},{16,18},{18,... | collective-permute-start | bytes 3981320 | tf_op jit(solution)/shard_map/ppermute | solution.py:62
  30.7 15.5 %collective-permute-start.1 = (bf16[288,1152]{1,0:T(8,128)(2,1)}, bf16[288,1152]{1,0:T(8,128)(2,1)}, u32[]{:S(2)}, u32[]{:S(2)}) collective-permute-start(bf16[288,1152]{1,0:T(8,128)(2,1)} %get-tuple-element.234), channel_id=1, source_target_pairs={{0,2},{2,0},{4,6},{6,4},{8,10},{10,8},{12,14},{14,12},{16,18},{18,... | collective-permute-start | bytes 1990664 | tf_op jit(solution)/shard_map/ppermute | solution.py:62
  32.7 205.0 %copy-start.62 = (f32[448]{0:T(512)}, f32[448]{0:T(512)S(1)}, u32[]{:S(2)}) copy-start(f32[448]{0:T(512)S(1)} %broadcast_multiply_fusion.3) | copy-start | bytes 5380
  33.1 204.6 %copy-start.72 = (f32[448]{0:T(512)}, f32[448]{0:T(512)S(1)}, u32[]{:S(2)}) copy-start(f32[448]{0:T(512)S(1)} %fusion.171) | copy-start | bytes 5380
  39.4 197.8 %all-to-all-start.1 = ((f32[16,1,2,6912]{3,2,1,0:T(2,128)}), f32[16,1,2,6912]{3,2,1,0:T(2,128)S(1)}, u32[]{:S(2)}, u32[]{:S(2)}) async-start(f32[16,1,2,6912]{3,2,1,0:T(2,128)} %copy.85), calls=%async_computation.1 | async-start | bytes 1769472 | tf_op jit(solution)/shard_map/all_to_all | solution.py:777
  45.5 510.7 %all-gather.15.cloned.1.call-start = ((), (), s32[]{:S(2)}) async-start(), calls=%async_computation.5 | async-start | bytes 2923008 | tf_op jit(solution)/shard_map/all_gather | solution.py:714
  237.6 16.2 %copy-start.58 = (f32[1152]{0:T(1024)}, f32[1152]{0:T(1024)S(1)}, u32[]{:S(2)}) copy-start(f32[1152]{0:T(1024)S(1)} %get-tuple-element.177) | copy-start | bytes 13828
  237.7 21.4 %copy-start.66 = (f32[1152]{0:T(1024)}, f32[1152]{0:T(1024)S(1)}, u32[]{:S(2)}) copy-start(f32[1152]{0:T(1024)S(1)} %get-tuple-element.173) | copy-start | bytes 13828
  237.7 21.4 %copy-start.68 = (f32[1152]{0:T(1024)}, f32[1152]{0:T(1024)S(1)}, u32[]{:S(2)}) copy-start(f32[1152]{0:T(1024)S(1)} %get-tuple-element.174) | copy-start | bytes 13828
  237.7 46.8 %copy-start.60 = (f32[1152]{0:T(1024)}, f32[1152]{0:T(1024)S(1)}, u32[]{:S(2)}) copy-start(f32[1152]{0:T(1024)S(1)} %get-tuple-element.172) | copy-start | bytes 13828
  258.6 25.8 %copy-start.8 = (f32[448,1152]{1,0:T(8,128)}, f32[448,1152]{1,0:T(8,128)S(1)}, u32[]{:S(2)}) copy-start(f32[448,1152]{1,0:T(8,128)S(1)} %get-tuple-element.222) | copy-start | bytes 6193156
  317.8 21.9 %copy-start.22 = (bf16[448,1152]{1,0:T(8,128)(2,1)S(1)}, bf16[448,1152]{1,0:T(8,128)(2,1)}, u32[]{:S(2)}) copy-start(bf16[448,1152]{1,0:T(8,128)(2,1)} %get-tuple-element.116.refs_9_) | copy-start | bytes 3096580
  383.6 27.8 %copy-start = (bf16[1,448,3456]{2,1,0:T(8,128)(2,1)}, bf16[1,448,3456]{2,1,0:T(8,128)(2,1)S(1)}, u32[]{:S(2)}) copy-start(bf16[1,448,3456]{2,1,0:T(8,128)(2,1)S(1)} %shard_map.425) | copy-start | bytes 9289732
  499.2 282.8 %all-gather.17.cloned.1.call-start = ((), (), s32[]{:S(2)}) async-start(), calls=%async_computation.6 | async-start | bytes 2128896 | tf_op jit(solution)/shard_map/all_gather | solution.py:714
  500.9 13.6 %copy-start.11 = (bf16[448,1152]{1,0:T(8,128)(2,1)S(1)}, bf16[448,1152]{1,0:T(8,128)(2,1)}, u32[]{:S(2)}) copy-start(bf16[448,1152]{1,0:T(8,128)(2,1)} %param.23) | copy-start | bytes 3096580
  500.9 13.6 %copy-start.57 = (f32[1152]{0:T(1024)S(1)}, f32[1152]{0:T(1024)}, u32[]{:S(2)}) copy-start(f32[1152]{0:T(1024)} %copy-done.56) | copy-start | bytes 13828
  500.9 13.6 %copy-start.63 = (f32[448]{0:T(512)S(1)}, f32[448]{0:T(512)}, u32[]{:S(2)}) copy-start(f32[448]{0:T(512)} %copy-done.62) | copy-start | bytes 5380
  514.5 14.8 %copy-start.1 = (bf16[1,448,3456]{2,1,0:T(8,128)(2,1)}, bf16[1,448,3456]{2,1,0:T(8,128)(2,1)S(1)}, u32[]{:S(2)}) copy-start(bf16[1,448,3456]{2,1,0:T(8,128)(2,1)S(1)} %shard_map.427) | copy-start | bytes 9289732
  991.6 28.0 %copy-start.13 = (f32[2,288,1152]{2,1,0:T(8,128)S(1)}, f32[2,288,1152]{2,1,0:T(8,128)}, u32[]{:S(2)}) copy-start(f32[2,288,1152]{2,1,0:T(8,128)} %param.29) | copy-start | bytes 7962628
  991.6 28.0 %copy-start.34 = (f32[2,288,1152]{2,1,0:T(8,128)S(1)}, f32[2,288,1152]{2,1,0:T(8,128)}, u32[]{:S(2)}) copy-start(f32[2,288,1152]{2,1,0:T(8,128)} %param.41) | copy-start | bytes 7962628
  (77 other events, 565.4 us)
Sparse Core Ops, SparseCore 0:
  16.8 227.5 all-gather.8
  247.2 92.5 all-gather.12
  342.6 92.4 all-gather.10
  499.4 56.7 all-gather.14
  560.5 59.8 all-gather.16

commit v5 on v4

--- a/solution.py
+++ b/solution.py
@@ -427,8 +427,11 @@
 
 
 def gather_body(pieces, chips, count, *refs):
-    sources, outs = refs[:count], refs[count : 2 * count]
-    ring_send, ring_recv, pass_send, pass_recv, twin_send, twin_recv, own_sem = refs[2 * count :]
+    sources, (tiles, weights) = refs[:count], refs[count : count + 2]
+    outs, products = refs[count + 2 : 2 * count + 2], refs[2 * count + 2]
+    refs = refs[2 * count + 3 :]
+    ring_send, ring_recv, pass_send, pass_recv, twin_send, twin_recv, own_sem = refs[:7]
+    met, partial_rows, met_rows, tile_send, tile_recv, row_send, row_recv = refs[7:]
     device = lax.axis_index("fsdp")
     plane = lax.axis_index("rep")
     core, chip = lax.rem(device, 2), lax.div(device, 2)
@@ -443,7 +446,8 @@
     ways = [{"fsdp": 2 * chip_back(1 - way, 1) + core} for way in range(2)]
 
     barrier = pltpu.get_barrier_semaphore()
-    partners = (ways[0], ways[1], sibling, twin)
+    peers = [lax.rem(device + step, 2 * chips) for step in range(1, 2 * chips)]
+    partners = [{"fsdp": peer} for peer in peers] + [twin]
     for partner in partners:
         pl.semaphore_signal(barrier, inc=1, device_id=partner, device_id_type=MESH)
     pl.semaphore_wait(barrier, len(partners))
@@ -511,6 +515,15 @@
                     ways[way],
                 )
             )
+
+    def spread(target, sems, step):
+        peer = peers[step]
+        return remote(target[0].at[peer], target[1].at[step], sems, step, {"fsdp": peer})
+
+    tile_sems, row_sems = (tile_send, tile_recv), (row_send, row_recv)
+    steps = range(len(peers))
+    for step in steps:
+        send(spread((tiles, met), tile_sems, step))
 
     def ring_arrivals(hop):
         for number, piece in enumerate(pieces):
@@ -557,10 +570,25 @@
                     )
                 )
 
-    for hop in range(1, chips // 2 + 1):
+    ring_arrivals(1)
+    for step in steps:
+        spread((tiles, met), tile_sems, step).wait_recv()
+    low = jnp.concatenate([met[step, :1, :] for step in steps] + [tiles[device, :1, :]])
+    partial = jnp.dot(
+        low.astype(jnp.bfloat16), weights[...], preferred_element_type=jnp.float32
+    )
+    for step in steps:
+        sender = lax.rem(device + 2 * chips - 1 - step, 2 * chips)
+        for at in range(partial_rows.shape[1]):
+            partial_rows[sender, pl.ds(at, 1), :] = partial[
+                step : step + 1, 128 * at : 128 * (at + 1)
+            ]
+    for step in steps:
+        send(spread((partial_rows, met_rows), row_sems, step))
+
+    for hop in range(2, chips // 2 + 1):
         ring_arrivals(hop)
-        if hop > 1:
-            twin_arrivals(hop - 1)
+        twin_arrivals(hop - 1)
     twin_arrivals(chips // 2)
     for number in range(len(pieces) + len(splits)):
         at = number if number < len(pieces) else splits[number - len(pieces)]
@@ -571,16 +599,28 @@
                 remote(
                     block, block, (pass_send, pass_recv), (number, way, hop - 1), sibling
                 ).wait_recv()
+    total = jnp.concatenate(
+        [
+            partial[len(peers) :, 128 * at : 128 * (at + 1)]
+            for at in range(partial_rows.shape[1])
+        ]
+    )
+    for step in steps:
+        spread((partial_rows, met_rows), row_sems, step).wait_recv()
+        total = total + met_rows[step]
+    products[...] = total
     for copy in sent:
         copy.wait_send()
     for copy in keep:
         copy.wait()
 
 
-def gather_pieces(pieces, sources, identity):
+def gather_pieces(pieces, sources, tiles, weights, identity):
     chips = lax.axis_size("fsdp") // 2
     splits = sum(piece.split for piece in pieces)
     hops = chips // 2
+    peers = 2 * chips - 1
+    lines = weights.shape[1] // 128
 
     def sems(number):
         return [pltpu.SemaphoreType.DMA((number, 2, hops))] * 2
@@ -590,15 +630,26 @@
         out_shape=[
             jax.ShapeDtypeStruct((chips * source.shape[0], source.shape[1]), source.dtype)
             for source in sources
-        ],
-        in_specs=[pl.BlockSpec(memory_space=pl.ANY)] * len(sources),
-        out_specs=[pl.BlockSpec(memory_space=pl.ANY)] * len(sources),
+        ]
+        + [jax.ShapeDtypeStruct((lines, 128), jnp.float32)],
+        in_specs=[pl.BlockSpec(memory_space=pl.ANY)] * len(sources)
+        + [pl.BlockSpec(memory_space=pltpu.VMEM)] * 2,
+        out_specs=[pl.BlockSpec(memory_space=pl.ANY)] * len(sources)
+        + [pl.BlockSpec(memory_space=pltpu.VMEM)],
         scratch_shapes=sems(len(pieces))
         + sems(len(pieces) + splits)
         + sems(splits)
-        + [pltpu.SemaphoreType.DMA((len(sources),))],
-        compiler_params=pltpu.CompilerParams(collective_id=identity, has_side_effects=True),
-    )(*sources)
+        + [pltpu.SemaphoreType.DMA((len(sources),))]
+        + [
+            pltpu.VMEM((peers, 8, 128), jnp.float32),
+            pltpu.VMEM((2 * chips, lines, 128), jnp.float32),
+            pltpu.VMEM((peers, lines, 128), jnp.float32),
+        ]
+        + [pltpu.SemaphoreType.DMA((peers,))] * 4,
+        compiler_params=pltpu.CompilerParams(
+            collective_id=identity, has_side_effects=True, vmem_limit_bytes=32 * 1024 * 1024
+        ),
+    )(*sources, tiles, weights)
 
 
 def chip_rows(shard):
@@ -614,9 +665,9 @@
     return values.T.reshape(chips, -1, values.shape[0])
 
 
-def by_device(values):
+def by_device(turned):
     chips = lax.axis_size("fsdp") // 2
-    return values.T.reshape(chips, 2, -1, values.shape[0])
+    return turned.reshape(chips, 2, -1, turned.shape[1])
 
 
 def join_cores(both, columns):
@@ -661,10 +712,10 @@
     terms = [
         Term(3, 3, deep_rows, 0, MODEL_WIDTH, 0, False, 0, 0, 1, 0, 0),
         Term(3, 3, deep_rows, deep_rows, MODEL_WIDTH, 0, False, 1, 0, 1, deep_rows, 0),
-        Term(2, 2, 2 * rows, 0, pre_part, plain_part, True, 1, 1, 0, 0, pre_at + plain_part),
-        Term(0, 0, 2 * rows, 0, triple_half // 2, 0, True, 0, 2, 0, 0, 0),
-        Term(2, 2, 2 * rows, 0, plain_part, 0, False, 1, 2, 0, 0, pre_at),
-        Term(1, 1, 2 * rows, 0, branch_half, 0, False, 0, 3, 0, 0, triple_half),
+        Term(2, 2, 2 * rows, 0, pre_part, plain_part, True, 1, 2, 0, 0, pre_at + plain_part),
+        Term(0, 0, 2 * rows, 0, triple_half // 2, 0, True, 0, 3, 0, 0, 0),
+        Term(2, 2, 2 * rows, 0, plain_part, 0, False, 1, 4, 0, 0, pre_at),
+        Term(1, 1, 2 * rows, 0, branch_half, 0, False, 0, 5, 0, 0, triple_half),
     ]
     lefts = [normed, attended, mixed, active]
     rights = [triple_grad, branch_grad, pre_grad, feed_grad]
@@ -683,7 +734,7 @@
         else:
             half = half // 2
             terms.append(Term(at, at, height, 0, half, 0, False, 0, 1, out, 0, 0))
-            terms.append(Term(at, at, height, 0, half // 2, half, True, 1, 1, out, 0, half))
+            terms.append(Term(at, at, height, 0, half // 2, half, True, 1, 3, out, 0, half))
         columns.append(pair[1].shape[1])
     outs = reduce_terms(tuple(terms), lefts, rights, identity)
     wide = join_cores(outs[0], [triple_grad.shape[1], branch_grad.shape[1], pre_grad.shape[1]])
@@ -714,11 +765,12 @@
     return lax.all_gather(row, ("fsdp", "rep"), axis=0, tiled=True)
 
 
-def fetch_block(wide_shard, deep_shard, identity):
-    rest = wide_shard[:, 6 * MODEL_WIDTH :].astype(jnp.bfloat16)
+def fetch_first(wide_weight, deep_shard, silu_low, block_bias, identity):
+    rest = wide_weight[0, :, 6 * MODEL_WIDTH :].astype(jnp.bfloat16)
     low = deep_shard.astype(jnp.bfloat16)
     rows = rest.shape[0]
-    if kernels_fit(rows):
+    count = lax.axis_size("fsdp")
+    if kernels_fit(rows) and silu_low.shape[0] == 1 and rows <= 128:
         unit = MODEL_WIDTH
         deep_rows = low.shape[0] // 2
         pieces = (
@@ -726,32 +778,47 @@
             Piece(1, deep_rows, unit, 2 * deep_rows, deep_rows, 0, 0, 0, True, 1),
             Piece(0, 2 * rows, unit, 0, 0, 2 * unit, 4 * unit, unit, True, 1),
         )
-        whole, deep = gather_pieces(pieces, [chip_rows(rest), chip_rows(low)], identity)
+        tiles = jnp.pad(
+            silu_low.astype(jnp.float32).reshape(count, 1, rows),
+            ((0, 0), (0, 7), (0, 128 - rows)),
+        )
+        weights = jnp.concatenate(
+            [wide_weight[block, :, : 6 * unit].astype(jnp.bfloat16) for block in range(2)], axis=1
+        )
+        weights = jnp.pad(weights, ((0, 128 - rows), (0, 0)))
+        whole, deep, products = gather_pieces(
+            pieces, [chip_rows(rest), chip_rows(low)], tiles, weights, identity
+        )
+        products = products.reshape(2, 1, 6 * unit)
+        modulations = [products[block] + block_bias[block, : 6 * unit] for block in range(2)]
     else:
         whole = lax.all_gather(rest, "fsdp", axis=0, tiled=True)
         deep = lax.all_gather(low, "fsdp", axis=0, tiled=True)
+        modulations = plane_modulation(silu_low, wide_weight, block_bias)
     split = (
         whole[:, : 3 * MODEL_WIDTH],
         whole[:, 3 * MODEL_WIDTH : 4 * MODEL_WIDTH],
         whole[:, 4 * MODEL_WIDTH :],
-    )
-    return (split, deep)
+        whole,
+    )
+    return (split, deep, modulations)
 
 
 def fetch_block_and(wide_shard, deep_shard, other_shard):
     rest = jnp.concatenate(
-        [other_shard.astype(jnp.bfloat16), wide_shard[:, 6 * MODEL_WIDTH :].astype(jnp.bfloat16)],
+        [wide_shard[:, 6 * MODEL_WIDTH :].astype(jnp.bfloat16), other_shard.astype(jnp.bfloat16)],
         axis=1,
     )
     whole = lax.all_gather(rest, "fsdp", axis=0, tiled=True)
     deep = lax.all_gather(deep_shard.astype(jnp.bfloat16), "fsdp", axis=0, tiled=True)
-    at = other_shard.shape[1]
+    end = whole.shape[1] - other_shard.shape[1]
     split = (
-        whole[:, at : at + 3 * MODEL_WIDTH],
-        whole[:, at + 3 * MODEL_WIDTH : at + 4 * MODEL_WIDTH],
-        whole[:, at + 4 * MODEL_WIDTH :],
-    )
-    return (split, deep, whole[:, :at])
+        whole[:, : 3 * MODEL_WIDTH],
+        whole[:, 3 * MODEL_WIDTH : 4 * MODEL_WIDTH],
+        whole[:, 4 * MODEL_WIDTH : end],
+        whole,
+    )
+    return (split, deep, whole[:, end:])
 
 
 def plane_modulation(silu_low, wide_weight, block_bias):
@@ -899,6 +966,79 @@
     )(lengths, triple, logs, upstream)
 
 
+def rise_body(mixed_ref, weight_ref, bias_ref, pre_ref, active_ref, turned_ref):
+    pre = (
+        jnp.dot(mixed_ref[...], weight_ref[...], preferred_element_type=jnp.float32)
+        + bias_ref[...]
+    )
+    active = gelu_tanh(pre).astype(jnp.bfloat16)
+    pre_ref[...] = pre
+    active_ref[...] = active
+    turned_ref[...] = active.T
+
+
+def rise(mixed, wide, bias):
+    tokens, width = mixed.shape
+    columns = bias.shape[1]
+    tile = width
+    return pl.pallas_call(
+        rise_body,
+        grid=(columns // tile,),
+        in_specs=[
+            pl.BlockSpec((tokens, width), lambda at: (0, 0)),
+            pl.BlockSpec((width, tile), lambda at: (0, 4 + at)),
+            pl.BlockSpec((1, tile), lambda at: (0, at)),
+        ],
+        out_specs=[
+            pl.BlockSpec((tokens, tile), lambda at: (0, at)),
+            pl.BlockSpec((tokens, tile), lambda at: (0, at)),
+            pl.BlockSpec((tile, tokens), lambda at: (at, 0)),
+        ],
+        out_shape=[
+            jax.ShapeDtypeStruct((tokens, columns), jnp.float32),
+            jax.ShapeDtypeStruct((tokens, columns), jnp.bfloat16),
+            jax.ShapeDtypeStruct((columns, tokens), jnp.bfloat16),
+        ],
+        compiler_params=pltpu.CompilerParams(vmem_limit_bytes=40 * 1024 * 1024),
+    )(mixed, wide, bias)
+
+
+def fall_body(active_ref, weight_ref, bias_ref, middle_ref, gate_ref, feed_ref, result_ref):
+    @pl.when(pl.program_id(0) == 0)
+    def _():
+        feed_ref[...] = jnp.broadcast_to(bias_ref[...], feed_ref.shape)
+
+    feed_ref[...] += jnp.dot(
+        active_ref[...], weight_ref[...], preferred_element_type=jnp.float32
+    )
+
+    @pl.when(pl.program_id(0) == pl.num_programs(0) - 1)
+    def _():
+        result_ref[...] = middle_ref[...] + gate_ref[...] * feed_ref[...]
+
+
+def fall(active, weight, bias, middle, gate):
+    tokens, depth = active.shape
+    width = weight.shape[1]
+    tile = depth // 3
+    whole = pl.BlockSpec((tokens, width), lambda at: (0, 0))
+    row = pl.BlockSpec((1, width), lambda at: (0, 0))
+    return pl.pallas_call(
+        fall_body,
+        grid=(depth // tile,),
+        in_specs=[
+            pl.BlockSpec((tokens, tile), lambda at: (0, at)),
+            pl.BlockSpec((tile, width), lambda at: (at, 0)),
+            row,
+            whole,
+            row,
+        ],
+        out_specs=[whole, whole],
+        out_shape=[jax.ShapeDtypeStruct((tokens, width), jnp.float32)] * 2,
+        compiler_params=pltpu.CompilerParams(vmem_limit_bytes=40 * 1024 * 1024),
+    )(active, weight, bias, middle, gate)
+
+
 def block_forward(hidden, modulation, wide_matrix, deep_matrix, bias, lengths):
     sequences = hidden.shape[0]
     offset_first, factor_first, gate_first, offset_second, factor_second, gate_second = (
@@ -931,16 +1071,29 @@
     )
     middle = hidden + gate_first * branch
     mixed_low = modulate(middle, offset_second, factor_second).astype(jnp.bfloat16)
-    pre_active = (
-        jnp.dot(mixed_low, wide_matrix[2], preferred_element_type=jnp.float32)
-        + bias[9 * MODEL_WIDTH : 9 * MODEL_WIDTH + FF]
-    )
-    active_low = gelu_tanh(pre_active).astype(jnp.bfloat16)
-    feed_out = (
-        jnp.dot(active_low, deep_matrix, preferred_element_type=jnp.float32)
-        + bias[9 * MODEL_WIDTH + FF :]
-    )
-    result = middle + gate_second * feed_out
+    pre_bias = bias[None, 9 * MODEL_WIDTH : 9 * MODEL_WIDTH + FF]
+    feed_bias = bias[None, 9 * MODEL_WIDTH + FF :]
+    if sequences == 1:
+        pre_active, active_low, active_turned = rise(mixed_low[0], wide_matrix[3], pre_bias)
+        feed_out, result = fall(
+            active_low, deep_matrix, feed_bias, middle[0], gate_second[0]
+        )
+        pre_active, active_low, feed_out, result = (
+            pre_active[None],
+            active_low[None],
+            feed_out[None],
+            result[None],
+        )
+    else:
+        pre_active = (
+            jnp.dot(mixed_low, wide_matrix[2], preferred_element_type=jnp.float32) + pre_bias
+        )
+        active_low = gelu_tanh(pre_active).astype(jnp.bfloat16)
+        active_turned = active_low.reshape(-1, FF).T
+        feed_out = (
+            jnp.dot(active_low, deep_matrix, preferred_element_type=jnp.float32) + feed_bias
+        )
+        result = middle + gate_second * feed_out
     saved = (
         hidden,
         modulation,
@@ -952,7 +1105,7 @@
         middle,
         mixed_low,
         pre_active,
-        active_low,
+        active_turned,
         feed_out,
     )
     return (result, saved)
@@ -970,7 +1123,7 @@
         middle,
         mixed_low,
         pre_active,
-        active_low,
+        active_turned,
         feed_out,
     ) = saved
     sequences = hidden.shape[0]
@@ -1038,7 +1191,7 @@
         return values.reshape(-1, values.shape[-1])
 
     entering = [by_chip(flat(values)) for values in (normed_low, attended_low, mixed_low)]
-    entering.append(by_device(flat(active_low)))
+    entering.append(by_device(active_turned))
     returning = [
         flat(values)
         for values in (
@@ -1090,8 +1243,9 @@
     hidden = tokens.astype(jnp.float32).reshape(sequences, SEQ_LEN, MODEL_WIDTH)
     silu_low = jax.nn.silu(condition.astype(jnp.float32)).astype(jnp.bfloat16)
     visible = jnp.arange(SEQ_LEN, dtype=jnp.int32)[None, :] < lengths[:, None]
-    wide_early, deep_early = fetch_block(wide_weight[0], deep_weight[0], 3)
-    modulation_early, modulation_late = plane_modulation(silu_low, wide_weight, block_bias)
+    wide_early, deep_early, (modulation_early, modulation_late) = fetch_first(
+        wide_weight, deep_weight[0], silu_low, block_bias, 3
+    )
     tapped, saved_early = block_forward(
         hidden, modulation_early, wide_early, deep_early, block_bias[0], lengths
     )
@@ -1156,7 +1310,7 @@
         [silu_low]
         + late_row
         + [column_sum(first_gradient), column_sum(second_grad), column_sum(projected_grad)],
-        jnp.bfloat16,
+        jnp.float32,
     )
     late_packed, late_input_grad = lax.optimization_barrier((late_packed, late_input_grad))
     late_rows = gathered_terms(late_packed)
@@ -1167,10 +1321,8 @@
     first_pair = [flat(tapped_low), flat(first_gradient)]
     second_pair = [flat(first_low), flat(second_grad)]
     third_pair = [flat(second_low), flat(projected_grad)]
-    early_packed, late_rows, early_factors, late_factors, second_pair = (
-        lax.optimization_barrier(
-            (early_packed, late_rows, early_factors, late_factors, second_pair)
-        )
+    early_packed, early_factors, late_factors, second_pair = lax.optimization_barrier(
+        (early_packed, early_factors, late_factors, second_pair)
     )
     early_rows = gathered_terms(early_packed)
     late_wide_grad, late_deep_grad, (first_weight_grad, third_weight_grad) = sum_grads(
@@ -1188,7 +1340,7 @@
         lax.axis_index("fsdp") * wide_weight.shape[1],
         wide_weight.shape[1],
         axis=1,
-    )
+    ).astype(jnp.bfloat16)
     late_rows = late_rows[:, MODEL_WIDTH:]
     bias_width = block_bias.shape[1]
 

time: 1050 us -> 1020 us (0.971)
  matrix products: 196 us -> 135 us
  Pallas kernels: 627 us -> 678 us
  other arithmetic: 74.6 us -> 93.6 us
  starting transfers between devices: 14.6 us -> 0.72 us
  local copies, waits for them, and re-layouts: 89.4 us -> 78.1 us
    dot_general x6 -> x0, matrix products: 54.2 us -> none  [the longest x2 26.6 us: block_forward(): jnp.dot(active_low, deep_matrix, preferred_element_type=jnp.float32)]
    pallas_call x0 -> x4, Pallas kernels: none -> 39.7 us  [the longest x2 22.4 us: rise(): pl.pallas_call(rise_body, grid=(columns // tile,), in_specs=[pl.BlockSpec...]
    pallas_call x1, Pallas kernels: 184 us -> 198 us  [gather_pieces(): pl.pallas_call(partial(gather_body, pieces, chips, len(sources)), out_sha...]
    all_to_all x2 -> x0, starting transfers between devices: 13.5 us -> none  [the longest x1 7.36 us: plane_modulation(): met = lax.all_to_all(spread, 'fsdp', 0, 0, tiled=True)]
    unnamed x194 -> x231, local copies, waits for them, and re-layouts: 28.1 us -> 30.2 us
  transfers between devices with their start and end apart: 9 -> 7, of which waited for: 3 -> 2; matrix products, arithmetic and copies ran while one was open for 22% -> 15% of each run, Pallas kernels for 41% -> 65%
where the time goes in v5:
time: 1020 us; the launch traced here: 1010 us
  Pallas kernels  678 us (66%)
  matrix products  135 us (13%)
  other arithmetic  93.6 us (9%)
  local copies, waits for them, and re-layouts  78.1 us (8%)
  between operations  16.2 us (2%)
    pallas_call x2, Pallas kernels, reduce_terms(): pl.pallas_call(partial(reduce_body, terms, chips, len(lefts), len(rights)...  395 us
    pallas_call x1, Pallas kernels, gather_pieces(): pl.pallas_call(partial(gather_body, pieces, chips, len(sources)), out_sha...  198 us
    sub x6, other arithmetic, adam_update(): weight - rate * (first_hat / (jnp.sqrt(second_hat) + adam_epsilon) + deca...  40.2 us
    unnamed x231, local copies, waits for them, and re-layouts  30.2 us
    pallas_call x2, Pallas kernels, attention_backward(): pl.pallas_call(attend_back_body, grid=(sequences,), out_shape=jax.ShapeDt...  27.9 us
    dot_general x2, matrix products, block_backward(): jnp.einsum('qvm,am->qva', preactivation_gradient, wide_matrix[2], preferr...  22.6 us
    pallas_call x2, Pallas kernels, rise(): pl.pallas_call(rise_body, grid=(columns // tile,), in_specs=[pl.BlockSpec...  22.4 us
    dot_general x2, matrix products, block_backward(): jnp.einsum('xjn,mn->xjm', feedforward_gradient, deep_matrix, preferred_el...  21 us
  transfers between devices with their start and end apart: 7, of which 2 were waited for; matrix products, arithmetic and copies ran while one was open for 15% of the time, Pallas kernels for 65%

profile of v5, /device:TPU:0, one launch (start us, length us, event | category | flops | bytes accessed | tf_op | source)
XLA Modules:
  0.0 1011.0 jit_solution(6783152353536688025)
XLA Ops:
  41.4 198.3 %shard_map.422 = (bf16[1152,9216]{1,0:T(8,128)(2,1)}, bf16[4608,1152]{1,0:T(8,128)(2,1)S(1)}, f32[108,128]{1,0:T(8,128)S(1)}) custom-call(bf16[144,9216]{1,0:T(8,128)(2,1)S(1)} %maximum_select_fusion.refs_0_, bf16[576,1152]{1,0:T(8,128)(2,1)S(1)} %maximum_select_fusion.1.refs_1_, f32[16,8,128]{2,1,0:T(8,128)S(1)} %copy-done.19, ...), custom_call_target="tpu_custom_call" | custom-call | tf_op jit(solution)/shard_map/pallas_call | solution.py:628
  245.2 8.4 fusion.37.triple_ref
  253.6 7.1 shard_map.423
  266.3 11.1 %shard_map.424 = (f32[448,4608]{1,0:T(8,128)}, bf16[448,4608]{1,0:T(8,128)(2,1)S(1)}, bf16[4608,448]{1,0:T(8,128)(2,1)S(1)}) custom-call(bf16[448,1152]{1,0:T(8,128)(2,1)S(1)} %add_convert_fusion.4.mixed_ref, bf16[1152,9216]{1,0:T(8,128)(2,1)} %get-tuple-element.92.weight_ref, f32[1,4608]{1,0:T(1,128)S(1)} %copy-done.21), custom_call_target="tpu_custom_call" | custom-call | tf_op jit(solution)/shard_map/pallas_call | solution.py:984
  279.7 8.4 shard_map.425
  299.9 8.7 fusion.40.triple_ref
  308.6 7.1 shard_map.426
  321.3 11.3 %shard_map.427 = (f32[448,4608]{1,0:T(8,128)}, bf16[448,4608]{1,0:T(8,128)(2,1)S(1)}, bf16[4608,448]{1,0:T(8,128)(2,1)S(1)}) custom-call(bf16[448,1152]{1,0:T(8,128)(2,1)S(1)} %add_convert_fusion.2.mixed_ref, bf16[1152,11264]{1,0:T(8,128)(2,1)} %all-gather.9.cloned.1.call-done.weight_ref, f32[1,4608]{1,0:T(1,128)S(1)} %copy-done.20), custom_call_target="tpu_custom_call" | custom-call | tf_op jit(solution)/shard_map/pallas_call | solution.py:984
  339.5 13.2 %convert_reduce_fusion.1 = (f32[4608]{0:T(1024)S(1)}, bf16[448,4608]{1,0:T(8,128)(2,1)S(1)}) fusion(f32[448,4608]{1,0:T(8,128)} %get-tuple-element.101, bf16[448,1152]{1,0:T(8,128)(2,1)} %get-tuple-element.136.refs_9_, bf16[1,4608,1152]{2,1,0:T(8,128)(2,1)} %all-gather.13.cloned.1.call-done), kind=kOutput, calls=%fused_computation.30 | convolution fusion | flops 4801752576 | bytes 24053760 | tf_op jit(solution)/shard_map/xjn,mn->xjm/dot_general | solution.py:1135
  352.7 11.3 %multiply_reduce_fusion.3 = (f32[1152]{0:T(1024)S(1)}, f32[448]{0:T(512)S(1)}, f32[1152]{0:T(1024)S(1)}, f32[448,1152]{1,0:T(8,128)S(1)}) fusion(f32[448,1152]{1,0:T(8,128)S(1)} %get-tuple-element.234.middle_ref, f32[448]{0:T(512)S(1)} %fusion.129, f32[448]{0:T(512)S(1)} %broadcast_multiply_fusion, f32[1152]{0:T(1024)S(1)} %get-tuple-element.190, ...), kind=kOutput, calls=%fused_computation.144 | convolution fusion | flops 4760466944 | bytes 18893568 | tf_op jit(solution)/shard_map/qvm,am->qva/dot_general | solution.py:1141
  369.7 13.9 %shard_map.429 = bf16[1,448,3456]{2,1,0:T(8,128)(2,1)S(1)} custom-call(s32[1]{0:T(128)} %copy.105.lengths_ref, bf16[1,448,3456]{2,1,0:T(8,128)(2,1)} %copy-done.9, f32[1,16,448]{2,1,0:T(8,128)S(1)} %get-tuple-element.100.log_ref, bf16[1,448,1152]{2,1,0:T(8,128)(2,1)S(1)} %fusion.72.upstream_ref), custom_call_target="tpu_custom_call" | custom-call | tf_op jit(solution)/shard_map/pallas_call | solution.py:953
  383.6 9.0 multiply_reduce_fusion.2
  393.7 8.9 shard_map.428
  421.4 7.2 multiply_convert_fusion.1
  434.9 9.2 fusion.56
  451.2 8.8 convert_reduce_fusion.5
  468.2 7.8 fusion.163
  476.0 9.5 convert_reduce_fusion
  485.5 11.3 %multiply_reduce_fusion = (f32[1152]{0:T(1024)S(1)}, f32[448]{0:T(512)S(1)}, f32[1152]{0:T(1024)S(1)}, f32[448,1152]{1,0:T(8,128)S(1)}) fusion(f32[448,1152]{1,0:T(8,128)S(1)} %copy-done.1, f32[448]{0:T(512)S(1)} %copy-done.80, f32[448]{0:T(512)S(1)} %copy-done.76, f32[1152]{0:T(1024)S(1)} %copy-done.67, ...), kind=kOutput, calls=%fused_computation.136 | convolution fusion | flops 4760466944 | bytes 18893568 | tf_op jit(solution)/shard_map/qvm,am->qva/dot_general | solution.py:1141
  503.6 14.0 %shard_map.431 = bf16[1,448,3456]{2,1,0:T(8,128)(2,1)S(1)} custom-call(s32[1]{0:T(128)} %copy.105.lengths_ref, bf16[1,448,3456]{2,1,0:T(8,128)(2,1)} %copy-done.8, f32[1,16,448]{2,1,0:T(8,128)S(1)} %get-tuple-element.108.log_ref, bf16[1,448,1152]{2,1,0:T(8,128)(2,1)S(1)} %fusion.73.upstream_ref), custom_call_target="tpu_custom_call" | custom-call | tf_op jit(solution)/shard_map/pallas_call | solution.py:953
  517.6 8.8 fusion.87
  549.7 207.6 %shard_map.433 = (f32[2,72,4736]{2,1,0:T(8,128)}, f32[1,288,1152]{2,1,0:T(8,128)}, f32[2,72,1024]{2,1,0:T(8,128)}, f32[2,128,384]{2,1,0:T(8,128)}) custom-call(bf16[8,144,448]{2,1,0:T(8,128)(2,1)} %bitcast.216, bf16[8,144,448]{2,1,0:T(8,128)(2,1)} %bitcast.217, bf16[8,144,448]{2,1,0:T(8,128)(2,1)} %bitcast.218, bf16[8,2,288,448]{3,2,1,0:T(8,128)(2,1)} %bitcast.201, ...), custom_call_target="tpu_custom_call" | custom-call | tf_op jit(solution)/shard_map/pallas_call | solution.py:401
  768.0 187.1 %shard_map.434 = (f32[2,72,4736]{2,1,0:T(8,128)}, f32[1,288,1152]{2,1,0:T(8,128)}, f32[2,128,1024]{2,1,0:T(8,128)}) custom-call(bf16[8,144,448]{2,1,0:T(8,128)(2,1)} %bitcast.219, bf16[8,144,448]{2,1,0:T(8,128)(2,1)} %bitcast.214, bf16[8,144,448]{2,1,0:T(8,128)(2,1)} %bitcast.215, bf16[8,2,288,448]{3,2,1,0:T(8,128)(2,1)} %bitcast.202, ...), custom_call_target="tpu_custom_call" | custom-call | tf_op jit(solution)/shard_map/pallas_call | solution.py:401
  977.5 25.4 %multiply_subtract_fusion = (f32[2,72,16128]{2,1,0:T(8,128)}, f32[2,72,16128]{2,1,0:T(8,128)}, f32[2,72,16128]{2,1,0:T(8,128)}, f32[2,72,16128]{2,1,0:T(8,128)}) fusion(f32[2,72,16128]{2,1,0:T(8,128)} %param.28, f32[2,72,16128]{2,1,0:T(8,128)} %param.40, f32[2,72,16128]{2,1,0:T(8,128)} %param.34, f32[1,72,16128]{2,1,0:T(8,128)} %bitcast.211, ...), kind=kLoop, calls=%fused_computation.11 | loop fusion | flops 37158912 | bytes 74317824 | tf_op jit(solution)/shard_map/sub | solution.py:1213
  (380 shorter events, 181.4 us)
Async XLA Ops:
  7.2 292.7 %all-gather.9.cloned.1.call-start = ((), (), s32[]{:S(2)}) async-start(), calls=%async_computation | async-start | bytes 27574272 | tf_op jit(solution)/shard_map/all_gather | solution.py:812
  15.2 324.3 %all-gather.13.cloned.1.call-start = ((), (), s32[]{:S(2)}) async-start(), calls=%async_computation.2 | async-start | bytes 11280384 | tf_op jit(solution)/shard_map/all_gather | solution.py:813
  17.5 417.4 %all-gather.11.cloned.1.call-start = ((), (), s32[]{:S(2)}) async-start(), calls=%async_computation.1 | async-start | bytes 12255232 | tf_op jit(solution)/shard_map/all_gather | solution.py:1255
  20.1 18.2 %collective-permute-start = (bf16[72,9216]{1,0:T(8,128)(2,1)}, bf16[72,9216]{1,0:T(8,128)(2,1)}, u32[]{:S(2)}, u32[]{:S(2)}) collective-permute-start(bf16[72,9216]{1,0:T(8,128)(2,1)} %slice_bitcast_fusion.1), channel_id=1, source_target_pairs={{0,2},{2,0},{4,6},{6,4},{8,10},{10,8},{12,14},{14,12},{16,18},{18,... | collective-permute-start | bytes 3981320 | tf_op jit(solution)/shard_map/ppermute | solution.py:62
  20.5 15.6 %collective-permute-start.1 = (bf16[288,1152]{1,0:T(8,128)(2,1)}, bf16[288,1152]{1,0:T(8,128)(2,1)}, u32[]{:S(2)}, u32[]{:S(2)}) collective-permute-start(bf16[288,1152]{1,0:T(8,128)(2,1)} %get-tuple-element.246), channel_id=1, source_target_pairs={{0,2},{2,0},{4,6},{6,4},{8,10},{10,8},{12,14},{14,12},{16,18},{18,... | collective-permute-start | bytes 1990664 | tf_op jit(solution)/shard_map/ppermute | solution.py:62
  21.5 743.2 %all-gather.17.cloned.1.call-start = ((), (), s32[]{:S(2)}) async-start(), calls=%async_computation.4 | async-start | bytes 2128896 | tf_op jit(solution)/shard_map/all_gather | solution.py:765
  34.2 211.0 %copy-start.90 = (f32[448]{0:T(512)}, f32[448]{0:T(512)S(1)}, u32[]{:S(2)}) copy-start(f32[448]{0:T(512)S(1)} %fusion.126) | copy-start | bytes 5380
  41.4 203.8 %copy-start.28 = (bf16[448,1152]{1,0:T(8,128)(2,1)S(1)}, bf16[448,1152]{1,0:T(8,128)(2,1)}, u32[]{:S(2)}) copy-start(bf16[448,1152]{1,0:T(8,128)(2,1)} %param.23) | copy-start | bytes 3096580
  41.4 203.8 %copy-start.77 = (f32[448]{0:T(512)S(1)}, f32[448]{0:T(512)}, u32[]{:S(2)}) copy-start(f32[448]{0:T(512)} %broadcast_multiply_fusion.3) | copy-start | bytes 5380
  41.4 203.8 %copy-start.97 = (f32[3456]{0:T(1024)S(1)}, f32[3456]{0:T(1024)}, u32[]{:S(2)}) copy-start(f32[3456]{0:T(1024)} %get-tuple-element.277) | copy-start | bytes 41476
  245.2 15.6 %copy-start.73 = (f32[1152]{0:T(1024)}, f32[1152]{0:T(1024)S(1)}, u32[]{:S(2)}) copy-start(f32[1152]{0:T(1024)S(1)} %get-tuple-element.187) | copy-start | bytes 13828
  245.2 52.2 %copy-start.66 = (f32[1152]{0:T(1024)}, f32[1152]{0:T(1024)S(1)}, u32[]{:S(2)}) copy-start(f32[1152]{0:T(1024)S(1)} %get-tuple-element.184) | copy-start | bytes 13828
  265.5 31.9 %copy-start = (f32[448,1152]{1,0:T(8,128)}, f32[448,1152]{1,0:T(8,128)S(1)}, u32[]{:S(2)}) copy-start(f32[448,1152]{1,0:T(8,128)S(1)} %get-tuple-element.236.middle_ref) | copy-start | bytes 6193156
  265.5 31.9 %copy-start.75 = (f32[448]{0:T(512)}, f32[448]{0:T(512)S(1)}, u32[]{:S(2)}) copy-start(f32[448]{0:T(512)S(1)} %broadcast_multiply_fusion.2) | copy-start | bytes 5380
  265.9 31.5 %copy-start.79 = (f32[448]{0:T(512)}, f32[448]{0:T(512)S(1)}, u32[]{:S(2)}) copy-start(f32[448]{0:T(512)S(1)} %fusion.127) | copy-start | bytes 5380
  383.5 27.7 %copy-start.2 = (bf16[1,448,3456]{2,1,0:T(8,128)(2,1)}, bf16[1,448,3456]{2,1,0:T(8,128)(2,1)S(1)}, u32[]{:S(2)}) copy-start(bf16[1,448,3456]{2,1,0:T(8,128)(2,1)S(1)} %shard_map.429) | copy-start | bytes 9289732
  428.6 15.6 %copy-start.59 = (bf16[448,2048]{1,0:T(8,128)(2,1)}, bf16[448,2048]{1,0:T(8,128)(2,1)S(1)}, u32[]{:S(2)}) copy-start(bf16[448,2048]{1,0:T(8,128)(2,1)S(1)} %get-tuple-element.143) | copy-start | bytes 5505028
  503.5 14.0 %copy-start.30 = (bf16[448,1152]{1,0:T(8,128)(2,1)S(1)}, bf16[448,1152]{1,0:T(8,128)(2,1)}, u32[]{:S(2)}) copy-start(bf16[448,1152]{1,0:T(8,128)(2,1)} %param.23) | copy-start | bytes 3096580
  503.5 14.0 %copy-start.72 = (f32[1152]{0:T(1024)S(1)}, f32[1152]{0:T(1024)}, u32[]{:S(2)}) copy-start(f32[1152]{0:T(1024)} %copy-done.71) | copy-start | bytes 13828
  539.2 429.1 %all-gather.15.cloned.1.call-start = ((), (), s32[]{:S(2)}) async-start(), calls=%async_computation.3 | async-start | bytes 2923008 | tf_op jit(solution)/shard_map/all_gather | solution.py:765
  768.0 188.6 %copy-start.61 = (f32[128,2816]{1,0:T(8,128)S(1)}, f32[128,2816]{1,0:T(8,128)}, u32[]{:S(2)}) copy-start(f32[128,2816]{1,0:T(8,128)} %param.43) | copy-start | bytes 4325380
  977.5 25.4 %copy-start.65 = (f32[2,16128]{1,0:T(2,128)S(1)}, f32[2,16128]{1,0:T(2,128)}, u32[]{:S(2)}) copy-start(f32[2,16128]{1,0:T(2,128)} %param.32) | copy-start | bytes 387076
  977.5 25.4 %copy-start.68 = (f32[2,16128]{1,0:T(2,128)S(1)}, f32[2,16128]{1,0:T(2,128)}, u32[]{:S(2)}) copy-start(f32[2,16128]{1,0:T(2,128)} %param.44) | copy-start | bytes 387076
  977.5 25.5 %copy-start.69 = (f32[2,16128]{1,0:T(2,128)S(1)}, f32[2,16128]{1,0:T(2,128)}, u32[]{:S(2)}) copy-start(f32[2,16128]{1,0:T(2,128)} %param.38) | copy-start | bytes 387076
  (93 other events, 501.2 us)
Sparse Core Ops, SparseCore 0:
  15.3 228.4 all-gather.8
  246.6 92.8 all-gather.12
  342.4 92.4 all-gather.10
  539.3 62.2 all-gather.16
  604.9 64.3 all-gather.14

commit v6 on v5

--- a/solution.py
+++ b/solution.py
@@ -660,9 +660,9 @@
     )
 
 
-def by_chip(values):
+def by_chip(turned):
     chips = lax.axis_size("fsdp") // 2
-    return values.T.reshape(chips, -1, values.shape[0])
+    return turned.reshape(chips, -1, turned.shape[1])
 
 
 def by_device(turned):
@@ -701,7 +701,7 @@
             plain_sum(left.reshape(-1, left.shape[-1]).T, right)
             for left, right in zip((normed, attended, mixed, active), factors[1])
         ]
-        return (wide[:3], wide[3], [plain_sum(*pair) for pair in extra])
+        return (wide[:3], wide[3], [plain_sum(left.T, right) for left, right in extra])
     triple_half = core_columns(triple_grad.shape[1])
     branch_half = core_columns(branch_grad.shape[1])
     pre_half = core_columns(pre_grad.shape[1])
@@ -732,9 +732,9 @@
         elif ways == "p":
             terms.append(Term(at, at, height, 0, half, 0, False, 1, 1, out, 0, 0))
         else:
-            half = half // 2
-            terms.append(Term(at, at, height, 0, half, 0, False, 0, 1, out, 0, 0))
-            terms.append(Term(at, at, height, 0, half // 2, half, True, 1, 3, out, 0, half))
+            alike, split = half // 4, 3 * half // 8
+            terms.append(Term(at, at, height, 0, alike, 0, False, 0, 1, out, 0, 0))
+            terms.append(Term(at, at, height, 0, split, alike, True, 1, 3, out, 0, alike))
         columns.append(pair[1].shape[1])
     outs = reduce_terms(tuple(terms), lefts, rights, identity)
     wide = join_cores(outs[0], [triple_grad.shape[1], branch_grad.shape[1], pre_grad.shape[1]])
@@ -818,7 +818,7 @@
         whole[:, 4 * MODEL_WIDTH : end],
         whole,
     )
-    return (split, deep, whole[:, end:])
+    return (split, deep, whole, end)
 
 
 def plane_modulation(silu_low, wide_weight, block_bias):
@@ -966,27 +966,26 @@
     )(lengths, triple, logs, upstream)
 
 
-def rise_body(mixed_ref, weight_ref, bias_ref, pre_ref, active_ref, turned_ref):
+def rise_body(activation, low_ref, weight_ref, bias_ref, pre_ref, active_ref, turned_ref):
     pre = (
-        jnp.dot(mixed_ref[...], weight_ref[...], preferred_element_type=jnp.float32)
+        jnp.dot(low_ref[...], weight_ref[...], preferred_element_type=jnp.float32)
         + bias_ref[...]
     )
-    active = gelu_tanh(pre).astype(jnp.bfloat16)
+    active = activation(pre).astype(jnp.bfloat16)
     pre_ref[...] = pre
     active_ref[...] = active
     turned_ref[...] = active.T
 
 
-def rise(mixed, wide, bias):
-    tokens, width = mixed.shape
+def rise(activation, low, weight, bias, tile, first):
+    tokens, depth = low.shape
     columns = bias.shape[1]
-    tile = width
     return pl.pallas_call(
-        rise_body,
+        partial(rise_body, activation),
         grid=(columns // tile,),
         in_specs=[
-            pl.BlockSpec((tokens, width), lambda at: (0, 0)),
-            pl.BlockSpec((width, tile), lambda at: (0, 4 + at)),
+            pl.BlockSpec((tokens, depth), lambda at: (0, 0)),
+            pl.BlockSpec((depth, tile), lambda at: (0, first + at)),
             pl.BlockSpec((1, tile), lambda at: (0, at)),
         ],
         out_specs=[
@@ -1000,7 +999,69 @@
             jax.ShapeDtypeStruct((columns, tokens), jnp.bfloat16),
         ],
         compiler_params=pltpu.CompilerParams(vmem_limit_bytes=40 * 1024 * 1024),
-    )(mixed, wide, bias)
+    )(low, weight, bias)
+
+
+def sink_body(gradient_ref, weight_ref, pre_ref, out_ref, sum_ref):
+    active_grad = against(gradient_ref[...], weight_ref[...])
+    pre = pre_ref[...]
+    scale, cubic = 0.7978845608028654, 0.044715
+    bent = jnp.tanh(scale * (pre + cubic * pre * pre * pre))
+    slope = 0.5 * (1.0 + bent) + 0.5 * pre * (1.0 - bent * bent) * scale * (
+        1.0 + 3.0 * cubic * pre * pre
+    )
+    low = (active_grad * slope).astype(jnp.bfloat16)
+    out_ref[...] = low
+    sum_ref[...] = jnp.sum(low.astype(jnp.float32), axis=0, keepdims=True)
+
+
+def sink(gradient, weight, pre):
+    tokens, width = gradient.shape
+    depth = pre.shape[1]
+    tile = depth // 6
+    return pl.pallas_call(
+        sink_body,
+        grid=(depth // tile,),
+        in_specs=[
+            pl.BlockSpec((tokens, width), lambda at: (0, 0)),
+            pl.BlockSpec((tile, width), lambda at: (at, 0)),
+            pl.BlockSpec((tokens, tile), lambda at: (0, at)),
+        ],
+        out_specs=[
+            pl.BlockSpec((tokens, tile), lambda at: (0, at)),
+            pl.BlockSpec((1, tile), lambda at: (0, at)),
+        ],
+        out_shape=[
+            jax.ShapeDtypeStruct((tokens, depth), jnp.bfloat16),
+            jax.ShapeDtypeStruct((1, depth), jnp.float32),
+        ],
+        compiler_params=pltpu.CompilerParams(vmem_limit_bytes=40 * 1024 * 1024),
+    )(gradient, weight, pre)
+
+
+def project_body(normed_ref, weight_ref, bias_ref, triple_ref):
+    triple_ref[...] = (
+        jnp.dot(normed_ref[...], weight_ref[...], preferred_element_type=jnp.float32)
+        + bias_ref[...]
+    ).astype(jnp.bfloat16)
+
+
+def project(normed, wide, bias):
+    tokens, width = normed.shape
+    columns = bias.shape[1]
+    tile = width
+    return pl.pallas_call(
+        project_body,
+        grid=(columns // tile,),
+        in_specs=[
+            pl.BlockSpec((tokens, width), lambda at: (0, 0)),
+            pl.BlockSpec((width, tile), lambda at: (0, at)),
+            pl.BlockSpec((1, tile), lambda at: (0, at)),
+        ],
+        out_specs=pl.BlockSpec((tokens, tile), lambda at: (0, at)),
+        out_shape=jax.ShapeDtypeStruct((tokens, columns), jnp.bfloat16),
+        compiler_params=pltpu.CompilerParams(vmem_limit_bytes=32 * 1024 * 1024),
+    )(normed, wide, bias)
 
 
 def fall_body(active_ref, weight_ref, bias_ref, middle_ref, gate_ref, feed_ref, result_ref):
@@ -1052,14 +1113,12 @@
             bias[7 * MODEL_WIDTH : 8 * MODEL_WIDTH],
         ]
     )
-    triple = (
-        jnp.dot(
-            normed_low,
-            wide_matrix[0],
-            preferred_element_type=jnp.float32,
-        )
-        + triple_bias
-    ).astype(jnp.bfloat16)
+    if sequences == 1:
+        triple = project(normed_low[0], wide_matrix[3], triple_bias[None])[None]
+    else:
+        triple = (
+            jnp.dot(normed_low, wide_matrix[0], preferred_element_type=jnp.float32) + triple_bias
+        ).astype(jnp.bfloat16)
     attended_low, log_total = attention_forward(triple, lengths)
     branch = (
         jnp.dot(
@@ -1074,7 +1133,9 @@
     pre_bias = bias[None, 9 * MODEL_WIDTH : 9 * MODEL_WIDTH + FF]
     feed_bias = bias[None, 9 * MODEL_WIDTH + FF :]
     if sequences == 1:
-        pre_active, active_low, active_turned = rise(mixed_low[0], wide_matrix[3], pre_bias)
+        pre_active, active_low, active_turned = rise(
+            gelu_tanh, mixed_low[0], wide_matrix[3], pre_bias, MODEL_WIDTH, 4
+        )
         feed_out, result = fall(
             active_low, deep_matrix, feed_bias, middle[0], gate_second[0]
         )
@@ -1132,12 +1193,21 @@
     )
     feedforward_gradient = (upstream * gate_second).astype(jnp.bfloat16)
     gate_second_grad = jnp.sum(upstream * feed_out, axis=1, keepdims=True)
-    activation_gradient = jnp.einsum(
-        "xjn,mn->xjm", feedforward_gradient, deep_matrix, preferred_element_type=jnp.float32
-    )
-    preactivation_gradient = jax.vjp(gelu_tanh, pre_active)[1](activation_gradient)[0].astype(
-        jnp.bfloat16
-    )
+    if sequences == 1:
+        preactivation_gradient, pre_sum = sink(
+            feedforward_gradient[0], deep_matrix, pre_active[0]
+        )
+        preactivation_gradient = preactivation_gradient[None]
+    else:
+        activation_gradient = jnp.einsum(
+            "xjn,mn->xjm", feedforward_gradient, deep_matrix, preferred_element_type=jnp.float32
+        )
+        preactivation_gradient = jax.vjp(gelu_tanh, pre_active)[1](activation_gradient)[
+            0
+        ].astype(jnp.bfloat16)
+        pre_sum = jnp.sum(
+            preactivation_gradient, axis=(0, 1), dtype=jnp.float32, keepdims=True
+        )[0]
     mixed_grad = jnp.einsum(
         "qvm,am->qva",
         preactivation_gradient,
@@ -1183,14 +1253,14 @@
         triple_sum[:, :MODEL_WIDTH],
         triple_sum[:, 2 * MODEL_WIDTH :],
         column_sum(branch_gradient),
-        column_sum(preactivation_gradient),
+        pre_sum,
         column_sum(feedforward_gradient),
     ]
 
     def flat(values):
         return values.reshape(-1, values.shape[-1])
 
-    entering = [by_chip(flat(values)) for values in (normed_low, attended_low, mixed_low)]
+    entering = [by_chip(flat(values).T) for values in (normed_low, attended_low, mixed_low)]
     entering.append(by_device(active_turned))
     returning = [
         flat(values)
@@ -1249,9 +1319,10 @@
     tapped, saved_early = block_forward(
         hidden, modulation_early, wide_early, deep_early, block_bias[0], lengths
     )
-    wide_late, deep_late, first_matrix = fetch_block_and(
+    wide_late, deep_late, joint, first_at = fetch_block_and(
         wide_weight[1], deep_weight[1], head_first
     )
+    first_matrix = joint[:, first_at:]
     second_w = lax.all_gather(head_second.astype(jnp.bfloat16), "fsdp", axis=0, tiled=True)
     final, saved_late = block_forward(
         tapped, modulation_late, wide_late, deep_late, block_bias[1], lengths
@@ -1272,15 +1343,33 @@
     tapped_low, late_input_grad, late_factors = lax.optimization_barrier(
         (tapped.astype(jnp.bfloat16), late_input_grad, late_factors)
     )
-    first_pre = (
-        jnp.dot(tapped_low, first_matrix, preferred_element_type=jnp.float32) + head_bias[:PH]
-    )
-    first_low = jax.nn.silu(first_pre).astype(jnp.bfloat16)
-    second_pre = (
-        jnp.dot(first_low, second_w[:, :PH], preferred_element_type=jnp.float32)
-        + head_bias[PH : 2 * PH]
-    )
-    second_low = jax.nn.silu(second_pre).astype(jnp.bfloat16)
+    first_bias, second_bias = head_bias[None, :PH], head_bias[None, PH : 2 * PH]
+    if sequences == 1:
+        tile = PH // 2
+        first_pre, first_low, first_turned = rise(
+            jax.nn.silu, tapped_low[0], joint, first_bias, tile, first_at // tile
+        )
+        second_pre, second_low, second_turned = rise(
+            jax.nn.silu, first_low, second_w, second_bias, tile, 0
+        )
+        first_pre, first_low, second_pre, second_low = (
+            first_pre[None],
+            first_low[None],
+            second_pre[None],
+            second_low[None],
+        )
+    else:
+        first_pre = (
+            jnp.dot(tapped_low, first_matrix, preferred_element_type=jnp.float32) + first_bias
+        )
+        first_low = jax.nn.silu(first_pre).astype(jnp.bfloat16)
+        second_pre = (
+            jnp.dot(first_low, second_w[:, :PH], preferred_element_type=jnp.float32)
+            + second_bias
+        )
+        second_low = jax.nn.silu(second_pre).astype(jnp.bfloat16)
+        first_turned = first_low.reshape(-1, PH).T
+        second_turned = second_low.reshape(-1, PH).T
     projected = (
         jnp.dot(second_low, second_w[:, PH:], preferred_element_type=jnp.float32)
         + head_bias[2 * PH :]
@@ -1318,9 +1407,9 @@
         late_input_grad + tapped_gradient, saved_early, wide_early, deep_early, lengths
     )
     early_packed = pack_rows(early_row, jnp.float32)
-    first_pair = [flat(tapped_low), flat(first_gradient)]
-    second_pair = [flat(first_low), flat(second_grad)]
-    third_pair = [flat(second_low), flat(projected_grad)]
+    first_pair = [flat(tapped_low).T, flat(first_gradient)]
+    second_pair = [first_turned, flat(second_grad)]
+    third_pair = [second_turned, flat(projected_grad)]
     early_packed, early_factors, late_factors, second_pair = lax.optimization_barrier(
         (early_packed, early_factors, late_factors, second_pair)
     )

time: 1020 us -> 1020 us (level)
  Pallas kernels: 678 us -> 735 us
  matrix products: 135 us -> 84.7 us
  local copies, waits for them, and re-layouts: 78.1 us -> 88.8 us
    dot_general x6 -> x0, matrix products: 54.4 us -> none  [the longest x2 21 us: block_backward(): jnp.einsum('xjn,mn->xjm', feedforward_gradient, deep_matrix, preferred_el...]
    pallas_call x2 -> x8, Pallas kernels: 22.4 us -> 74.2 us  [the longest x4 34.6 us: rise(): pl.pallas_call(partial(rise_body, activation), grid=(columns // tile,), i...]
    unnamed x231 -> x221, local copies, waits for them, and re-layouts: 30.2 us -> 44.7 us
    reduce_sum x8 -> x7, other arithmetic: 14.9 us -> 4.46 us  [column_sum(): return jnp.sum(values, axis=(0, 1), dtype=jnp.float32, keepdims=True)[0]]
  transfers between devices with their start and end apart: 7 -> 7, of which waited for: 2 -> 0; matrix products, arithmetic and copies ran while one was open for 15% -> 12% of each run, Pallas kernels for 65% -> 69%
where the time goes in v6:
time: 1020 us; the launch traced here: 1010 us
  Pallas kernels  735 us (72%)
  local copies, waits for them, and re-layouts  88.8 us (9%)
  other arithmetic  84.9 us (8%)
  matrix products  84.7 us (8%)
  between operations  16.2 us (2%)
    pallas_call x2, Pallas kernels, reduce_terms(): pl.pallas_call(partial(reduce_body, terms, chips, len(lefts), len(rights)...  401 us
    pallas_call x1, Pallas kernels, gather_pieces(): pl.pallas_call(partial(gather_body, pieces, chips, len(sources)), out_sha...  199 us
    unnamed x221, local copies, waits for them, and re-layouts  44.7 us
    sub x6, other arithmetic, adam_update(): weight - rate * (first_hat / (jnp.sqrt(second_hat) + adam_epsilon) + deca...  38.6 us
    pallas_call x4, Pallas kernels, rise(): pl.pallas_call(partial(rise_body, activation), grid=(columns // tile,), i...  34.6 us
    pallas_call x2, Pallas kernels, attention_backward(): pl.pallas_call(attend_back_body, grid=(sequences,), out_shape=jax.ShapeDt...  27.5 us
    pallas_call x2, Pallas kernels, sink(): pl.pallas_call(sink_body, grid=(depth // tile,), in_specs=[pl.BlockSpec((...  24.9 us
    dot_general x2, matrix products, block_backward(): jnp.einsum('qvm,am->qva', preactivation_gradient, wide_matrix[2], preferr...  22.6 us
  transfers between devices with their start and end apart: 7, of which 0 were waited for; matrix products, arithmetic and copies ran while one was open for 12% of the time, Pallas kernels for 69%

profile of v6, /device:TPU:0, one launch (start us, length us, event | category | flops | bytes accessed | tf_op | source)
XLA Modules:
  0.0 1011.4 jit_solution(2455948158420915353)
XLA Ops:
  42.5 198.5 %shard_map.422 = (bf16[1152,9216]{1,0:T(8,128)(2,1)}, bf16[4608,1152]{1,0:T(8,128)(2,1)S(1)}, f32[108,128]{1,0:T(8,128)S(1)}) custom-call(bf16[144,9216]{1,0:T(8,128)(2,1)S(1)} %maximum_select_fusion.refs_0_, bf16[576,1152]{1,0:T(8,128)(2,1)S(1)} %maximum_select_fusion.1.refs_1_, f32[16,8,128]{2,1,0:T(8,128)S(1)} %copy-done.31, ...), custom_call_target="tpu_custom_call" | custom-call | tf_op jit(solution)/shard_map/pallas_call | solution.py:628
  246.5 7.4 shard_map.423
  254.0 7.1 shard_map.424
  267.4 11.1 %shard_map.425 = (f32[448,4608]{1,0:T(8,128)}, bf16[448,4608]{1,0:T(8,128)(2,1)S(1)}, bf16[4608,448]{1,0:T(8,128)(2,1)S(1)}) custom-call(bf16[448,1152]{1,0:T(8,128)(2,1)S(1)} %add_convert_fusion.2.low_ref, bf16[1152,9216]{1,0:T(8,128)(2,1)} %get-tuple-element.102.weight_ref, f32[1,4608]{1,0:T(1,128)S(1)} %copy-done.33), custom_call_target="tpu_custom_call" | custom-call | tf_op jit(solution)/shard_map/pallas_call | solution.py:983
  280.7 8.6 shard_map.426
  312.6 7.2 shard_map.427
  319.9 7.1 shard_map.428
  327.0 5.2 fusion.106
  333.6 11.1 %shard_map.429 = (f32[448,4608]{1,0:T(8,128)}, bf16[448,4608]{1,0:T(8,128)(2,1)S(1)}, bf16[4608,448]{1,0:T(8,128)(2,1)S(1)}) custom-call(bf16[448,1152]{1,0:T(8,128)(2,1)S(1)} %add_convert_fusion.low_ref, bf16[1152,11264]{1,0:T(8,128)(2,1)} %all-gather.9.cloned.1.call-done.weight_ref, f32[1,4608]{1,0:T(1,128)S(1)} %copy-done.32), custom_call_target="tpu_custom_call" | custom-call | tf_op jit(solution)/shard_map/pallas_call | solution.py:983
  352.2 12.6 %shard_map.431 = (bf16[448,4608]{1,0:T(8,128)(2,1)S(1)}, f32[1,4608]{1,0:T(1,128)S(1)}) custom-call(bf16[448,1152]{1,0:T(8,128)(2,1)S(1)} %get-tuple-element.156.gradient_ref.refs_9_, bf16[4608,1152]{1,0:T(8,128)(2,1)} %bitcast.186, f32[448,4608]{1,0:T(8,128)S(1)} %copy-done.15), custom_call_target="tpu_custom_call" | custom-call | tf_op jit(solution)/shard_map/pallas_call | solution.py:1022
  365.4 11.3 %multiply_reduce_fusion.3 = (f32[1152]{0:T(1024)S(1)}, f32[448]{0:T(512)S(1)}, f32[1152]{0:T(1024)S(1)}, f32[448,1152]{1,0:T(8,128)S(1)}) fusion(f32[448,1152]{1,0:T(8,128)S(1)} %copy-done.3, f32[448]{0:T(512)S(1)} %fusion.91, f32[448]{0:T(512)S(1)} %broadcast_multiply_fusion, f32[1152]{0:T(1024)S(1)} %get-tuple-element.210, ...), kind=kOutput, calls=%fused_computation.102 | convolution fusion | flops 4760466944 | bytes 18893568 | tf_op jit(solution)/shard_map/qvm,am->qva/dot_general | solution.py:1211
  383.2 13.7 %shard_map.432 = bf16[1,448,3456]{2,1,0:T(8,128)(2,1)S(1)} custom-call(s32[1]{0:T(128)} %copy.97.lengths_ref, bf16[1,448,3456]{2,1,0:T(8,128)(2,1)} %bitcast.175, f32[1,16,448]{2,1,0:T(8,128)S(1)} %get-tuple-element.110.log_ref, bf16[1,448,1152]{2,1,0:T(8,128)(2,1)S(1)} %fusion.36.upstream_ref), custom_call_target="tpu_custom_call" | custom-call | tf_op jit(solution)/shard_map/pallas_call | solution.py:953
  396.9 9.0 multiply_reduce_fusion.2
  407.1 8.4 shard_map.430
  440.2 7.2 shard_map.434
  457.4 8.2 convert_reduce_fusion.3
  467.1 6.2 fusion.25
  477.5 12.3 %shard_map.436 = (bf16[448,4608]{1,0:T(8,128)(2,1)S(1)}, f32[1,4608]{1,0:T(1,128)S(1)}) custom-call(bf16[448,1152]{1,0:T(8,128)(2,1)S(1)} %get-tuple-element.167.gradient_ref.refs_8_, bf16[4608,1152]{1,0:T(8,128)(2,1)} %copy-done.5, f32[448,4608]{1,0:T(8,128)S(1)} %copy-done.14), custom_call_target="tpu_custom_call" | custom-call | tf_op jit(solution)/shard_map/pallas_call | solution.py:1022
  490.5 11.3 %multiply_reduce_fusion = (f32[1152]{0:T(1024)S(1)}, f32[448]{0:T(512)S(1)}, f32[1152]{0:T(1024)S(1)}, f32[448,1152]{1,0:T(8,128)S(1)}) fusion(f32[448,1152]{1,0:T(8,128)S(1)} %copy-done.1, f32[448]{0:T(512)S(1)} %fusion.89, f32[448]{0:T(512)S(1)} %broadcast_multiply_fusion.2, f32[1152]{0:T(1024)S(1)} %get-tuple-element.204, ...), kind=kOutput, calls=%fused_computation.94 | convolution fusion | flops 4760466944 | bytes 18893568 | tf_op jit(solution)/shard_map/qvm,am->qva/dot_general | solution.py:1211
  508.5 13.8 %shard_map.437 = bf16[1,448,3456]{2,1,0:T(8,128)(2,1)S(1)} custom-call(s32[1]{0:T(128)} %copy.97.lengths_ref, bf16[1,448,3456]{2,1,0:T(8,128)(2,1)} %bitcast.171, f32[1,16,448]{2,1,0:T(8,128)S(1)} %get-tuple-element.125.log_ref, bf16[1,448,1152]{2,1,0:T(8,128)(2,1)S(1)} %fusion.37.upstream_ref), custom_call_target="tpu_custom_call" | custom-call | tf_op jit(solution)/shard_map/pallas_call | solution.py:953
  522.3 8.8 fusion.51
  543.4 216.9 %shard_map.439 = (f32[2,72,4736]{2,1,0:T(8,128)}, f32[1,288,1152]{2,1,0:T(8,128)}, f32[2,72,1024]{2,1,0:T(8,128)}, f32[2,128,384]{2,1,0:T(8,128)}) custom-call(bf16[8,144,448]{2,1,0:T(8,128)(2,1)} %bitcast.199, bf16[8,144,448]{2,1,0:T(8,128)(2,1)} %bitcast.200, bf16[8,144,448]{2,1,0:T(8,128)(2,1)} %bitcast.201, bf16[8,2,288,448]{3,2,1,0:T(8,128)(2,1)} %bitcast.178, ...), custom_call_target="tpu_custom_call" | custom-call | tf_op jit(solution)/shard_map/pallas_call | solution.py:401
  771.0 183.9 %shard_map.440 = (f32[2,72,4736]{2,1,0:T(8,128)}, f32[1,288,1152]{2,1,0:T(8,128)}, f32[2,128,1024]{2,1,0:T(8,128)}) custom-call(bf16[8,144,448]{2,1,0:T(8,128)(2,1)} %bitcast.196, bf16[8,144,448]{2,1,0:T(8,128)(2,1)} %bitcast.197, bf16[8,144,448]{2,1,0:T(8,128)(2,1)} %bitcast.198, bf16[8,2,288,448]{3,2,1,0:T(8,128)(2,1)} %bitcast.179, ...), custom_call_target="tpu_custom_call" | custom-call | tf_op jit(solution)/shard_map/pallas_call | solution.py:401
  977.9 25.4 %multiply_subtract_fusion = (f32[2,72,16128]{2,1,0:T(8,128)}, f32[2,72,16128]{2,1,0:T(8,128)}, f32[2,72,16128]{2,1,0:T(8,128)}, f32[2,72,16128]{2,1,0:T(8,128)}) fusion(f32[2,72,16128]{2,1,0:T(8,128)} %param.28, f32[2,72,16128]{2,1,0:T(8,128)} %param.40, f32[2,72,16128]{2,1,0:T(8,128)} %param.34, f32[1,72,16128]{2,1,0:T(8,128)} %bitcast.195, ...), kind=kLoop, calls=%fused_computation.7 | loop fusion | flops 37158912 | bytes 74317824 | tf_op jit(solution)/shard_map/sub | solution.py:1283
  (371 shorter events, 182.6 us)
Async XLA Ops:
  7.2 304.2 %all-gather.9.cloned.1.call-start = ((), (), s32[]{:S(2)}) async-start(), calls=%async_computation | async-start | bytes 27574272 | tf_op jit(solution)/shard_map/all_gather | solution.py:812
  15.0 333.8 %all-gather.13.cloned.1.call-start = ((), (), s32[]{:S(2)}) async-start(), calls=%async_computation.2 | async-start | bytes 11280384 | tf_op jit(solution)/shard_map/all_gather | solution.py:813
  17.4 422.8 %all-gather.11.cloned.1.call-start = ((), (), s32[]{:S(2)}) async-start(), calls=%async_computation.1 | async-start | bytes 12255232 | tf_op jit(solution)/shard_map/all_gather | solution.py:1326
  20.0 19.4 %collective-permute-start = (bf16[72,9216]{1,0:T(8,128)(2,1)}, bf16[72,9216]{1,0:T(8,128)(2,1)}, u32[]{:S(2)}, u32[]{:S(2)}) collective-permute-start(bf16[72,9216]{1,0:T(8,128)(2,1)} %slice_bitcast_fusion.1), channel_id=1, source_target_pairs={{0,2},{2,0},{4,6},{6,4},{8,10},{10,8},{12,14},{14,12},{16,18},{18,... | collective-permute-start | bytes 3981320 | tf_op jit(solution)/shard_map/ppermute | solution.py:62
  20.4 16.8 %collective-permute-start.1 = (bf16[288,1152]{1,0:T(8,128)(2,1)}, bf16[288,1152]{1,0:T(8,128)(2,1)}, u32[]{:S(2)}, u32[]{:S(2)}) collective-permute-start(bf16[288,1152]{1,0:T(8,128)(2,1)} %get-tuple-element.263), channel_id=1, source_target_pairs={{0,2},{2,0},{4,6},{6,4},{8,10},{10,8},{12,14},{14,12},{16,18},{18,... | collective-permute-start | bytes 1990664 | tf_op jit(solution)/shard_map/ppermute | solution.py:62
  21.5 746.2 %all-gather.17.cloned.1.call-start = ((), (), s32[]{:S(2)}) async-start(), calls=%async_computation.4 | async-start | bytes 2128896 | tf_op jit(solution)/shard_map/all_gather | solution.py:765
  35.4 210.7 %copy-start.87 = (f32[448]{0:T(512)}, f32[448]{0:T(512)S(1)}, u32[]{:S(2)}) copy-start(f32[448]{0:T(512)S(1)} %fusion.88) | copy-start | bytes 5380
  42.5 203.6 %copy-start.43 = (bf16[448,1152]{1,0:T(8,128)(2,1)S(1)}, bf16[448,1152]{1,0:T(8,128)(2,1)}, u32[]{:S(2)}) copy-start(bf16[448,1152]{1,0:T(8,128)(2,1)} %param.23) | copy-start | bytes 3096580
  42.5 203.6 %copy-start.83 = (f32[448]{0:T(512)S(1)}, f32[448]{0:T(512)}, u32[]{:S(2)}) copy-start(f32[448]{0:T(512)} %broadcast_multiply_fusion.3) | copy-start | bytes 5380
  246.0 15.1 %copy-start.85 = (f32[1152]{0:T(1024)}, f32[1152]{0:T(1024)S(1)}, u32[]{:S(2)}) copy-start(f32[1152]{0:T(1024)S(1)} %get-tuple-element.207) | copy-start | bytes 13828
  266.2 14.5 %copy-start = (f32[448,1152]{1,0:T(8,128)}, f32[448,1152]{1,0:T(8,128)S(1)}, u32[]{:S(2)}) copy-start(f32[448,1152]{1,0:T(8,128)S(1)} %get-tuple-element.254.middle_ref) | copy-start | bytes 6193156
  267.4 13.3 %copy-start.37 = (f32[1,1152]{1,0:T(1,128)S(1)}, f32[1,1152]{1,0:T(1,128)}, u32[]{:S(2)}) copy-start(f32[1,1152]{1,0:T(1,128)} %get-tuple-element.271.bias_ref) | copy-start | bytes 13828
  292.4 56.4 %copy-start.10 = (bf16[448,1152]{1,0:T(8,128)(2,1)}, bf16[448,1152]{1,0:T(8,128)(2,1)S(1)}, u32[]{:S(2)}) copy-start(bf16[448,1152]{1,0:T(8,128)(2,1)S(1)} %get-tuple-element.156.gradient_ref.refs_9_) | copy-start | bytes 3096580
  352.2 13.2 %copy-start.3 = (f32[448,1152]{1,0:T(8,128)S(1)}, f32[448,1152]{1,0:T(8,128)}, u32[]{:S(2)}) copy-start(f32[448,1152]{1,0:T(8,128)} %copy-done.2) | copy-start | bytes 6193156
  396.9 26.6 %copy-start.7 = (bf16[1,448,3456]{2,1,0:T(8,128)(2,1)}, bf16[1,448,3456]{2,1,0:T(8,128)(2,1)S(1)}, u32[]{:S(2)}) copy-start(bf16[1,448,3456]{2,1,0:T(8,128)(2,1)S(1)} %shard_map.432) | copy-start | bytes 9289732
  416.8 14.3 %copy-start.12 = (bf16[1,448,1152]{2,1,0:T(8,128)(2,1)}, bf16[1,448,1152]{2,1,0:T(8,128)(2,1)S(1)}, u32[]{:S(2)}) copy-start(bf16[1,448,1152]{2,1,0:T(8,128)(2,1)S(1)} %get-tuple-element.116) | copy-start | bytes 3096580
  473.8 16.0 %copy-start.11 = (bf16[448,1152]{1,0:T(8,128)(2,1)}, bf16[448,1152]{1,0:T(8,128)(2,1)S(1)}, u32[]{:S(2)}) copy-start(bf16[448,1152]{1,0:T(8,128)(2,1)S(1)} %get-tuple-element.167.gradient_ref.refs_8_) | copy-start | bytes 3096580
  508.5 13.8 %copy-start.44 = (bf16[448,1152]{1,0:T(8,128)(2,1)S(1)}, bf16[448,1152]{1,0:T(8,128)(2,1)}, u32[]{:S(2)}) copy-start(bf16[448,1152]{1,0:T(8,128)(2,1)} %param.23) | copy-start | bytes 3096580
  539.8 428.4 %all-gather.15.cloned.1.call-start = ((), (), s32[]{:S(2)}) async-start(), calls=%async_computation.3 | async-start | bytes 2923008 | tf_op jit(solution)/shard_map/all_gather | solution.py:765
  543.4 219.4 %copy-start.77 = (f32[72,2048]{1,0:T(8,128)S(1)}, f32[72,2048]{1,0:T(8,128)}, u32[]{:S(2)}) copy-start(f32[72,2048]{1,0:T(8,128)} %param.36) | copy-start | bytes 1769476
  771.0 185.4 %copy-start.73 = (f32[128,2816]{1,0:T(8,128)S(1)}, f32[128,2816]{1,0:T(8,128)}, u32[]{:S(2)}) copy-start(f32[128,2816]{1,0:T(8,128)} %param.43) | copy-start | bytes 4325380
  977.9 25.4 %copy-start.79 = (f32[2,16128]{1,0:T(2,128)S(1)}, f32[2,16128]{1,0:T(2,128)}, u32[]{:S(2)}) copy-start(f32[2,16128]{1,0:T(2,128)} %param.32) | copy-start | bytes 387076
  977.9 25.4 %copy-start.80 = (f32[2,16128]{1,0:T(2,128)S(1)}, f32[2,16128]{1,0:T(2,128)}, u32[]{:S(2)}) copy-start(f32[2,16128]{1,0:T(2,128)} %param.44) | copy-start | bytes 387076
  977.9 25.4 %copy-start.81 = (f32[2,16128]{1,0:T(2,128)S(1)}, f32[2,16128]{1,0:T(2,128)}, u32[]{:S(2)}) copy-start(f32[2,16128]{1,0:T(2,128)} %param.38) | copy-start | bytes 387076
  (88 other events, 389.1 us)
Sparse Core Ops, SparseCore 0:
  15.1 228.4 all-gather.8
  246.5 92.8 all-gather.12
  341.6 92.4 all-gather.10
  539.9 70.7 all-gather.16
  614.0 64.1 all-gather.14

commit v7 on v6

--- a/solution.py
+++ b/solution.py
@@ -730,11 +730,12 @@
         if ways == "s":
             terms.append(Term(at, at, height, 0, half // 2, 0, True, 0, 1, out, 0, 0))
         elif ways == "p":
-            terms.append(Term(at, at, height, 0, half, 0, False, 1, 1, out, 0, 0))
+            terms.append(Term(at, at, height, 0, 128, 0, False, 0, 1, out, 0, 0))
+            terms.append(Term(at, at, height, 0, half - 128, 128, False, 1, 1, out, 0, 128))
         else:
             alike, split = half // 4, 3 * half // 8
-            terms.append(Term(at, at, height, 0, alike, 0, False, 0, 1, out, 0, 0))
-            terms.append(Term(at, at, height, 0, split, alike, True, 1, 3, out, 0, alike))
+            terms.append(Term(at, at, height, 0, alike, 0, False, 1, 1, out, 0, 0))
+            terms.append(Term(at, at, height, 0, split, alike, True, 0, 2, out, 0, alike))
         columns.append(pair[1].shape[1])
     outs = reduce_terms(tuple(terms), lefts, rights, identity)
     wide = join_cores(outs[0], [triple_grad.shape[1], branch_grad.shape[1], pre_grad.shape[1]])

time: 1020 us -> 1010 us (level)
  Pallas kernels: 735 us -> 724 us
    pallas_call x2, Pallas kernels: 401 us -> 390 us  [reduce_terms(): pl.pallas_call(partial(reduce_body, terms, chips, len(lefts), len(rights)...]
where the time goes in v7:
time: 1010 us; the launch traced here: 1000 us
  Pallas kernels  724 us (72%)
  local copies, waits for them, and re-layouts  88.8 us (9%)
  other arithmetic  84.9 us (8%)
  matrix products  84.7 us (8%)
  between operations  16.2 us (2%)
    pallas_call x2, Pallas kernels, reduce_terms(): pl.pallas_call(partial(reduce_body, terms, chips, len(lefts), len(rights)...  390 us
    pallas_call x1, Pallas kernels, gather_pieces(): pl.pallas_call(partial(gather_body, pieces, chips, len(sources)), out_sha...  199 us
    unnamed x221, local copies, waits for them, and re-layouts  44.7 us
    sub x6, other arithmetic, adam_update(): weight - rate * (first_hat / (jnp.sqrt(second_hat) + adam_epsilon) + deca...  38.6 us
    pallas_call x4, Pallas kernels, rise(): pl.pallas_call(partial(rise_body, activation), grid=(columns // tile,), i...  34.6 us
    pallas_call x2, Pallas kernels, attention_backward(): pl.pallas_call(attend_back_body, grid=(sequences,), out_shape=jax.ShapeDt...  27.5 us
    pallas_call x2, Pallas kernels, sink(): pl.pallas_call(sink_body, grid=(depth // tile,), in_specs=[pl.BlockSpec((...  24.9 us
    dot_general x2, matrix products, block_backward(): jnp.einsum('qvm,am->qva', preactivation_gradient, wide_matrix[2], preferr...  22.6 us
  transfers between devices with their start and end apart: 7, of which 0 were waited for; matrix products, arithmetic and copies ran while one was open for 12% of the time, Pallas kernels for 69%

profile of v7, /device:TPU:0, one launch (start us, length us, event | category | flops | bytes accessed | tf_op | source)
XLA Modules:
  0.0 1000.3 jit_solution(7563145530349730832)
XLA Ops:
  42.5 198.5 %shard_map.422 = (bf16[1152,9216]{1,0:T(8,128)(2,1)}, bf16[4608,1152]{1,0:T(8,128)(2,1)S(1)}, f32[108,128]{1,0:T(8,128)S(1)}) custom-call(bf16[144,9216]{1,0:T(8,128)(2,1)S(1)} %maximum_select_fusion.refs_0_, bf16[576,1152]{1,0:T(8,128)(2,1)S(1)} %maximum_select_fusion.1.refs_1_, f32[16,8,128]{2,1,0:T(8,128)S(1)} %copy-done.31, ...), custom_call_target="tpu_custom_call" | custom-call | tf_op jit(solution)/shard_map/pallas_call | solution.py:628
  246.5 7.4 shard_map.423
  254.0 7.1 shard_map.424
  267.4 11.1 %shard_map.425 = (f32[448,4608]{1,0:T(8,128)}, bf16[448,4608]{1,0:T(8,128)(2,1)S(1)}, bf16[4608,448]{1,0:T(8,128)(2,1)S(1)}) custom-call(bf16[448,1152]{1,0:T(8,128)(2,1)S(1)} %add_convert_fusion.2.low_ref, bf16[1152,9216]{1,0:T(8,128)(2,1)} %get-tuple-element.102.weight_ref, f32[1,4608]{1,0:T(1,128)S(1)} %copy-done.33), custom_call_target="tpu_custom_call" | custom-call | tf_op jit(solution)/shard_map/pallas_call | solution.py:984
  280.7 8.6 shard_map.426
  312.6 7.2 shard_map.427
  319.9 7.1 shard_map.428
  327.0 5.2 fusion.106
  333.6 11.1 %shard_map.429 = (f32[448,4608]{1,0:T(8,128)}, bf16[448,4608]{1,0:T(8,128)(2,1)S(1)}, bf16[4608,448]{1,0:T(8,128)(2,1)S(1)}) custom-call(bf16[448,1152]{1,0:T(8,128)(2,1)S(1)} %add_convert_fusion.low_ref, bf16[1152,11264]{1,0:T(8,128)(2,1)} %all-gather.9.cloned.1.call-done.weight_ref, f32[1,4608]{1,0:T(1,128)S(1)} %copy-done.32), custom_call_target="tpu_custom_call" | custom-call | tf_op jit(solution)/shard_map/pallas_call | solution.py:984
  352.2 12.6 %shard_map.431 = (bf16[448,4608]{1,0:T(8,128)(2,1)S(1)}, f32[1,4608]{1,0:T(1,128)S(1)}) custom-call(bf16[448,1152]{1,0:T(8,128)(2,1)S(1)} %get-tuple-element.156.gradient_ref.refs_9_, bf16[4608,1152]{1,0:T(8,128)(2,1)} %bitcast.186, f32[448,4608]{1,0:T(8,128)S(1)} %copy-done.15), custom_call_target="tpu_custom_call" | custom-call | tf_op jit(solution)/shard_map/pallas_call | solution.py:1023
  365.4 11.3 %multiply_reduce_fusion.3 = (f32[1152]{0:T(1024)S(1)}, f32[448]{0:T(512)S(1)}, f32[1152]{0:T(1024)S(1)}, f32[448,1152]{1,0:T(8,128)S(1)}) fusion(f32[448,1152]{1,0:T(8,128)S(1)} %copy-done.3, f32[448]{0:T(512)S(1)} %fusion.91, f32[448]{0:T(512)S(1)} %broadcast_multiply_fusion, f32[1152]{0:T(1024)S(1)} %get-tuple-element.210, ...), kind=kOutput, calls=%fused_computation.102 | convolution fusion | flops 4760466944 | bytes 18893568 | tf_op jit(solution)/shard_map/qvm,am->qva/dot_general | solution.py:1212
  383.2 13.7 %shard_map.432 = bf16[1,448,3456]{2,1,0:T(8,128)(2,1)S(1)} custom-call(s32[1]{0:T(128)} %copy.97.lengths_ref, bf16[1,448,3456]{2,1,0:T(8,128)(2,1)} %bitcast.175, f32[1,16,448]{2,1,0:T(8,128)S(1)} %get-tuple-element.110.log_ref, bf16[1,448,1152]{2,1,0:T(8,128)(2,1)S(1)} %fusion.36.upstream_ref), custom_call_target="tpu_custom_call" | custom-call | tf_op jit(solution)/shard_map/pallas_call | solution.py:954
  396.9 9.0 multiply_reduce_fusion.2
  407.1 8.4 shard_map.430
  440.2 7.2 shard_map.434
  457.4 8.2 convert_reduce_fusion.3
  467.1 6.2 fusion.25
  477.5 12.3 %shard_map.436 = (bf16[448,4608]{1,0:T(8,128)(2,1)S(1)}, f32[1,4608]{1,0:T(1,128)S(1)}) custom-call(bf16[448,1152]{1,0:T(8,128)(2,1)S(1)} %get-tuple-element.167.gradient_ref.refs_8_, bf16[4608,1152]{1,0:T(8,128)(2,1)} %copy-done.5, f32[448,4608]{1,0:T(8,128)S(1)} %copy-done.14), custom_call_target="tpu_custom_call" | custom-call | tf_op jit(solution)/shard_map/pallas_call | solution.py:1023
  490.5 11.3 %multiply_reduce_fusion = (f32[1152]{0:T(1024)S(1)}, f32[448]{0:T(512)S(1)}, f32[1152]{0:T(1024)S(1)}, f32[448,1152]{1,0:T(8,128)S(1)}) fusion(f32[448,1152]{1,0:T(8,128)S(1)} %copy-done.1, f32[448]{0:T(512)S(1)} %fusion.89, f32[448]{0:T(512)S(1)} %broadcast_multiply_fusion.2, f32[1152]{0:T(1024)S(1)} %get-tuple-element.204, ...), kind=kOutput, calls=%fused_computation.94 | convolution fusion | flops 4760466944 | bytes 18893568 | tf_op jit(solution)/shard_map/qvm,am->qva/dot_general | solution.py:1212
  508.5 13.8 %shard_map.437 = bf16[1,448,3456]{2,1,0:T(8,128)(2,1)S(1)} custom-call(s32[1]{0:T(128)} %copy.97.lengths_ref, bf16[1,448,3456]{2,1,0:T(8,128)(2,1)} %bitcast.171, f32[1,16,448]{2,1,0:T(8,128)S(1)} %get-tuple-element.125.log_ref, bf16[1,448,1152]{2,1,0:T(8,128)(2,1)S(1)} %fusion.37.upstream_ref), custom_call_target="tpu_custom_call" | custom-call | tf_op jit(solution)/shard_map/pallas_call | solution.py:954
  522.3 8.8 fusion.51
  543.4 209.1 %shard_map.439 = (f32[2,72,4736]{2,1,0:T(8,128)}, f32[1,288,1152]{2,1,0:T(8,128)}, f32[2,72,1024]{2,1,0:T(8,128)}, f32[2,128,384]{2,1,0:T(8,128)}) custom-call(bf16[8,144,448]{2,1,0:T(8,128)(2,1)} %bitcast.199, bf16[8,144,448]{2,1,0:T(8,128)(2,1)} %bitcast.200, bf16[8,144,448]{2,1,0:T(8,128)(2,1)} %bitcast.201, bf16[8,2,288,448]{3,2,1,0:T(8,128)(2,1)} %bitcast.178, ...), custom_call_target="tpu_custom_call" | custom-call | tf_op jit(solution)/shard_map/pallas_call | solution.py:401
  763.2 180.7 %shard_map.440 = (f32[2,72,4736]{2,1,0:T(8,128)}, f32[1,288,1152]{2,1,0:T(8,128)}, f32[2,128,1024]{2,1,0:T(8,128)}) custom-call(bf16[8,144,448]{2,1,0:T(8,128)(2,1)} %bitcast.196, bf16[8,144,448]{2,1,0:T(8,128)(2,1)} %bitcast.197, bf16[8,144,448]{2,1,0:T(8,128)(2,1)} %bitcast.198, bf16[8,2,288,448]{3,2,1,0:T(8,128)(2,1)} %bitcast.179, ...), custom_call_target="tpu_custom_call" | custom-call | tf_op jit(solution)/shard_map/pallas_call | solution.py:401
  966.9 25.4 %multiply_subtract_fusion = (f32[2,72,16128]{2,1,0:T(8,128)}, f32[2,72,16128]{2,1,0:T(8,128)}, f32[2,72,16128]{2,1,0:T(8,128)}, f32[2,72,16128]{2,1,0:T(8,128)}) fusion(f32[2,72,16128]{2,1,0:T(8,128)} %param.28, f32[2,72,16128]{2,1,0:T(8,128)} %param.40, f32[2,72,16128]{2,1,0:T(8,128)} %param.34, f32[1,72,16128]{2,1,0:T(8,128)} %bitcast.195, ...), kind=kLoop, calls=%fused_computation.7 | loop fusion | flops 37158912 | bytes 74317824 | tf_op jit(solution)/shard_map/sub | solution.py:1284
  (371 shorter events, 182.6 us)
Async XLA Ops:
  7.2 304.2 %all-gather.9.cloned.1.call-start = ((), (), s32[]{:S(2)}) async-start(), calls=%async_computation | async-start | bytes 27574272 | tf_op jit(solution)/shard_map/all_gather | solution.py:813
  15.0 333.8 %all-gather.13.cloned.1.call-start = ((), (), s32[]{:S(2)}) async-start(), calls=%async_computation.2 | async-start | bytes 11280384 | tf_op jit(solution)/shard_map/all_gather | solution.py:814
  17.4 422.8 %all-gather.11.cloned.1.call-start = ((), (), s32[]{:S(2)}) async-start(), calls=%async_computation.1 | async-start | bytes 12255232 | tf_op jit(solution)/shard_map/all_gather | solution.py:1327
  20.0 19.4 %collective-permute-start = (bf16[72,9216]{1,0:T(8,128)(2,1)}, bf16[72,9216]{1,0:T(8,128)(2,1)}, u32[]{:S(2)}, u32[]{:S(2)}) collective-permute-start(bf16[72,9216]{1,0:T(8,128)(2,1)} %slice_bitcast_fusion.1), channel_id=1, source_target_pairs={{0,2},{2,0},{4,6},{6,4},{8,10},{10,8},{12,14},{14,12},{16,18},{18,... | collective-permute-start | bytes 3981320 | tf_op jit(solution)/shard_map/ppermute | solution.py:62
  20.4 16.8 %collective-permute-start.1 = (bf16[288,1152]{1,0:T(8,128)(2,1)}, bf16[288,1152]{1,0:T(8,128)(2,1)}, u32[]{:S(2)}, u32[]{:S(2)}) collective-permute-start(bf16[288,1152]{1,0:T(8,128)(2,1)} %get-tuple-element.263), channel_id=1, source_target_pairs={{0,2},{2,0},{4,6},{6,4},{8,10},{10,8},{12,14},{14,12},{16,18},{18,... | collective-permute-start | bytes 1990664 | tf_op jit(solution)/shard_map/ppermute | solution.py:62
  21.5 738.4 %all-gather.17.cloned.1.call-start = ((), (), s32[]{:S(2)}) async-start(), calls=%async_computation.4 | async-start | bytes 2128896 | tf_op jit(solution)/shard_map/all_gather | solution.py:766
  35.4 210.7 %copy-start.87 = (f32[448]{0:T(512)}, f32[448]{0:T(512)S(1)}, u32[]{:S(2)}) copy-start(f32[448]{0:T(512)S(1)} %fusion.88) | copy-start | bytes 5380
  42.5 203.6 %copy-start.43 = (bf16[448,1152]{1,0:T(8,128)(2,1)S(1)}, bf16[448,1152]{1,0:T(8,128)(2,1)}, u32[]{:S(2)}) copy-start(bf16[448,1152]{1,0:T(8,128)(2,1)} %param.23) | copy-start | bytes 3096580
  42.5 203.6 %copy-start.83 = (f32[448]{0:T(512)S(1)}, f32[448]{0:T(512)}, u32[]{:S(2)}) copy-start(f32[448]{0:T(512)} %broadcast_multiply_fusion.3) | copy-start | bytes 5380
  246.0 15.1 %copy-start.85 = (f32[1152]{0:T(1024)}, f32[1152]{0:T(1024)S(1)}, u32[]{:S(2)}) copy-start(f32[1152]{0:T(1024)S(1)} %get-tuple-element.207) | copy-start | bytes 13828
  266.2 14.5 %copy-start = (f32[448,1152]{1,0:T(8,128)}, f32[448,1152]{1,0:T(8,128)S(1)}, u32[]{:S(2)}) copy-start(f32[448,1152]{1,0:T(8,128)S(1)} %get-tuple-element.254.middle_ref) | copy-start | bytes 6193156
  267.4 13.3 %copy-start.37 = (f32[1,1152]{1,0:T(1,128)S(1)}, f32[1,1152]{1,0:T(1,128)}, u32[]{:S(2)}) copy-start(f32[1,1152]{1,0:T(1,128)} %get-tuple-element.271.bias_ref) | copy-start | bytes 13828
  292.4 56.4 %copy-start.10 = (bf16[448,1152]{1,0:T(8,128)(2,1)}, bf16[448,1152]{1,0:T(8,128)(2,1)S(1)}, u32[]{:S(2)}) copy-start(bf16[448,1152]{1,0:T(8,128)(2,1)S(1)} %get-tuple-element.156.gradient_ref.refs_9_) | copy-start | bytes 3096580
  352.2 13.2 %copy-start.3 = (f32[448,1152]{1,0:T(8,128)S(1)}, f32[448,1152]{1,0:T(8,128)}, u32[]{:S(2)}) copy-start(f32[448,1152]{1,0:T(8,128)} %copy-done.2) | copy-start | bytes 6193156
  396.9 26.6 %copy-start.7 = (bf16[1,448,3456]{2,1,0:T(8,128)(2,1)}, bf16[1,448,3456]{2,1,0:T(8,128)(2,1)S(1)}, u32[]{:S(2)}) copy-start(bf16[1,448,3456]{2,1,0:T(8,128)(2,1)S(1)} %shard_map.432) | copy-start | bytes 9289732
  416.8 14.3 %copy-start.12 = (bf16[1,448,1152]{2,1,0:T(8,128)(2,1)}, bf16[1,448,1152]{2,1,0:T(8,128)(2,1)S(1)}, u32[]{:S(2)}) copy-start(bf16[1,448,1152]{2,1,0:T(8,128)(2,1)S(1)} %get-tuple-element.116) | copy-start | bytes 3096580
  473.8 16.0 %copy-start.11 = (bf16[448,1152]{1,0:T(8,128)(2,1)}, bf16[448,1152]{1,0:T(8,128)(2,1)S(1)}, u32[]{:S(2)}) copy-start(bf16[448,1152]{1,0:T(8,128)(2,1)S(1)} %get-tuple-element.167.gradient_ref.refs_8_) | copy-start | bytes 3096580
  508.5 13.8 %copy-start.44 = (bf16[448,1152]{1,0:T(8,128)(2,1)S(1)}, bf16[448,1152]{1,0:T(8,128)(2,1)}, u32[]{:S(2)}) copy-start(bf16[448,1152]{1,0:T(8,128)(2,1)} %param.23) | copy-start | bytes 3096580
  539.8 417.3 %all-gather.15.cloned.1.call-start = ((), (), s32[]{:S(2)}) async-start(), calls=%async_computation.3 | async-start | bytes 2923008 | tf_op jit(solution)/shard_map/all_gather | solution.py:766
  543.4 211.6 %copy-start.77 = (f32[72,2048]{1,0:T(8,128)S(1)}, f32[72,2048]{1,0:T(8,128)}, u32[]{:S(2)}) copy-start(f32[72,2048]{1,0:T(8,128)} %param.36) | copy-start | bytes 1769476
  763.2 182.1 %copy-start.73 = (f32[128,2816]{1,0:T(8,128)S(1)}, f32[128,2816]{1,0:T(8,128)}, u32[]{:S(2)}) copy-start(f32[128,2816]{1,0:T(8,128)} %param.43) | copy-start | bytes 4325380
  966.9 25.4 %copy-start.79 = (f32[2,16128]{1,0:T(2,128)S(1)}, f32[2,16128]{1,0:T(2,128)}, u32[]{:S(2)}) copy-start(f32[2,16128]{1,0:T(2,128)} %param.32) | copy-start | bytes 387076
  966.9 25.4 %copy-start.80 = (f32[2,16128]{1,0:T(2,128)S(1)}, f32[2,16128]{1,0:T(2,128)}, u32[]{:S(2)}) copy-start(f32[2,16128]{1,0:T(2,128)} %param.44) | copy-start | bytes 387076
  966.9 25.4 %copy-start.81 = (f32[2,16128]{1,0:T(2,128)S(1)}, f32[2,16128]{1,0:T(2,128)}, u32[]{:S(2)}) copy-start(f32[2,16128]{1,0:T(2,128)} %param.38) | copy-start | bytes 387076
  (88 other events, 389.1 us)
Sparse Core Ops, SparseCore 0:
  15.1 228.4 all-gather.8
  246.5 92.8 all-gather.12
  341.6 92.4 all-gather.10
  539.9 70.6 all-gather.16
  613.9 64.5 all-gather.14
